TPU v7x, 128 devices: a whole 4x4x4 slice. The times are simulated.
128 devices in a mesh: dp: 16 (over x_lo, y, core), expert: 8 (over z, x_hi).
Axes of the slice: x: 4 (x_hi: 2, x_lo: 2; x = x_hi * 2 + x_lo), y: 4, z: 4, core: 2. Of those that a mesh axis runs over, the one named last changes fastest.
Arguments:
- tokens: bfloat16 [16384, 1536], P(('dp', 'expert')), may hold values from -6 to 6
- cotangent: bfloat16 [16384, 1536], P(('dp', 'expert')), may hold values from -6 to 6
- seq_lengths: int32 [16, 4], P('dp'), may hold values from 1 to 1021, as said below
- expert_ids: int32 [16384, 8], P(('dp', 'expert')), may hold values from 0 to 39, all different within a row; in each aligned block of 128 rows (0 to 127, 128 to 255, ...) at most 32 rows name the same one
- w_query: bfloat16 [1536, 1536], P(('dp', 'expert')), may hold values from -0.15625 to 0.15625
- w_key: bfloat16 [1536, 512], P(('dp', 'expert')), may hold values from -0.15625 to 0.15625
- w_value: bfloat16 [1536, 512], P(('dp', 'expert')), may hold values from -0.15625 to 0.15625
- w_output: bfloat16 [1536, 1536], P(('dp', 'expert')), may hold values from -2.5 to 2.5
- norm_one: bfloat16 [1536], P(('dp', 'expert')), may hold values from 0.5 to 1.5
- norm_two: bfloat16 [1536], P(('dp', 'expert')), may hold values from 0.5 to 1.5
- w_router: bfloat16 [1536, 40], P(('dp', 'expert')), may hold values from -0.078125 to 0.078125
- w_gate: bfloat16 [40, 1536, 512], P('expert', 'dp'), may hold values from -0.15625 to 0.15625
- w_up: bfloat16 [40, 1536, 512], P('expert', 'dp'), may hold values from -0.15625 to 0.15625
- w_down: bfloat16 [40, 512, 1536], P('expert', 'dp'), may hold values from -1 to 1
Outputs:
- mixed: bfloat16 [16384, 1536], P(('dp', 'expert'))
- grad_tokens: float32 [16384, 1536], P(('dp', 'expert'))
- grad_w_query: float32 [1536, 1536], P(('dp', 'expert'))
- grad_w_key: float32 [1536, 512], P(('dp', 'expert'))
- grad_w_value: float32 [1536, 512], P(('dp', 'expert'))
- grad_w_output: float32 [1536, 1536], P(('dp', 'expert'))
- grad_norm_one: float32 [1536], P(('dp', 'expert'))
- grad_norm_two: float32 [1536], P(('dp', 'expert'))
- grad_w_router: float32 [1536, 40], P(('dp', 'expert'))
- grad_w_gate: float32 [40, 1536, 512], P('expert', 'dp')
- grad_w_up: float32 [40, 1536, 512], P('expert', 'dp')
- grad_w_down: float32 [40, 512, 1536], P('expert', 'dp')
Inputs may be any that keep to these rules, and one draw needn't show every extreme that they name: `seq_lengths`: each row lists the lengths of the 4 sequences of one group in order; they sum to 1024. One of them, at a place drawn from the seed, holds all but at most 3 * (32) of the group's tokens. In one group, drawn from the seed, all the others have length 1. `expert_ids`: A token's 8 experts differ. Among the 128 rows of one device each expert is named at most 32 times.
All inputs are finite; a program needn't handle non-finite values.
Results may differ from a plain program's by a relative error of at most 0.02.
Values may be sent and summed in bfloat16 or wider, within the bound.
A program may use at most 256 MiB of HBM per device.

v0:
```python
import math

import jax
import jax.numpy as jnp
from jax import lax
from jax.sharding import PartitionSpec as P

HEADS = 24
KV_HEADS = 8
HEAD = 64


epsilon = 1e-06
rope_base = 10000.0
masked_score = -1e30


def rms_scale(values):
    return lax.rsqrt(jnp.mean(values * values, axis=-1, keepdims=True) + epsilon)


def rope_tables(offsets, head_width):
    exponent = jnp.arange(head_width // 2, dtype=jnp.float32) * (2.0 / head_width)
    frequency = jnp.exp(-exponent * math.log(rope_base))
    phase_angles = offsets.astype(jnp.float32)[:, None] * frequency[None, :]
    return (jnp.cos(phase_angles)[:, None, :], jnp.sin(phase_angles)[:, None, :])


def rotate(values, cosine, sine_table):
    half_width = values.shape[-1] // 2
    first_half = values[..., :half_width]
    second_half = values[..., half_width:]
    return jnp.concatenate(
        [
            first_half * cosine - second_half * sine_table,
            second_half * cosine + first_half * sine_table,
        ],
        axis=-1,
    )


def unrotate(grad_values, cosine, sine_table):
    half_width = grad_values.shape[-1] // 2
    first_half = grad_values[..., :half_width]
    second_half = grad_values[..., half_width:]
    return jnp.concatenate(
        [
            first_half * cosine + second_half * sine_table,
            second_half * cosine - first_half * sine_table,
        ],
        axis=-1,
    )


def layout(lengths, group_count):
    seq_ends = jnp.cumsum(lengths)
    starts = seq_ends - lengths
    places = jnp.arange(group_count, dtype=jnp.int32)
    member = ((places[:, None] >= starts[None, :]) & (places[:, None] < seq_ends[None, :])).astype(
        jnp.int32
    )
    numbers = jnp.arange(lengths.shape[0], dtype=jnp.int32)
    segment = jnp.sum(member * numbers[None, :], axis=1)
    offsets = places - jnp.sum(member * starts[None, :], axis=1)
    return (segment, offsets)


def slot_of(expert_rows, expert_count):
    flat_ids = expert_rows.reshape(-1)
    one_hot = (flat_ids[:, None] == jnp.arange(expert_count, dtype=jnp.int32)[None, :]).astype(
        jnp.int32
    )
    earlier = jnp.cumsum(one_hot, axis=0) - one_hot
    return jnp.sum(earlier * one_hot, axis=1)


def norm_back(values, row_scale, gain_vector, grad_normed):
    weighted = grad_normed * gain_vector
    grad_gain = jnp.sum(grad_normed * values * row_scale, axis=0)
    grad_values = row_scale * weighted - values * row_scale**3 * jnp.mean(
        weighted * values, axis=-1, keepdims=True
    )
    return (grad_values, grad_gain)


def attention_scores(query_heads, key_heads, allowed, score_scale):
    scores = (
        jnp.einsum("qgrh,kgh->grqk", query_heads, key_heads, preferred_element_type=jnp.float32)
        * score_scale
    )
    return jnp.where(allowed, scores, masked_score)


def local(
    tokens,
    cotangent,
    seq_lengths,
    expert_ids,
    w_query,
    w_key,
    w_value,
    w_output,
    norm_one,
    norm_two,
    w_router,
    w_gate,
    w_up,
    w_down,
):
    dense_gathered = (
        lax.all_gather(w_query, ("dp", "expert"), axis=0, tiled=True),
        lax.all_gather(w_key, ("dp", "expert"), axis=0, tiled=True),
        lax.all_gather(w_value, ("dp", "expert"), axis=0, tiled=True),
        lax.all_gather(w_output, ("dp", "expert"), axis=0, tiled=True),
        lax.all_gather(norm_one, ("dp", "expert"), axis=0, tiled=True),
        lax.all_gather(norm_two, ("dp", "expert"), axis=0, tiled=True),
        lax.all_gather(w_router, ("dp", "expert"), axis=0, tiled=True),
    )
    query_all, key_all, value_all, output_all, gain_one, gain_two, router_all = dense_gathered
    expert_full = (
        lax.all_gather(w_gate, "dp", axis=1, tiled=True),
        lax.all_gather(w_up, "dp", axis=1, tiled=True),
        lax.all_gather(w_down, "dp", axis=1, tiled=True),
    )
    gate_full, up_full, down_full = expert_full
    pieces = lax.axis_size("expert")
    piece_index = lax.axis_index("expert")
    local_count, model_width = tokens.shape
    group_count = local_count * pieces
    top_count = expert_ids.shape[1]
    expert_count = router_all.shape[1]
    local_experts = gate_full.shape[0]
    capacity = local_count * top_count * 5 // (4 * expert_count)
    repeats = HEADS // KV_HEADS
    score_scale = HEAD ** (-0.5)
    segment, offsets = layout(seq_lengths[0], group_count)
    first_row = piece_index * local_count
    local_offsets = lax.dynamic_slice_in_dim(offsets, first_row, local_count)
    local_segment = lax.dynamic_slice_in_dim(segment, first_row, local_count)
    cosine, sine_table = rope_tables(local_offsets, HEAD)
    places = jnp.arange(group_count, dtype=jnp.int32)
    local_places = first_row + jnp.arange(local_count, dtype=jnp.int32)
    allowed = (local_segment[:, None] == segment[None, :]) & (
        places[None, :] <= local_places[:, None]
    )
    inputs = tokens.astype(jnp.float32)
    scale_one = rms_scale(inputs)
    normed = (inputs * scale_one * gain_one).astype(jnp.bfloat16)
    query_raw = jnp.dot(normed, query_all, preferred_element_type=jnp.float32).reshape(
        local_count, HEADS, HEAD
    )
    query_heads = (
        rotate(query_raw, cosine, sine_table)
        .astype(jnp.bfloat16)
        .reshape(local_count, KV_HEADS, repeats, HEAD)
    )
    key_raw = jnp.dot(normed, key_all, preferred_element_type=jnp.float32).reshape(
        local_count, KV_HEADS, HEAD
    )
    key_local = (
        rotate(key_raw, cosine, sine_table)
        .astype(jnp.bfloat16)
        .reshape(local_count, KV_HEADS * HEAD)
    )
    value_local = jnp.dot(normed, value_all, preferred_element_type=jnp.float32).astype(
        jnp.bfloat16
    )
    key_group, value_group = (
        lax.all_gather(key_local, "expert", axis=0, tiled=True),
        lax.all_gather(value_local, "expert", axis=0, tiled=True),
    )
    key_heads = key_group.reshape(group_count, KV_HEADS, HEAD)
    value_heads = value_group.reshape(group_count, KV_HEADS, HEAD)
    scores = attention_scores(query_heads, key_heads, allowed, score_scale)
    highest_score = jnp.max(scores, axis=-1, keepdims=True)
    exponent_terms = jnp.exp(scores - highest_score)
    totals = jnp.sum(exponent_terms, axis=-1, keepdims=True)
    probabilities = exponent_terms / totals
    log_total = highest_score + jnp.log(totals)
    attended = jnp.einsum(
        "grqk,kgh->qgrh",
        probabilities.astype(jnp.bfloat16),
        value_heads,
        preferred_element_type=jnp.float32,
    )
    attended = attended.reshape(local_count, HEADS * HEAD).astype(jnp.bfloat16)
    middle = inputs + jnp.dot(attended, output_all, preferred_element_type=jnp.float32)
    scale_two = rms_scale(middle)
    normed_two = (middle * scale_two * gain_two).astype(jnp.bfloat16)
    logits = jnp.dot(normed_two, router_all, preferred_element_type=jnp.float32)
    one_hot = (
        expert_ids[:, :, None] == jnp.arange(expert_count, dtype=jnp.int32)[None, None, :]
    ).astype(jnp.float32)
    chosen = jnp.sum(one_hot * logits[:, None, :], axis=-1)
    gate_values = jax.nn.softmax(chosen, axis=-1)
    slot_index = slot_of(expert_ids, expert_count)
    target = expert_ids.reshape(-1) * capacity + slot_index
    token_rows = jnp.repeat(normed_two, top_count, axis=0)
    outgoing = (
        jnp.zeros((expert_count * capacity, model_width), jnp.bfloat16).at[target].set(token_rows)
    )
    arrived = lax.all_to_all(
        outgoing.reshape(pieces, local_experts * capacity, model_width),
        "expert",
        split_axis=0,
        concat_axis=0,
        tiled=True,
    )
    arrived = arrived.reshape(pieces, local_experts, capacity, model_width)
    gate_act = jnp.einsum("secd,edf->secf", arrived, gate_full, preferred_element_type=jnp.float32)
    up_act = jnp.einsum("secd,edf->secf", arrived, up_full, preferred_element_type=jnp.float32)
    silu_act = jax.nn.silu(gate_act)
    hidden = (silu_act * up_act).astype(jnp.bfloat16)
    expert_out = jnp.einsum(
        "secf,efd->secd", hidden, down_full, preferred_element_type=jnp.float32
    ).astype(jnp.bfloat16)
    returned = lax.all_to_all(
        expert_out.reshape(pieces, local_experts * capacity, model_width),
        "expert",
        split_axis=0,
        concat_axis=0,
        tiled=True,
    )
    returned = returned.reshape(expert_count * capacity, model_width)[target].reshape(
        local_count, top_count, model_width
    )
    mixed = middle + jnp.sum(gate_values[:, :, None] * returned.astype(jnp.float32), axis=1)
    dense_back = (
        lax.all_gather(w_query, ("dp", "expert"), axis=0, tiled=True),
        lax.all_gather(w_key, ("dp", "expert"), axis=0, tiled=True),
        lax.all_gather(w_value, ("dp", "expert"), axis=0, tiled=True),
        lax.all_gather(w_output, ("dp", "expert"), axis=0, tiled=True),
        lax.all_gather(norm_one, ("dp", "expert"), axis=0, tiled=True),
        lax.all_gather(norm_two, ("dp", "expert"), axis=0, tiled=True),
        lax.all_gather(w_router, ("dp", "expert"), axis=0, tiled=True),
    )
    expert_back = (
        lax.all_gather(w_gate, "dp", axis=1, tiled=True),
        lax.all_gather(w_up, "dp", axis=1, tiled=True),
        lax.all_gather(w_down, "dp", axis=1, tiled=True),
    )
    query_back, key_back, value_back, output_back, gain_one_back, gain_two_back, router_back = (
        dense_back
    )
    gate_back, up_back, down_back = expert_back
    grad_out = cotangent.astype(jnp.float32)
    grad_gates = jnp.sum(returned.astype(jnp.float32) * grad_out[:, None, :], axis=-1)
    grad_returned = (gate_values[:, :, None] * grad_out[:, None, :]).astype(jnp.bfloat16)
    grad_outgoing = (
        jnp.zeros((expert_count * capacity, model_width), jnp.bfloat16)
        .at[target]
        .set(grad_returned.reshape(-1, model_width))
    )
    grad_expert_out = lax.all_to_all(
        grad_outgoing.reshape(pieces, local_experts * capacity, model_width),
        "expert",
        split_axis=0,
        concat_axis=0,
        tiled=True,
    )
    grad_expert_out = grad_expert_out.reshape(pieces, local_experts, capacity, model_width)
    grad_hidden = jnp.einsum(
        "secd,efd->secf", grad_expert_out, down_back, preferred_element_type=jnp.float32
    )
    sigmoid_act = jax.nn.sigmoid(gate_act)
    grad_gate_act = (
        grad_hidden * up_act * sigmoid_act * (1.0 + gate_act * (1.0 - sigmoid_act))
    ).astype(jnp.bfloat16)
    grad_up_act = (grad_hidden * silu_act).astype(jnp.bfloat16)
    grad_arrived = jnp.einsum(
        "secf,edf->secd", grad_gate_act, gate_back, preferred_element_type=jnp.float32
    )
    grad_arrived = (
        grad_arrived
        + jnp.einsum("secf,edf->secd", grad_up_act, up_back, preferred_element_type=jnp.float32)
    ).astype(jnp.bfloat16)
    grad_token_rows = lax.all_to_all(
        grad_arrived.reshape(pieces, local_experts * capacity, model_width),
        "expert",
        split_axis=0,
        concat_axis=0,
        tiled=True,
    )
    grad_token_rows = grad_token_rows.reshape(expert_count * capacity, model_width)[target].reshape(
        local_count, top_count, model_width
    )
    grad_normed_two = jnp.sum(grad_token_rows.astype(jnp.float32), axis=1)
    grad_chosen = gate_values * (
        grad_gates - jnp.sum(gate_values * grad_gates, axis=-1, keepdims=True)
    )
    grad_logits = jnp.sum(one_hot * grad_chosen[:, :, None], axis=1).astype(jnp.bfloat16)
    grad_router = jnp.einsum(
        "td,te->de", normed_two, grad_logits, preferred_element_type=jnp.float32
    )
    grad_normed_two = grad_normed_two + jnp.einsum(
        "te,de->td", grad_logits, router_back, preferred_element_type=jnp.float32
    )
    grad_middle_norm, grad_gain_two = norm_back(middle, scale_two, gain_two_back, grad_normed_two)
    grad_middle = grad_out + grad_middle_norm
    grad_branch = grad_middle.astype(jnp.bfloat16)
    grad_output = jnp.einsum("tq,td->qd", attended, grad_branch, preferred_element_type=jnp.float32)
    grad_attended = jnp.einsum(
        "td,qd->tq", grad_branch, output_back, preferred_element_type=jnp.float32
    ).astype(jnp.bfloat16)
    grad_attended = grad_attended.reshape(local_count, KV_HEADS, repeats, HEAD)
    scores_again = attention_scores(query_heads, key_heads, allowed, score_scale)
    probs_again = jnp.exp(scores_again - log_total)
    grad_probs = jnp.einsum(
        "qgrh,kgh->grqk", grad_attended, value_heads, preferred_element_type=jnp.float32
    )
    grad_scores = (
        probs_again * (grad_probs - jnp.sum(probs_again * grad_probs, axis=-1, keepdims=True))
    ).astype(jnp.bfloat16)
    grad_query_rot = (
        jnp.einsum("grqk,kgh->qgrh", grad_scores, key_heads, preferred_element_type=jnp.float32)
        * score_scale
    )
    grad_key_rot = (
        jnp.einsum("grqk,qgrh->kgh", grad_scores, query_heads, preferred_element_type=jnp.float32)
        * score_scale
    )
    grad_value_group = jnp.einsum(
        "grqk,qgrh->kgh",
        probs_again.astype(jnp.bfloat16),
        grad_attended,
        preferred_element_type=jnp.float32,
    )
    grad_key_local, grad_value_local = (
        lax.psum_scatter(
            grad_key_rot.reshape(group_count, KV_HEADS * HEAD).astype(jnp.bfloat16),
            "expert",
            scatter_dimension=0,
            tiled=True,
        ).astype(jnp.float32),
        lax.psum_scatter(
            grad_value_group.reshape(group_count, KV_HEADS * HEAD).astype(jnp.bfloat16),
            "expert",
            scatter_dimension=0,
            tiled=True,
        ).astype(jnp.float32),
    )
    grad_query_raw = (
        unrotate(grad_query_rot.reshape(local_count, HEADS, HEAD), cosine, sine_table)
        .reshape(local_count, HEADS * HEAD)
        .astype(jnp.bfloat16)
    )
    grad_key_raw = (
        unrotate(grad_key_local.reshape(local_count, KV_HEADS, HEAD), cosine, sine_table)
        .reshape(local_count, KV_HEADS * HEAD)
        .astype(jnp.bfloat16)
    )
    grad_value_raw = grad_value_local.astype(jnp.bfloat16)
    grad_query = jnp.einsum("td,tq->dq", normed, grad_query_raw, preferred_element_type=jnp.float32)
    grad_key = jnp.einsum("td,tq->dq", normed, grad_key_raw, preferred_element_type=jnp.float32)
    grad_value = jnp.einsum("td,tq->dq", normed, grad_value_raw, preferred_element_type=jnp.float32)
    grad_normed = jnp.einsum(
        "tq,dq->td", grad_query_raw, query_back, preferred_element_type=jnp.float32
    )
    grad_normed = grad_normed + jnp.einsum(
        "tq,dq->td", grad_key_raw, key_back, preferred_element_type=jnp.float32
    )
    grad_normed = grad_normed + jnp.einsum(
        "tq,dq->td", grad_value_raw, value_back, preferred_element_type=jnp.float32
    )
    grad_inputs_norm, grad_gain_one = norm_back(inputs, scale_one, gain_one_back, grad_normed)
    grad_tokens = grad_middle + grad_inputs_norm
    dense_grads = (
        lax.psum_scatter(grad_query, ("dp", "expert"), scatter_dimension=0, tiled=True),
        lax.psum_scatter(grad_key, ("dp", "expert"), scatter_dimension=0, tiled=True),
        lax.psum_scatter(grad_value, ("dp", "expert"), scatter_dimension=0, tiled=True),
        lax.psum_scatter(grad_output, ("dp", "expert"), scatter_dimension=0, tiled=True),
        lax.psum_scatter(grad_gain_one, ("dp", "expert"), scatter_dimension=0, tiled=True),
        lax.psum_scatter(grad_gain_two, ("dp", "expert"), scatter_dimension=0, tiled=True),
        lax.psum_scatter(grad_router, ("dp", "expert"), scatter_dimension=0, tiled=True),
    )
    grad_gate = jnp.einsum(
        "secd,secf->edf", arrived, grad_gate_act, preferred_element_type=jnp.float32
    )
    grad_up = jnp.einsum("secd,secf->edf", arrived, grad_up_act, preferred_element_type=jnp.float32)
    grad_down = jnp.einsum(
        "secf,secd->efd", hidden, grad_expert_out, preferred_element_type=jnp.float32
    )
    expert_grads = (
        lax.psum_scatter(
            grad_gate.astype(jnp.bfloat16), "dp", scatter_dimension=1, tiled=True
        ).astype(jnp.float32),
        lax.psum_scatter(
            grad_up.astype(jnp.bfloat16), "dp", scatter_dimension=1, tiled=True
        ).astype(jnp.float32),
        lax.psum_scatter(
            grad_down.astype(jnp.bfloat16), "dp", scatter_dimension=1, tiled=True
        ).astype(jnp.float32),
    )
    grad_gate_out, grad_up_out, grad_down_out = expert_grads
    return (
        mixed.astype(jnp.bfloat16),
        grad_tokens,
        dense_grads[0],
        dense_grads[1],
        dense_grads[2],
        dense_grads[3],
        dense_grads[4],
        dense_grads[5],
        dense_grads[6],
        grad_gate_out,
        grad_up_out,
        grad_down_out,
    )


def solution(mesh):
    in_specs = (
        P(("dp", "expert"), None),
        P(("dp", "expert"), None),
        P("dp", None),
        P(("dp", "expert"), None),
        P(("dp", "expert"), None),
        P(("dp", "expert"), None),
        P(("dp", "expert"), None),
        P(("dp", "expert"), None),
        P(("dp", "expert")),
        P(("dp", "expert")),
        P(("dp", "expert"), None),
        P("expert", "dp", None),
        P("expert", "dp", None),
        P("expert", "dp", None),
    )
    out_specs = (
        P(("dp", "expert"), None),
        P(("dp", "expert"), None),
        P(("dp", "expert"), None),
        P(("dp", "expert"), None),
        P(("dp", "expert"), None),
        P(("dp", "expert"), None),
        P(("dp", "expert")),
        P(("dp", "expert")),
        P(("dp", "expert"), None),
        P("expert", "dp", None),
        P("expert", "dp", None),
        P("expert", "dp", None),
    )
    return jax.shard_map(local, mesh=mesh, in_specs=in_specs, out_specs=out_specs, check_vma=False)
```

profile of v0, /device:TPU:0, one launch (start us, length us, event | category | flops | bytes accessed | tf_op | source)
XLA Modules:
  0.0 3732.6 jit_solution(4418554195950589906)
XLA Ops:
  10.5 68.4 %all-reduce.15 = (bf16[1536]{0:T(1024)(128)(2,1)S(1)}, bf16[1536]{0:T(1024)(128)(2,1)S(1)}) all-reduce(bf16[1536]{0:T(1024)(128)(2,1)S(1)} %dynamic-update-slice, bf16[1536]{0:T(1024)(128)(2,1)S(1)} %dynamic-update-slice.1), channel_id=1, replica_groups=mesh['dp'=16,'expert'=8] {'dp','expert'}, use_global_device_ids=true, to_apply=%add | all-reduce | flops 3072 | bytes 12288
  80.5 229.8 %all-gather.25.cloned.1.call-done = bf16[128,12,512]{2,1,0:T(8,128)(2,1)} async-done(((bf16[1,12,512]{2,1,0:T(8,128)(2,1)}), bf16[128,12,512]{2,1,0:T(8,128)(2,1)}) %all-gather.25.cloned.1.call-update) | async-done | bytes 1572880 | tf_op jit(solution)/shard_map/all_gather | solution.py:113
  315.8 297.5 %all-gather.27.cloned.1.call-done = bf16[128,12,512]{2,1,0:T(8,128)(2,1)} async-done(((bf16[1,12,512]{2,1,0:T(8,128)(2,1)}), bf16[128,12,512]{2,1,0:T(8,128)(2,1)}) %all-gather.27.cloned.1.call-update) | async-done | bytes 1572880 | tf_op jit(solution)/shard_map/all_gather | solution.py:112
  620.2 11.3 reduce-window.11
  632.8 31.3 all-gather.15.cloned.1.call-done
  666.5 308.7 %all-gather.29.cloned.1.call-done = bf16[128,12,1536]{2,1,0:T(8,128)(2,1)} async-done(((bf16[1,12,1536]{2,1,0:T(8,128)(2,1)}), bf16[128,12,1536]{2,1,0:T(8,128)(2,1)}) %all-gather.29.cloned.1.call-update) | async-done | bytes 4718608 | tf_op jit(solution)/shard_map/all_gather | solution.py:111
  983.4 305.8 %all-gather.31.cloned.1.call-done = bf16[128,12,1536]{2,1,0:T(8,128)(2,1)} async-done(((bf16[1,12,1536]{2,1,0:T(8,128)(2,1)}), bf16[128,12,1536]{2,1,0:T(8,128)(2,1)}) %all-gather.31.cloned.1.call-update) | async-done | bytes 4718608 | tf_op jit(solution)/shard_map/all_gather | solution.py:114
  1302.0 37.0 all-gather.17.cloned.1.call-done
  1368.1 411.3 %all-gather.4 = bf16[128,12,40]{2,1,0:T(8,128)(2,1)S(1)} all-gather(bf16[1,12,40]{2,1,0:T(8,128)(2,1)S(1)} %bitcast.286), channel_id=1, replica_groups=mesh['dp'=16,'expert'=8] {'dp','expert'}, dimensions={0}, use_global_device_ids=true | all-gather | bytes 123840 | tf_op jit(solution)/shard_map/all_gather | solution.py:117
  1811.3 14.4 all-to-all-done.2
  1825.7 10.3 fusion.53
  1870.6 28.0 all-to-all-done.3
  1916.5 15.3 all-to-all-done.1
  1931.8 10.1 gather_fusion
  1955.0 10.9 fusion.5
  2032.3 14.8 reduce-scatter.26.cloned.1.call-done
  2049.5 72.4 %reduce-scatter.28.cloned.1.call-done = bf16[128,512]{1,0:T(8,128)(2,1)} async-done(((bf16[1024,512]{1,0:T(8,128)(2,1)}), bf16[128,512]{1,0:T(8,128)(2,1)}) %reduce-scatter.28.cloned.1.call-update) | async-done | bytes 131088
  2125.2 867.1 %fusion.111 = (f32[16,1536]{1,0:T(8,128)}, f32[16,512]{1,0:T(8,128)}, f32[16,512]{1,0:T(8,128)}, f32[16,1536]{1,0:T(8,128)}, f32[16,40]{1,0:T(8,128)S(1)}) fusion(f32[1536,1536]{1,0:T(8,128)} %fusion.104, f32[1536,512]{1,0:T(8,128)S(1)} %fusion.102, f32[1536,512]{1,0:T(8,128)} %fusion.100, f32[1536,1536]{1,0:T(8,128)} %fusion.80, f32[1536,40]{1,0:T(8,128)} %fusion.114), kind=kCustom, calls=%all-reduce-scatter.5 | all-reduce-scatter fusion | flops 8470529 | bytes 25676288
  3451.6 64.6 %all-reduce.14 = (f32[1536]{0:T(1024)S(1)}, f32[1536]{0:T(1024)S(1)}) all-reduce(f32[1536]{0:T(1024)S(1)} %get-tuple-element.16, f32[1536]{0:T(1024)S(1)} %copy-done.161), channel_id=8, replica_groups=mesh['dp'=16,'expert'=8] {'dp','expert'}, use_global_device_ids=true, to_apply=%region_30.31.clone | all-reduce | flops 3072 | bytes 24576
  3517.5 14.0 concatenate.31
  3553.6 13.8 concatenate.28
  3567.4 25.9 concatenate.29
  3632.6 31.7 concatenate.27
  3664.4 52.7 %concatenate.30 = f32[524,1536]{1,0:T(8,128)} concatenate(f32[12,1536]{1,0:T(8,128)S(1)} %copy-done.53, f32[16,1536]{1,0:T(8,128)} %copy-done.72, f32[16,1536]{1,0:T(8,128)} %copy-done.74, f32[16,1536]{1,0:T(8,128)} %copy-done.76, f32[16,1536]{1,0:T(8,128)} %copy-done.77, f32[16,1536]{1,0:T(8,128)} %copy-done.78, f32[16,1536]{1,0:T(8,128)} %copy-done.79, f32[16,1536]{1,0:T(8,128)} %copy-done.80, ...), dimensions={0} | concatenate | bytes 6438912
  (935 shorter events, 765.9 us)
Async XLA Ops:
  7.2 303.1 %all-gather.25.cloned.1.call-start = ((), (), s32[]{:S(2)}) async-start(), calls=%async_computation.17 | async-start | bytes 2113536 | tf_op jit(solution)/shard_map/all_gather | solution.py:113
  7.9 605.4 %all-gather.27.cloned.1.call-start = ((), (), s32[]{:S(2)}) async-start(), calls=%async_computation.18 | async-start | bytes 2113536 | tf_op jit(solution)/shard_map/all_gather | solution.py:112
  8.7 655.5 %all-gather.15.cloned.1.call-start = ((), (), s32[]{:S(2)}) async-start(), calls=%async_computation.9 | async-start | bytes 1179648 | tf_op jit(solution)/shard_map/all_gather | solution.py:170
  314.0 661.2 %all-gather.29.cloned.1.call-start = ((), (), s32[]{:S(2)}) async-start(), calls=%async_computation.19 | async-start | bytes 6340608 | tf_op jit(solution)/shard_map/all_gather | solution.py:111
  314.6 974.6 %all-gather.31.cloned.1.call-start = ((), (), s32[]{:S(2)}) async-start(), calls=%async_computation.20 | async-start | bytes 6340608 | tf_op jit(solution)/shard_map/all_gather | solution.py:114
  315.2 1023.8 %all-gather.17.cloned.1.call-start = ((), (), s32[]{:S(2)}) async-start(), calls=%async_computation.10 | async-start | bytes 1179648 | tf_op jit(solution)/shard_map/all_gather | solution.py:169
  617.4 1177.7 %all-gather.21.cloned.1.call-start = ((), (), s32[]{:S(2)}) async-start(), calls=%async_computation.12 | async-start | bytes 8355840 | tf_op jit(solution)/shard_map/all_gather | solution.py:122
  618.1 1185.0 %all-gather.19.cloned.1.call-start = ((), (), s32[]{:S(2)}) async-start(), calls=%async_computation.11 | async-start | bytes 8355840 | tf_op jit(solution)/shard_map/all_gather | solution.py:121
  618.9 1206.9 %all-gather.23.cloned.1.call-start = ((), (), s32[]{:S(2)}) async-start(), calls=%async_computation.13 | async-start | bytes 8355840 | tf_op jit(solution)/shard_map/all_gather | solution.py:123
  1363.4 426.3 %all-to-all-start = ((bf16[8,160,1536]{2,1,0:T(8,128)(2,1)}), bf16[8,160,1536]{2,1,0:T(8,128)(2,1)}, u32[]{:S(2)}, u32[]{:S(2)}) async-start(bf16[8,160,1536]{2,1,0:T(8,128)(2,1)} %bitcast.249), calls=%async_computation | async-start | bytes 7864320 | tf_op jit(solution)/shard_map/all_to_all | solution.py:202
  1903.2 143.8 %reduce-scatter.26.cloned.1.call-start = ((), (), s32[]{:S(2)}) async-start(), calls=%async_computation.21 | async-start | bytes 1179648
  1980.4 141.6 %reduce-scatter.28.cloned.1.call-start = ((), (), s32[]{:S(2)}) async-start(), calls=%async_computation.22 | async-start | bytes 1179648
  1989.9 1729.4 %reduce-scatter.24.cloned.1.call-start = ((), (), s32[]{:S(2)}) async-start(), calls=%async_computation.16 | async-start | bytes 8355840 | tf_op jit(solution)/shard_map/reduce_scatter | solution.py:390
  1998.0 1723.5 %reduce-scatter.20.cloned.1.call-start = ((), (), s32[]{:S(2)}) async-start(), calls=%async_computation.14 | async-start | bytes 8355840 | tf_op jit(solution)/shard_map/reduce_scatter | solution.py:384
  2006.7 1716.8 %reduce-scatter.22.cloned.1.call-start = ((), (), s32[]{:S(2)}) async-start(), calls=%async_computation.15 | async-start | bytes 8355840 | tf_op jit(solution)/shard_map/reduce_scatter | solution.py:387
  3055.3 79.7 %collective-permute-start.95 = (f32[12,512]{1,0:T(8,128)S(1)}, f32[12,512]{1,0:T(8,128)S(1)}, u32[]{:S(2)}, u32[]{:S(2)}) collective-permute-start(f32[12,512]{1,0:T(8,128)S(1)} %slice.56), channel_id=1, source_target_pairs={{0,32},{1,33},{2,34},{3,35},{4,36},{5,37},{6,38},{7,39},{8,40},{9,... | collective-permute-start | bytes 73736
  3057.2 84.3 %collective-permute-start.62 = (f32[16,512]{1,0:T(8,128)}, f32[16,512]{1,0:T(8,128)S(1)}, u32[]{:S(2)}, u32[]{:S(2)}) collective-permute-start(f32[16,512]{1,0:T(8,128)} %get-tuple-element.30), channel_id=1, source_target_pairs={{0,31},{1,32},{2,33},{3,34},{4,35},{5,36},{6,37},{7,38},{8,39},{9,... | collective-permute-start | bytes 98312
  3062.4 80.5 %collective-permute-start.61 = (f32[16,512]{1,0:T(8,128)}, f32[16,512]{1,0:T(8,128)S(1)}, u32[]{:S(2)}, u32[]{:S(2)}) collective-permute-start(f32[16,512]{1,0:T(8,128)} %get-tuple-element.30), channel_id=1, source_target_pairs={{0,30},{1,31},{2,32},{3,33},{4,34},{5,35},{6,36},{7,37},{8,38},{9,... | collective-permute-start | bytes 98312
  3438.7 92.9 %collective-permute-start.115 = (f32[16,1536]{1,0:T(8,128)S(1)}, f32[16,1536]{1,0:T(8,128)S(1)}, u32[]{:S(2)}, u32[]{:S(2)}) collective-permute-start(f32[16,1536]{1,0:T(8,128)S(1)} %copy-done.34), channel_id=1, source_target_pairs={{0,20},{1,21},{2,22},{3,23},{4,24},{5,25},{6,26},{7,27},{8,28},{9,... | collective-permute-start | bytes 294920
  3440.0 95.7 %collective-permute-start.114 = (f32[16,1536]{1,0:T(8,128)S(1)}, f32[16,1536]{1,0:T(8,128)S(1)}, u32[]{:S(2)}, u32[]{:S(2)}) collective-permute-start(f32[16,1536]{1,0:T(8,128)S(1)} %copy-done.34), channel_id=1, source_target_pairs={{0,19},{1,20},{2,21},{3,22},{4,23},{5,24},{6,25},{7,26},{8,27},{9,... | collective-permute-start | bytes 294920
  3441.3 96.4 %collective-permute-start.113 = (f32[16,1536]{1,0:T(8,128)S(1)}, f32[16,1536]{1,0:T(8,128)S(1)}, u32[]{:S(2)}, u32[]{:S(2)}) collective-permute-start(f32[16,1536]{1,0:T(8,128)S(1)} %copy-done.34), channel_id=1, source_target_pairs={{0,18},{1,19},{2,20},{3,21},{4,22},{5,23},{6,24},{7,25},{8,26},{9,... | collective-permute-start | bytes 294920
  3442.6 99.5 %collective-permute-start.112 = (f32[16,1536]{1,0:T(8,128)S(1)}, f32[16,1536]{1,0:T(8,128)S(1)}, u32[]{:S(2)}, u32[]{:S(2)}) collective-permute-start(f32[16,1536]{1,0:T(8,128)S(1)} %copy-done.34), channel_id=1, source_target_pairs={{0,17},{1,18},{2,19},{3,20},{4,21},{5,22},{6,23},{7,24},{8,25},{9,... | collective-permute-start | bytes 294920
  3446.5 101.7 %collective-permute-start.111 = (f32[16,1536]{1,0:T(8,128)S(1)}, f32[16,1536]{1,0:T(8,128)S(1)}, u32[]{:S(2)}, u32[]{:S(2)}) collective-permute-start(f32[16,1536]{1,0:T(8,128)S(1)} %copy-done.34), channel_id=1, source_target_pairs={{0,16},{1,17},{2,18},{3,19},{4,20},{5,21},{6,22},{7,23},{8,24},{9,... | collective-permute-start | bytes 294920
  3537.7 62.7 %collective-permute-start.108 = (f32[16,1536]{1,0:T(8,128)S(1)}, f32[16,1536]{1,0:T(8,128)S(1)}, u32[]{:S(2)}, u32[]{:S(2)}) collective-permute-start(f32[16,1536]{1,0:T(8,128)S(1)} %copy-done.34), channel_id=1, source_target_pairs={{0,13},{1,14},{2,15},{3,16},{4,17},{5,18},{6,19},{7,20},{8,21},{9,... | collective-permute-start | bytes 294920
  (380 other events, 24394.5 us)
Sparse Core Ops, SparseCore 0:
  9.7 300.5 all-gather.24
  312.0 301.2 all-gather.26
  616.3 47.8 all-gather.14
  665.7 309.3 all-gather.28
  976.7 312.4 all-gather.30
  1291.8 47.2 all-gather.16
  1340.7 65.8 all-gather.20
  1408.2 60.0 all-gather.18
  1470.0 52.5 all-gather.22
  1980.5 66.5 reduce-scatter.25
  2051.1 70.8 reduce-scatter.27
  2124.2 125.8 reduce-scatter.23
  2252.6 133.2 reduce-scatter.19
  2388.2 130.8 reduce-scatter.21
where the time goes:
time: 3750 us; the launch traced here: 3730 us
  blocking collectives  1410 us (38%)
  waiting for transfers between devices  1370 us (37%)
  starting transfers between devices  514 us (14%)
  local copies, waits for them, and re-layouts  227 us (6%)
  matrix products  136 us (4%)
  other arithmetic  52.5 us (1%)
    unnamed x3, blocking collectives  1000 us
    unnamed x162, starting transfers between devices  490 us
    all_gather x1, blocking collectives, local(): lax.all_gather(w_router, ('dp', 'expert'), axis=0, tiled=True)  411 us
    all_gather x1, waiting for transfers between devices, local(): lax.all_gather(w_query, ('dp', 'expert'), axis=0, tiled=True)  309 us
    all_gather x1, waiting for transfers between devices, local(): lax.all_gather(w_output, ('dp', 'expert'), axis=0, tiled=True)  306 us
    all_gather x1, waiting for transfers between devices, local(): lax.all_gather(w_key, ('dp', 'expert'), axis=0, tiled=True)  298 us
    all_gather x1, waiting for transfers between devices, local(): lax.all_gather(w_value, ('dp', 'expert'), axis=0, tiled=True)  230 us
    unnamed x482, local copies, waits for them, and re-layouts  189 us
  transfers between devices with their start and end apart: 178, of which 19 were waited for; matrix products, arithmetic and copies ran while one was open for 32% of the time, Pallas kernels for 0%

commit v1 on v0

v1 whole, which is shorter than its diff:
```python
import math

import jax
import jax.numpy as jnp
from jax import lax
from jax.experimental import pallas as pl
from jax.experimental.pallas import tpu as pltpu
from jax.sharding import PartitionSpec as P

HEADS = 24
KV_HEADS = 8
HEAD = 64
DIM = 1536
FFE = 512
EXPERTS = 40
LOCAL = 5
CAP = 32
TOK = 128
PEERS = 8
DP = 16
GROUP = TOK * PEERS
REP = HEADS // KV_HEADS
SLICE = 384
QS = REP * HEAD
ROWS = 96

epsilon = 1e-06
rope_base = 10000.0
masked_score = -1e30
MESH = pl.DeviceIdType.MESH
BF = jnp.bfloat16
F32 = jnp.float32

RELATIVE = ((2, 1), (2, 0), (1, 1), (3, 1), (0, 1), (1, 0), (3, 0))
SLOTS = ((0, 0), (1, 0), (0, 1), (0, 3), (1, 1), (1, 3), (0, 2), (1, 2))


def expert_peers():
    me = lax.axis_index("expert")
    z, x = me // 2, me % 2
    return me, [(z + rz) % 4 * 2 + (x + rx) % 2 for rz, rx in RELATIVE]


def dp_place():
    d = lax.axis_index("dp")
    return d // 8, (d // 2) % 4, d % 2


def dp_index(x, y, core):
    return (x % 2 * 4 + y % 4) * 2 + core % 2


def signal_all(expert_ids, dp_ids):
    barrier = pltpu.get_barrier_semaphore()
    for p in expert_ids:
        pl.semaphore_signal(barrier, inc=1, device_id={"expert": p}, device_id_type=MESH)
    for p in dp_ids:
        pl.semaphore_signal(barrier, inc=1, device_id={"dp": p}, device_id_type=MESH)
    pl.semaphore_wait(barrier, len(expert_ids) + len(dp_ids))


def any_specs(count):
    return [pl.BlockSpec(memory_space=pl.ANY)] * count


def expert_copies(ins, outs, modes, send, recv):
    me, peers = expert_peers()
    copies = []
    for r, p in enumerate(peers):
        for i, mode in enumerate(modes):
            copies.append(
                pltpu.make_async_remote_copy(
                    src_ref=ins[i] if mode == "gather" else ins[i].at[p],
                    dst_ref=outs[i].at[me],
                    send_sem=send.at[i, r],
                    recv_sem=recv.at[i, r],
                    device_id={"expert": p},
                    device_id_type=MESH,
                )
            )
    return copies


def own_copies(ins, outs, modes, sems):
    me = lax.axis_index("expert")
    return [
        pltpu.make_async_copy(
            ins[i] if mode == "gather" else ins[i].at[me], outs[i].at[me], sems.at[i]
        )
        for i, mode in enumerate(modes)
    ]


def exchange(arrays, modes, cid):
    n = len(arrays)

    def kernel(*refs):
        ins, outs = refs[:n], refs[n : 2 * n]
        send, recv, local = refs[2 * n :]
        _, peers = expert_peers()
        signal_all(peers, [])
        copies = expert_copies(ins, outs, modes, send, recv) + own_copies(ins, outs, modes, local)
        for c in copies:
            c.start()
        for c in copies:
            c.wait()

    shapes = [
        jax.ShapeDtypeStruct(((PEERS,) + a.shape) if m == "gather" else a.shape, a.dtype)
        for a, m in zip(arrays, modes)
    ]
    return pl.pallas_call(
        kernel,
        out_shape=shapes,
        in_specs=any_specs(n),
        out_specs=any_specs(n),
        scratch_shapes=[
            pltpu.SemaphoreType.DMA((n, 7)),
            pltpu.SemaphoreType.DMA((n, 7)),
            pltpu.SemaphoreType.DMA((n,)),
        ],
        compiler_params=pltpu.CompilerParams(collective_id=cid, has_side_effects=True),
    )(*arrays)


def gather_start(dense, arrays, modes, cid):
    m, n = len(dense), len(arrays)

    def kernel(*refs):
        dins, ins = refs[:m], refs[m : m + n]
        douts, outs = refs[m + n : 2 * m + n], refs[2 * m + n : 2 * (m + n)]
        dsend, drecv, dlocal, send, recv, local = refs[2 * (m + n) :]
        x, y, core = dp_place()
        mine = dp_index(x, y, core)
        to_x, to_up, to_down, to_core = (
            dp_index(x + 1, y, core),
            dp_index(x, y + 1, core),
            dp_index(x, y + 3, core),
            dp_index(x, y, core + 1),
        )
        _, peers = expert_peers()
        signal_all(peers, [to_x, to_up, to_down, to_core])

        def move(i, k, slot, target, src=None):
            return pltpu.make_async_remote_copy(
                src_ref=douts[i].at[slot] if src is None else src,
                dst_ref=douts[i].at[slot],
                send_sem=dsend.at[i, k],
                recv_sem=drecv.at[i, k],
                device_id={"dp": target},
                device_id_type=MESH,
            )

        def arrived(i, k, slot):
            move(i, k, slot, to_x).wait_recv()

        started = []

        def go(c):
            c.start()
            started.append(c)

        sibling = [dp_index(x + rx, y + ry, core) for rx, ry in SLOTS]
        locals_ = []
        for i in range(m):
            c = pltpu.make_async_copy(dins[i], douts[i].at[mine], dlocal.at[i])
            c.start()
            locals_.append(c)
            go(move(i, 0, mine, to_x, dins[i]))
            go(move(i, 1, mine, to_up, dins[i]))
            go(move(i, 2, mine, to_down, dins[i]))
            go(move(i, 7, mine, to_core, dins[i]))
        more = expert_copies(ins, outs, modes, send, recv) + own_copies(ins, outs, modes, local)
        for c in more:
            c.start()
        for i in range(m):
            arrived(i, 0, sibling[1])
            go(move(i, 3, sibling[1], to_up))
            go(move(i, 4, sibling[1], to_down))
            go(move(i, 8, sibling[1], to_core))
            arrived(i, 1, sibling[3])
            go(move(i, 5, sibling[3], to_up))
            go(move(i, 10, sibling[3], to_core))
            arrived(i, 2, sibling[2])
            go(move(i, 9, sibling[2], to_core))
        for i in range(m):
            arrived(i, 4, sibling[4])
            go(move(i, 6, sibling[4], to_down))
            go(move(i, 11, sibling[4], to_core))
            arrived(i, 3, sibling[5])
            go(move(i, 12, sibling[5], to_core))
        for i in range(m):
            arrived(i, 5, sibling[6])
            go(move(i, 13, sibling[6], to_core))
            arrived(i, 6, sibling[7])
            go(move(i, 14, sibling[7], to_core))
        for i in range(m):
            for k in range(8):
                rx, ry = SLOTS[k]
                arrived(i, 7 + k, dp_index(x + rx, y + ry, core + 1))
        for c in started:
            c.wait_send()
        for c in more + locals_:
            c.wait()

    shapes = [jax.ShapeDtypeStruct((DP,) + a.shape, a.dtype) for a in dense] + [
        jax.ShapeDtypeStruct(((PEERS,) + a.shape) if k == "gather" else a.shape, a.dtype)
        for a, k in zip(arrays, modes)
    ]
    return pl.pallas_call(
        kernel,
        out_shape=shapes,
        in_specs=any_specs(m + n),
        out_specs=any_specs(m + n),
        scratch_shapes=[
            pltpu.SemaphoreType.DMA((m, 15)),
            pltpu.SemaphoreType.DMA((m, 15)),
            pltpu.SemaphoreType.DMA((m,)),
            pltpu.SemaphoreType.DMA((n, 7)),
            pltpu.SemaphoreType.DMA((n, 7)),
            pltpu.SemaphoreType.DMA((n,)),
        ],
        compiler_params=pltpu.CompilerParams(collective_id=cid, has_side_effects=True),
    )(*dense, *arrays)


def exchange_and_share(arrays, modes, pieces, cid):
    n, m = len(arrays), len(pieces)

    def kernel(*refs):
        ins, parts = refs[:n], refs[n : n + m]
        outs, shared = refs[n + m : 2 * n + m], refs[2 * n + m]
        send, recv, local, csend, crecv = refs[2 * n + m + 1 :]
        x, y, core = dp_place()
        other = dp_index(x, y, core + 1)
        _, peers = expert_peers()
        signal_all(peers, [other])
        copies = expert_copies(ins, outs, modes, send, recv) + own_copies(ins, outs, modes, local)
        for k in range(m):
            copies.append(
                pltpu.make_async_remote_copy(
                    src_ref=parts[k],
                    dst_ref=shared.at[k],
                    send_sem=csend.at[k],
                    recv_sem=crecv.at[k],
                    device_id={"dp": other},
                    device_id_type=MESH,
                )
            )
        for c in copies:
            c.start()
        for c in copies:
            c.wait()

    shapes = [
        jax.ShapeDtypeStruct(((PEERS,) + a.shape) if k == "gather" else a.shape, a.dtype)
        for a, k in zip(arrays, modes)
    ] + [jax.ShapeDtypeStruct((m,) + pieces[0].shape, pieces[0].dtype)]
    return pl.pallas_call(
        kernel,
        out_shape=shapes,
        in_specs=any_specs(n + m),
        out_specs=any_specs(n + 1),
        scratch_shapes=[
            pltpu.SemaphoreType.DMA((n, 7)),
            pltpu.SemaphoreType.DMA((n, 7)),
            pltpu.SemaphoreType.DMA((n,)),
            pltpu.SemaphoreType.DMA((m,)),
            pltpu.SemaphoreType.DMA((m,)),
        ],
        compiler_params=pltpu.CompilerParams(collective_id=cid, has_side_effects=True),
    )(*arrays, *pieces)


def scatter_sum(arrays, dense, cid):
    n = len(arrays)
    _, rows, cols = dense.shape

    def kernel(*refs):
        ins, dref = refs[:n], refs[n]
        outs, total = refs[n + 1 : 2 * n + 1], refs[2 * n + 1]
        send, recv, local, mine, theirs, summed, got, lsem, csend, crecv, dsend, drecv = refs[
            2 * n + 2 :
        ]
        x, y, core = dp_place()
        to_core = dp_index(x, y, core + 1)
        targets = [dp_index(x + rx, y + ry, core) for rx, ry in SLOTS[1:]]
        _, peers = expert_peers()
        signal_all(peers, [to_core] + targets)
        modes = ["exchange"] * n
        loads, shares = [], []
        for k, (rx, ry) in enumerate(SLOTS):
            c = pltpu.make_async_remote_copy(
                src_ref=dref.at[dp_index(x + rx, y + ry, core + 1)],
                dst_ref=theirs.at[k],
                send_sem=csend.at[k],
                recv_sem=crecv.at[k],
                device_id={"dp": to_core},
                device_id_type=MESH,
            )
            c.start()
            shares.append(c)
            c = pltpu.make_async_copy(
                dref.at[dp_index(x + rx, y + ry, core)], mine.at[k], lsem.at[k]
            )
            c.start()
            loads.append(c)
        copies = expert_copies(ins, outs, modes, send, recv) + own_copies(ins, outs, modes, local)
        for c in copies:
            c.start()
        moves = []
        for k in range(8):
            loads[k].wait()
            shares[k].wait_recv()
            summed[k] = (mine[k].astype(F32) + theirs[k].astype(F32)).astype(BF)
            if k > 0:
                c = pltpu.make_async_remote_copy(
                    src_ref=summed.at[k],
                    dst_ref=got.at[k - 1],
                    send_sem=dsend.at[k - 1],
                    recv_sem=drecv.at[k - 1],
                    device_id={"dp": targets[k - 1]},
                    device_id_type=MESH,
                )
                c.start()
                moves.append(c)
        acc = summed[0].astype(F32)
        for k, c in enumerate(moves):
            c.wait_recv()
            acc = acc + got[k].astype(F32)
        total[...] = acc
        for c in moves:
            c.wait_send()
        for c in shares:
            c.wait_send()
        for c in copies:
            c.wait()

    shapes = [jax.ShapeDtypeStruct(a.shape, a.dtype) for a in arrays] + [
        jax.ShapeDtypeStruct((rows, cols), F32)
    ]
    return pl.pallas_call(
        kernel,
        out_shape=shapes,
        in_specs=any_specs(n + 1),
        out_specs=any_specs(n) + [pl.BlockSpec(memory_space=pltpu.VMEM)],
        scratch_shapes=[
            pltpu.SemaphoreType.DMA((n, 7)),
            pltpu.SemaphoreType.DMA((n, 7)),
            pltpu.SemaphoreType.DMA((n,)),
            pltpu.VMEM((8, rows, cols), BF),
            pltpu.VMEM((8, rows, cols), BF),
            pltpu.VMEM((8, rows, cols), BF),
            pltpu.VMEM((7, rows, cols), BF),
            pltpu.SemaphoreType.DMA((8,)),
            pltpu.SemaphoreType.DMA((8,)),
            pltpu.SemaphoreType.DMA((8,)),
            pltpu.SemaphoreType.DMA((7,)),
            pltpu.SemaphoreType.DMA((7,)),
        ],
        compiler_params=pltpu.CompilerParams(
            collective_id=cid, has_side_effects=True, vmem_limit_bytes=40 << 20
        ),
    )(*arrays, dense)


def dot(a, b, contract):
    return lax.dot_general(a, b, ((contract[0], contract[1]), ((), ())), preferred_element_type=F32)


def experts_kernel(*refs):
    (rows_ref, cot_ref, slot_ref, gate_ref), refs = refs[:4], refs[4:]
    pieces, shared, refs = refs[:8], refs[8], refs[9:]
    (out_ref, back_ref, inner_ref, keep_ref, give_ref), refs = refs[:5], refs[5:]
    xg, cg, weights, grads, gates, inners, wsem, gsem = refs
    x, y, core = dp_place()

    def loads(e, b):
        copies = []
        for k, (rx, ry) in enumerate(SLOTS):
            for c in range(2):
                src = pieces[k].at[e] if c == 0 else shared.at[k, e]
                copies.append(
                    pltpu.make_async_copy(
                        src,
                        weights.at[b, dp_index(x + rx, y + ry, core + c)],
                        wsem.at[b, 2 * k + c],
                    )
                )
        return copies

    def stores(e, b):
        copies = []
        for k, (rx, ry) in enumerate(SLOTS):
            for c in range(2):
                dst = keep_ref.at[k, e] if c == 0 else give_ref.at[k, e]
                copies.append(
                    pltpu.make_async_copy(
                        grads.at[b, dp_index(x + rx, y + ry, core + c)],
                        dst,
                        gsem.at[b, 2 * k + c],
                    )
                )
        return copies

    for c in loads(0, 0):
        c.start()

    def onehot(b):
        places = lax.broadcasted_iota(jnp.int32, (CAP, TOK), 0).astype(F32)
        return [(places == slot_ref[b, e : e + 1, :]) for e in range(LOCAL)]

    def collect(b, _):
        hot = onehot(b)
        pick = jnp.concatenate([h.astype(F32) for h in hot], axis=0).astype(BF)
        xg[b] = dot(pick, rows_ref[b], ((1,), (0,))).astype(BF)
        cg[b] = dot(pick, cot_ref[b], ((1,), (0,))).astype(BF)
        for e in range(LOCAL):
            g = jnp.sum(jnp.where(hot[e], gate_ref[b, e : e + 1, :], 0.0), axis=1, keepdims=True)
            gates[e, pl.ds(b * CAP, CAP), :] = jnp.broadcast_to(g, (CAP, 128))
        return _

    lax.fori_loop(0, PEERS, collect, 0)

    def expert(e, _):
        b = lax.rem(e, 2)
        for c in loads(e, b):
            c.wait()

        @pl.when(e + 1 < LOCAL)
        def _next():
            for c in loads(e + 1, 1 - b):
                c.start()

        @pl.when(e >= 2)
        def _free():
            for c in stores(e - 2, b):
                c.wait()

        span = pl.ds(pl.multiple_of(e * CAP, CAP), CAP)
        rows = xg[:, span, :].reshape(PEERS * CAP, DIM)
        cot = cg[:, span, :].reshape(PEERS * CAP, DIM)
        gate = gates[e][:, :1]
        w_gate = weights[b, :, 0:96, :].reshape(DIM, FFE)
        gate_act = dot(rows, w_gate, ((1,), (0,)))
        w_up = weights[b, :, 96:192, :].reshape(DIM, FFE)
        up_act = dot(rows, w_up, ((1,), (0,)))
        sig = 1.0 / (1.0 + jnp.exp(-gate_act))
        silu = gate_act * sig
        hidden = (silu * up_act).astype(BF)
        grad_out = (cot.astype(F32) * gate).astype(BF)
        inner = jnp.zeros((PEERS * CAP, 1), F32)
        grad_hidden = jnp.zeros((PEERS * CAP, FFE), F32)
        gated = []
        for k in range(3):
            lanes = slice(k * FFE, (k + 1) * FFE)
            w_down = weights[b, :, 192 + 32 * k : 224 + 32 * k, :].reshape(FFE, FFE)
            part = dot(hidden, w_down, ((1,), (0,))).astype(BF).astype(F32)
            inner = inner + jnp.sum(part * cot[:, lanes].astype(F32), axis=1, keepdims=True)
            gated.append((part * gate).astype(BF))
            grad_hidden = grad_hidden + dot(grad_out[:, lanes], w_down, ((1,), (1,)))
            grads[b, :, 192 + 32 * k : 224 + 32 * k, :] = (
                dot(hidden, grad_out[:, lanes], ((0,), (0,))).astype(BF).reshape(DP, 32, FFE)
            )
        inners[e] = jnp.broadcast_to(inner, (PEERS * CAP, 128))
        grad_gate = (grad_hidden * up_act * sig * (1.0 + gate_act * (1.0 - sig))).astype(BF)
        grad_up = (grad_hidden * silu).astype(BF)
        grads[b, :, 0:96, :] = (
            dot(rows, grad_gate, ((0,), (0,))).astype(BF).reshape(DP, ROWS, FFE)
        )
        grads[b, :, 96:192, :] = (
            dot(rows, grad_up, ((0,), (0,))).astype(BF).reshape(DP, ROWS, FFE)
        )
        for c in stores(e, b):
            c.start()
        back = dot(grad_gate, w_gate, ((1,), (1,))) + dot(grad_up, w_up, ((1,), (1,)))
        xg[:, span, :] = back.astype(BF).reshape(PEERS, CAP, DIM)
        for k in range(3):
            cg[:, span, k * FFE : (k + 1) * FFE] = gated[k].reshape(PEERS, CAP, FFE)
        return _

    lax.fori_loop(0, LOCAL, expert, 0)

    def combine(b, _):
        hot = onehot(b)
        pick = jnp.concatenate([h.astype(F32) for h in hot], axis=0).astype(BF)
        out_ref[b] = dot(pick, cg[b], ((0,), (0,))).astype(BF)
        back_ref[b] = dot(pick, xg[b], ((0,), (0,))).astype(BF)
        lines = []
        for e in range(LOCAL):
            value = inners[e, pl.ds(b * CAP, CAP), :][:, :1]
            lines.append(jnp.sum(jnp.where(hot[e], value, 0.0), axis=0, keepdims=True))
        inner_ref[b] = jnp.concatenate(lines + [jnp.zeros((8 - LOCAL, TOK), F32)], axis=0)
        return _

    lax.fori_loop(0, PEERS, combine, 0)
    for e in (LOCAL - 2, LOCAL - 1):
        for c in stores(e, e % 2):
            c.wait()


def run_experts(rows, cot, slots, gates, pieces, shared):
    vmem = pl.BlockSpec(memory_space=pltpu.VMEM)
    piece = (LOCAL, 3 * ROWS, FFE)
    return pl.pallas_call(
        experts_kernel,
        out_shape=[
            jax.ShapeDtypeStruct((PEERS, TOK, DIM), BF),
            jax.ShapeDtypeStruct((PEERS, TOK, DIM), BF),
            jax.ShapeDtypeStruct((PEERS, 8, TOK), F32),
            jax.ShapeDtypeStruct((8,) + piece, BF),
            jax.ShapeDtypeStruct((8,) + piece, BF),
        ],
        in_specs=[vmem] * 4 + any_specs(9),
        out_specs=[vmem] * 3 + any_specs(2),
        scratch_shapes=[
            pltpu.VMEM((PEERS, LOCAL * CAP, DIM), BF),
            pltpu.VMEM((PEERS, LOCAL * CAP, DIM), BF),
            pltpu.VMEM((2, DP, 3 * ROWS, FFE), BF),
            pltpu.VMEM((2, DP, 3 * ROWS, FFE), BF),
            pltpu.VMEM((LOCAL, PEERS * CAP, 128), F32),
            pltpu.VMEM((LOCAL, PEERS * CAP, 128), F32),
            pltpu.SemaphoreType.DMA((2, 16)),
            pltpu.SemaphoreType.DMA((2, 16)),
        ],
        compiler_params=pltpu.CompilerParams(vmem_limit_bytes=60 << 20),
        cost_estimate=pl.CostEstimate(
            flops=20_000_000_000, bytes_accessed=60_000_000, transcendentals=700_000
        ),
    )(rows, cot, slots, gates, *pieces, shared)


def shift(value, move):
    pairs = []
    for d in range(DP):
        x, y, core = move(d // 8, d // 2 % 4, d % 2)
        pairs.append((d, (x % 2 * 4 + y % 4) * 2 + core % 2))
    return lax.ppermute(value, "dp", pairs)


def up(value):
    return shift(value, lambda x, y, c: (x, y + 1, c))


def down(value):
    return shift(value, lambda x, y, c: (x, y + 3, c))


def across(value):
    return shift(value, lambda x, y, c: (x + 1, y, c))


def other_core(value):
    return shift(value, lambda x, y, c: (x, y, c + 1))


def add(a, b):
    return (a.astype(F32) + b.astype(F32)).astype(BF)


def rms_scale(values):
    return lax.rsqrt(jnp.mean(values * values, axis=-1, keepdims=True) + epsilon)


def rope_tables(offsets, head_width):
    exponent = jnp.arange(head_width // 2, dtype=jnp.float32) * (2.0 / head_width)
    frequency = jnp.exp(-exponent * math.log(rope_base))
    phase_angles = offsets.astype(jnp.float32)[:, None] * frequency[None, :]
    return (jnp.cos(phase_angles)[:, None, :], jnp.sin(phase_angles)[:, None, :])


def rotate(values, cosine, sine_table):
    half = values.shape[-1] // 2
    first, second = values[..., :half], values[..., half:]
    return jnp.concatenate(
        [first * cosine - second * sine_table, second * cosine + first * sine_table], axis=-1
    )


def layout(lengths, group_count):
    seq_ends = jnp.cumsum(lengths)
    starts = seq_ends - lengths
    places = jnp.arange(group_count, dtype=jnp.int32)
    member = ((places[:, None] >= starts[None, :]) & (places[:, None] < seq_ends[None, :])).astype(
        jnp.int32
    )
    numbers = jnp.arange(lengths.shape[0], dtype=jnp.int32)
    segment = jnp.sum(member * numbers[None, :], axis=1)
    offsets = places - jnp.sum(member * starts[None, :], axis=1)
    return (segment, offsets)


def norm_back(values, row_scale, gain_vector, grad_normed):
    weighted = grad_normed * gain_vector
    return row_scale * weighted - values * row_scale**3 * jnp.mean(
        weighted * values, axis=-1, keepdims=True
    )


def by_peer(table):
    return jnp.pad(table.reshape(PEERS, LOCAL, TOK), ((0, 0), (0, 8 - LOCAL), (0, 0)))


def local(
    tokens,
    cotangent,
    seq_lengths,
    expert_ids,
    w_query,
    w_key,
    w_value,
    w_output,
    norm_one,
    norm_two,
    w_router,
    w_gate,
    w_up,
    w_down,
):
    score_scale = HEAD ** (-0.5)
    down_piece = w_down.reshape(LOCAL, 32, 3, FFE).transpose(0, 2, 1, 3).reshape(LOCAL, ROWS, FFE)
    piece = jnp.concatenate([w_gate, w_up, down_piece], axis=1)

    slices = jnp.concatenate(
        [
            w_query.reshape(12, PEERS, QS).transpose(1, 0, 2),
            w_key.reshape(12, PEERS, HEAD).transpose(1, 0, 2),
            w_value.reshape(12, PEERS, HEAD).transpose(1, 0, 2),
            jnp.broadcast_to(
                jnp.concatenate(
                    [
                        norm_one[:, None],
                        norm_two[:, None],
                        w_router,
                        jnp.zeros((12, SLICE - QS - 2 * HEAD - 2 - EXPERTS), BF),
                    ],
                    axis=1,
                )[None],
                (PEERS, 12, SLICE - QS - 2 * HEAD),
            ),
        ],
        axis=2,
    )
    slices_rows, output_rows = exchange([slices, w_output], ["exchange", "gather"], 1)
    slices_rows = slices_rows.reshape(ROWS, SLICE)
    output_rows = output_rows.reshape(ROWS, DIM)

    member = jnp.any(
        expert_ids[None, :, :] == jnp.arange(EXPERTS, dtype=jnp.int32)[:, None, None], axis=-1
    )
    before = jnp.arange(TOK)[:, None] < jnp.arange(TOK)[None, :]
    places = jnp.dot(member.astype(BF), before.astype(BF), preferred_element_type=F32)
    slot_table = by_peer(jnp.where(member, places, -1.0))

    slices_all, output_all, tokens_all, cot_all, slots_all = gather_start(
        [slices_rows, output_rows],
        [tokens, cotangent, slot_table],
        ["gather", "gather", "exchange"],
        2,
    )
    piece, _ = lax.optimization_barrier((piece, slots_all))
    x1 = across(piece)
    y3, y1 = up(piece), down(piece)
    x1y3, x1y1 = up(x1), down(x1)
    y2, x1y2 = up(y3), down(x1y1)
    pieces = [piece, x1, y1, y3, x1y1, x1y3, y2, x1y2]

    slices_all = slices_all.reshape(DIM, SLICE)
    output_all = output_all.reshape(DIM, DIM)
    qkv_all = slices_all[:, : QS + 2 * HEAD]
    gains = slices_all[:, QS + 2 * HEAD : QS + 2 * HEAD + 2].astype(F32).T
    gain_one, gain_two = gains[0], gains[1]
    router_all = slices_all[:, QS + 2 * HEAD + 2 : QS + 2 * HEAD + 2 + EXPERTS]

    segment, offsets = layout(seq_lengths[0], GROUP)
    cosine, sine_table = rope_tables(offsets, HEAD)
    places = jnp.arange(GROUP, dtype=jnp.int32)
    allowed = (segment[:, None] == segment[None, :]) & (places[None, :] <= places[:, None])

    inputs_all = tokens_all.reshape(GROUP, DIM).astype(F32)
    scale_all = rms_scale(inputs_all)
    normed_all = (inputs_all * scale_all * gain_one).astype(BF)
    qkv = jnp.dot(normed_all, qkv_all, preferred_element_type=F32)
    heads = rotate(
        qkv[:, : QS + HEAD].reshape(GROUP, REP + 1, HEAD), cosine, sine_table
    ).astype(BF)
    query, key = heads[:, :REP], heads[:, REP]
    value = qkv[:, QS + HEAD :].astype(BF)
    scores = jnp.einsum("qrh,kh->rqk", query, key, preferred_element_type=F32) * score_scale
    scores = jnp.where(allowed, scores, masked_score)
    highest = jnp.max(scores, axis=-1, keepdims=True)
    terms = jnp.exp(scores - highest)
    probs = terms / jnp.sum(terms, axis=-1, keepdims=True)
    probs_low = probs.astype(BF)
    attended = jnp.einsum("rqk,kh->qrh", probs_low, value, preferred_element_type=F32).astype(BF)
    (attended,) = exchange([attended.reshape(PEERS, TOK, QS)], ["exchange"], 3)
    attended = attended.transpose(1, 0, 2).reshape(TOK, DIM)

    inputs = tokens.astype(F32)
    middle = inputs + jnp.dot(attended, output_all, preferred_element_type=F32)
    scale_two = rms_scale(middle)
    normed_two = (middle * scale_two * gain_two).astype(BF)
    logits = lax.dot_general(
        router_all, normed_two, (((0,), (1,)), ((), ())), preferred_element_type=F32
    )
    chosen = jnp.where(member, logits, masked_score)
    weight = jnp.where(member, jnp.exp(chosen - jnp.max(chosen, axis=0, keepdims=True)), 0.0)
    gate_values = weight / jnp.sum(weight, axis=0, keepdims=True)

    rows_all, gates_all, shared = exchange_and_share(
        [normed_two, by_peer(gate_values)], ["gather", "exchange"], pieces, 4
    )
    out_part, back_part, inner_part, keep, give = run_experts(
        rows_all, cot_all, slots_all, gates_all, pieces, shared
    )

    given = other_core(give)
    sums = {s: add(keep[k], given[k]) for k, s in enumerate(SLOTS)}
    sums[(0, 1)] = add(sums[(0, 1)], up(sums[(0, 2)]))
    sums[(1, 3)] = add(sums[(1, 3)], down(sums[(1, 2)]))
    halves = [
        (
            sums[(r, 0)].astype(F32)
            + up(sums[(r, 1)]).astype(F32)
            + down(sums[(r, 3)]).astype(F32)
        )
        for r in (0, 1)
    ]
    expert_grads = halves[0] + across(halves[1].astype(BF)).astype(F32)

    back_all, inner_all = exchange([back_part, inner_part], ["exchange", "exchange"], 5)
    grad_normed_two = jnp.sum(back_all.astype(F32), axis=0)
    grad_gates = inner_all[:, :LOCAL, :].reshape(EXPERTS, TOK)
    grad_chosen = gate_values * (
        grad_gates - jnp.sum(gate_values * grad_gates, axis=0, keepdims=True)
    )
    grad_logits = grad_chosen.astype(BF)
    grad_out = cotangent.astype(F32)
    grad_router = lax.dot_general(
        normed_two, grad_logits, (((0,), (1,)), ((), ())), preferred_element_type=F32
    )
    grad_normed_two = grad_normed_two + lax.dot_general(
        grad_logits, router_all, (((0,), (1,)), ((), ())), preferred_element_type=F32
    )
    grad_gain_two = jnp.sum(grad_normed_two * middle * scale_two, axis=0)
    grad_middle = grad_out + norm_back(middle, scale_two, gain_two, grad_normed_two)
    grad_branch = grad_middle.astype(BF)
    grad_attended = lax.dot_general(
        grad_branch, output_all, (((1,), (1,)), ((), ())), preferred_element_type=F32
    ).astype(BF)
    grad_attended = grad_attended.reshape(TOK, PEERS, QS).transpose(1, 0, 2)
    (grad_attended,) = exchange([grad_attended], ["exchange"], 6)
    grad_attended = grad_attended.reshape(GROUP, REP, HEAD)
    grad_output = lax.dot_general(
        attended, grad_branch, (((0,), (0,)), ((), ())), preferred_element_type=F32
    )

    grad_probs = jnp.einsum("qrh,kh->rqk", grad_attended, value, preferred_element_type=F32)
    grad_scores = (
        probs * (grad_probs - jnp.sum(probs * grad_probs, axis=-1, keepdims=True))
    ).astype(BF)
    grad_query = (
        jnp.einsum("rqk,kh->qrh", grad_scores, key, preferred_element_type=F32) * score_scale
    )
    grad_key = (
        jnp.einsum("rqk,qrh->kh", grad_scores, query, preferred_element_type=F32) * score_scale
    )
    grad_value = jnp.einsum("rqk,qrh->kh", probs_low, grad_attended, preferred_element_type=F32)
    grad_heads = rotate(
        jnp.concatenate([grad_query, grad_key[:, None, :]], axis=1), cosine, -sine_table
    ).reshape(GROUP, QS + HEAD)
    grad_qkv = jnp.concatenate([grad_heads, grad_value], axis=1).astype(BF)
    grad_slices = lax.dot_general(
        normed_all, grad_qkv, (((0,), (0,)), ((), ())), preferred_element_type=F32
    )
    grad_normed = lax.dot_general(
        grad_qkv, qkv_all, (((1,), (1,)), ((), ())), preferred_element_type=F32
    )
    grad_gain_one = jnp.sum(grad_normed * inputs_all * scale_all, axis=0)
    dense = jnp.concatenate(
        [
            grad_slices,
            grad_gain_one[:, None],
            grad_gain_two[:, None],
            grad_router,
            jnp.zeros((DIM, SLICE - QS - 2 * HEAD - 2 - EXPERTS), F32),
            grad_output,
        ],
        axis=1,
    ).astype(BF)
    normed_back, out_all, dense_rows = scatter_sum(
        [grad_normed.astype(BF).reshape(PEERS, TOK, DIM), out_part],
        dense.reshape(DP, ROWS, SLICE + DIM),
        7,
    )
    mixed = middle + jnp.sum(out_all.astype(F32), axis=0)
    grad_tokens = grad_middle + norm_back(
        inputs, scale_all_own(scale_all), gain_one, jnp.sum(normed_back.astype(F32), axis=0)
    )
    (dense_own,) = exchange([dense_rows.reshape(PEERS, 12, SLICE + DIM)], ["exchange"], 8)
    own_sum = jnp.sum(dense_own[:, :, QS + 2 * HEAD :], axis=0)
    last = QS + 2 * HEAD
    return (
        mixed.astype(BF),
        grad_tokens,
        dense_own[:, :, :QS].transpose(1, 0, 2).reshape(12, DIM),
        dense_own[:, :, QS : QS + HEAD].transpose(1, 0, 2).reshape(12, KV_HEADS * HEAD),
        dense_own[:, :, QS + HEAD : last].transpose(1, 0, 2).reshape(12, KV_HEADS * HEAD),
        own_sum[:, SLICE - last :],
        own_sum[:, 0],
        own_sum[:, 1],
        own_sum[:, 2 : 2 + EXPERTS],
        expert_grads[:, :ROWS],
        expert_grads[:, ROWS : 2 * ROWS],
        expert_grads[:, 2 * ROWS :]
        .reshape(LOCAL, 3, 32, FFE)
        .transpose(0, 2, 1, 3)
        .reshape(LOCAL, 32, DIM),
    )


def scale_all_own(scale_all):
    return lax.dynamic_slice_in_dim(scale_all, lax.axis_index("expert") * TOK, TOK)


def solution(mesh):
    both = P(("dp", "expert"), None)
    line = P(("dp", "expert"))
    cube = P("expert", "dp", None)
    in_specs = (both, both, P("dp", None), both, both, both, both, both)
    in_specs = in_specs + (line, line, both, cube, cube, cube)
    out_specs = (both,) * 6 + (line, line, both, cube, cube, cube)
    return jax.shard_map(local, mesh=mesh, in_specs=in_specs, out_specs=out_specs, check_vma=False)
```

time: 3750 us -> 647 us (0.17)
  blocking collectives: 1410 us -> 0 us
  waiting for transfers between devices: 1370 us -> 99.9 us
  starting transfers between devices: 514 us -> 16.8 us
  Pallas kernels: 0 us -> 349 us
  local copies, waits for them, and re-layouts: 227 us -> 67.1 us
  matrix products: 136 us -> 53.6 us
    all_gather x9 -> x0, waiting for transfers between devices: 1210 us -> none  [the longest x1 309 us: local(): lax.all_gather(w_query, ('dp', 'expert'), axis=0, tiled=True)]
    unnamed x3 -> x0, blocking collectives: 1000 us -> none
    unnamed x162 -> x0, starting transfers between devices: 490 us -> none
    all_gather x1 -> x0, blocking collectives: 411 us -> none  [local(): lax.all_gather(w_router, ('dp', 'expert'), axis=0, tiled=True)]
    pallas_call x0 -> x9, Pallas kernels: none -> 349 us  [the longest x1 104 us: scatter_sum(): pl.pallas_call(kernel, out_shape=shapes, in_specs=any_specs(n + 1), out_s...]
    unnamed x482 -> x124, local copies, waits for them, and re-layouts: 189 us -> 11.6 us
    unnamed x176 -> x0, waiting for transfers between devices: 104 us -> none
    ppermute x0 -> x15, waiting for transfers between devices: none -> 99.9 us  [shift(): return lax.ppermute(value, 'dp', pairs)]
  transfers between devices with their start and end apart: 178 -> 15, of which waited for: 19 -> 9; matrix products, arithmetic and copies ran while one was open for 32% -> 21% of each run, Pallas kernels for 0% -> 28%
where the time goes in v1:
time: 647 us; the launch traced here: 637 us
  Pallas kernels  349 us (54%)
  waiting for transfers between devices  99.9 us (15%)
  local copies, waits for them, and re-layouts  67.1 us (10%)
  matrix products  53.6 us (8%)
  other arithmetic  49.4 us (8%)
  starting transfers between devices  16.8 us (3%)
    pallas_call x1, Pallas kernels, scatter_sum(): pl.pallas_call(kernel, out_shape=shapes, in_specs=any_specs(n + 1), out_s...  104 us
    ppermute x15, waiting for transfers between devices, shift(): return lax.ppermute(value, 'dp', pairs)  99.9 us
    pallas_call x5, Pallas kernels, exchange(): pl.pallas_call(kernel, out_shape=shapes, in_specs=any_specs(n), out_specs...  90.8 us
    pallas_call x1, Pallas kernels, gather_start(): pl.pallas_call(kernel, out_shape=shapes, in_specs=any_specs(m + n), out_s...  82.8 us
    pallas_call x1, Pallas kernels, exchange_and_share(): pl.pallas_call(kernel, out_shape=shapes, in_specs=any_specs(n + m), out_s...  37.9 us
    pallas_call x1, Pallas kernels, run_experts(): pl.pallas_call(experts_kernel, out_shape=[jax.ShapeDtypeStruct((PEERS, TO...  33.4 us
    ppermute x15, starting transfers between devices, shift(): return lax.ppermute(value, 'dp', pairs)  16.8 us
    concatenate x3, local copies, waits for them, and re-layouts, local(): jnp.concatenate([grad_slices, grad_gain_one[:, None], grad_gain_two[:, No...  13.4 us
  transfers between devices with their start and end apart: 15, of which 9 were waited for; matrix products, arithmetic and copies ran while one was open for 21% of the time, Pallas kernels for 28%

profile of v1, /device:TPU:0, one launch (start us, length us, event | category | flops | bytes accessed | tf_op | source)
XLA Modules:
  0.0 637.5 jit_solution(2852735783356289771)
XLA Ops:
  6.4 13.7 %shard_map.229 = (bf16[8,12,384]{2,1,0:T(8,128)(2,1)}, bf16[8,12,1536]{2,1,0:T(8,128)(2,1)}) custom-call(bf16[8,12,384]{2,1,0:T(8,128)(2,1)} %pad_maximum_fusion.7.refs_0_, bf16[12,1536]{1,0:T(8,128)(2,1)} %refs_1_.1), custom_call_target="tpu_custom_call" | custom-call | tf_op jit(solution)/shard_map/pallas_call | solution.py:112
  28.8 82.8 %shard_map.230 = (bf16[16,96,384]{2,1,0:T(8,128)(2,1)}, bf16[16,96,1536]{2,1,0:T(8,128)(2,1)}, bf16[8,128,1536]{2,1,0:T(8,128)(2,1)}, bf16[8,128,1536]{2,1,0:T(8,128)(2,1)}, f32[8,8,128]{2,1,0:T(8,128)}) custom-call(bf16[96,384]{1,0:T(8,128)(2,1)} %reshape.319.refs_0_, bf16[96,1536]{1,0:T(8,128)(2,1)} %reshape.320.refs_1_, bf16[128,1536]{1,0:T(8,128)(2,1)} %refs_2_.1, ...), custom_call_target="tpu_custom_call" | custom-call | tf_op jit(solution)/shard_map/pallas_call | solution.py:210
  127.4 7.3 %fusion.79 = (f32[3,1024]{1,0:T(4,128)S(1)}, f32[3,1024,1024]{1,2,0:T(8,128)}) fusion(pred[1024,1024]{0,1:T(8,128)(4,1)S(1)} %fusion.13, bf16[1024,64,1]{0,1,2:T(8,128)(2,1)S(1)} %maximum_bitcast_fusion, bf16[1024,4,32]{0,2,1:T(8,128)(2,1)S(1)} %get-tuple-element.76, bf16[1024,4,32]{0,2,1:T(8,128)(2,1)S(1)} %get-tuple-element.75), kind=kOutput, calls=%fused_computation.161 | convolution fusion | flops 416023552 | bytes 14299136 | tf_op jit(solution)/shard_map/sub | solution.py:692
  134.7 10.0 %collective-permute-done.refs_3_.refs_5_ = bf16[5,288,512]{2,1,0:T(8,128)(2,1)} collective-permute-done((bf16[5,288,512]{2,1,0:T(8,128)(2,1)}, bf16[5,288,512]{2,1,0:T(8,128)(2,1)}, u32[]{:S(2)}, u32[]{:S(2)}) %collective-permute-start) | collective-permute-done | bytes 1474592 | tf_op jit(solution)/shard_map/ppermute | solution.py:538
  148.6 5.9 fusion.35
  155.6 10.0 %shard_map.231 = bf16[8,128,192]{2,1,0:T(8,128)(2,1)} custom-call(bf16[8,128,192]{2,1,0:T(8,128)(2,1)} %copy.72.refs_0_), custom_call_target="tpu_custom_call" | custom-call | tf_op jit(solution)/shard_map/pallas_call | solution.py:112
  167.6 10.9 %collective-permute-done.3.refs_6_.refs_8_ = bf16[5,288,512]{2,1,0:T(8,128)(2,1)S(1)} collective-permute-done((bf16[5,288,512]{2,1,0:T(8,128)(2,1)}, bf16[5,288,512]{2,1,0:T(8,128)(2,1)S(1)}, u32[]{:S(2)}, u32[]{:S(2)}) %collective-permute-start.3) | collective-permute-done | bytes 1474592 | tf_op jit(solution)/shard_map/ppermute | solution.py:538
  188.0 15.8 %collective-permute-done.4.refs_7_.refs_9_ = bf16[5,288,512]{2,1,0:T(8,128)(2,1)} collective-permute-done((bf16[5,288,512]{2,1,0:T(8,128)(2,1)}, bf16[5,288,512]{2,1,0:T(8,128)(2,1)}, u32[]{:S(2)}, u32[]{:S(2)}) %collective-permute-start.4) | collective-permute-done | bytes 1474592 | tf_op jit(solution)/shard_map/ppermute | solution.py:538
  203.8 27.7 %collective-permute-done.5.refs_8_.refs_10_ = bf16[5,288,512]{2,1,0:T(8,128)(2,1)} collective-permute-done((bf16[5,288,512]{2,1,0:T(8,128)(2,1)}, bf16[5,288,512]{2,1,0:T(8,128)(2,1)}, u32[]{:S(2)}, u32[]{:S(2)}) %collective-permute-start.5) | collective-permute-done | bytes 1474592 | tf_op jit(solution)/shard_map/ppermute | solution.py:538
  231.5 37.9 %shard_map.232 = (bf16[8,128,1536]{2,1,0:T(8,128)(2,1)}, f32[8,8,128]{2,1,0:T(8,128)}, bf16[8,5,288,512]{3,2,1,0:T(8,128)(2,1)}) custom-call(bf16[128,1536]{1,0:T(8,128)(2,1)} %copy-done.17, f32[8,8,128]{2,1,0:T(8,128)} %pad.8.refs_1_, bf16[5,288,512]{2,1,0:T(8,128)(2,1)} %pad_maximum_fusion.refs_2_.refs_4_, ...), custom_call_target="tpu_custom_call" | custom-call | tf_op jit(solution)/shard_map/pallas_call | solution.py:259
  269.4 33.4 %shard_map.233 = (bf16[8,128,1536]{2,1,0:T(8,128)(2,1)}, bf16[8,128,1536]{2,1,0:T(8,128)(2,1)}, f32[8,8,128]{2,1,0:T(8,128)}, bf16[8,5,288,512]{3,2,1,0:T(8,128)(2,1)}, bf16[8,5,288,512]{3,2,1,0:T(8,128)(2,1)}) custom-call(bf16[8,128,1536]{2,1,0:T(8,128)(2,1)} %get-tuple-element.40.refs_0_, bf16[8,128,1536]{2,1,0:T(8,128)(2,1)} %get-tuple-element.41.refs_1_, ...), custom_call_target="tpu_custom_call" | custom-call | flops 20000000000 | bytes 60000000 | tf_op jit(solution)/shard_map/pallas_call | solution.py:505
  309.0 40.7 %shard_map.234 = (bf16[8,128,1536]{2,1,0:T(8,128)(2,1)}, f32[8,8,128]{2,1,0:T(8,128)}) custom-call(bf16[8,128,1536]{2,1,0:T(8,128)(2,1)} %get-tuple-element.44.refs_0_, f32[8,8,128]{2,1,0:T(8,128)} %get-tuple-element.45.refs_1_), custom_call_target="tpu_custom_call" | custom-call | tf_op jit(solution)/shard_map/pallas_call | solution.py:112
  361.5 11.6 %shard_map.235 = bf16[8,128,192]{2,1,0:T(8,128)(2,1)} custom-call(bf16[8,128,192]{2,1,0:T(8,128)(2,1)} %bitcast.184), custom_call_target="tpu_custom_call" | custom-call | tf_op jit(solution)/shard_map/pallas_call | solution.py:112
  374.7 5.9 fusion.1
  380.6 7.3 %fusion.3 = bf16[3,1024,1024]{1,2,0:T(8,128)(2,1)S(1)} fusion(f32[1024,1024,3]{1,0,2:T(8,128)S(1)} %get-tuple-element.96, f32[3,1024]{1,0:T(4,128)S(1)} %get-tuple-element.95, f32[3,1024,1024]{1,2,0:T(8,128)} %get-tuple-element.89, f32[3,1024]{1,0:T(4,128)S(1)} %copy-done.47), kind=kLoop, calls=%fused_computation.5 | loop fusion | flops 12582912 | bytes 31481856 | tf_op jit(solution)/shard_map/convert_element_type | solution.py:761
  395.4 5.5 fusion.26
  407.6 6.0 fusion.9
  421.3 13.3 %collective-permute-done.12 = bf16[5,288,512]{2,1,0:T(8,128)(2,1)} collective-permute-done((bf16[5,288,512]{2,1,0:T(8,128)(2,1)}, bf16[5,288,512]{2,1,0:T(8,128)(2,1)}, u32[]{:S(2)}, u32[]{:S(2)}) %collective-permute-start.12) | collective-permute-done | bytes 1474592 | tf_op jit(solution)/shard_map/ppermute | solution.py:538
  438.1 6.5 %fusion.21 = (bf16[5,288,512]{2,1,0:T(8,128)(2,1)}, bf16[5,288,512]{2,1,0:T(8,128)(2,1)}) fusion(bf16[5,288,512]{2,1,0:T(8,128)(2,1)} %collective-permute-done.8, bf16[8,5,288,512]{3,2,1,0:T(8,128)(2,1)} %collective-permute-done.7, bf16[8,5,288,512]{3,2,1,0:T(8,128)(2,1)} %get-tuple-element.52, bf16[5,288,512]{2,1,0:T(8,128)(2,1)} %collective-permute-done.12), kind=kLoop, calls=%fused_computation.37 | loop fusion | flops 11796480 | bytes 11796480 | tf_op jit(solution)/shard_map/convert_element_type | solution.py:558
  449.2 10.6 %concatenate.45.refs_2_ = bf16[16,96,1920]{2,1,0:T(8,128)(2,1)} concatenate(bf16[16,96,320]{2,1,0:T(8,128)(2,1)} %convolution_convert_fusion.3, bf16[16,96,1]{2,1,0:T(8,128)(2,1)S(1)} %concatenate.46, bf16[16,96,1]{2,1,0:T(8,128)(2,1)} %concatenate.47, bf16[16,96,40]{2,1,0:T(8,128)(2,1)} %bitcast.186, bf16[16,96,22]{2,1,0:T(8,128)(2,1)} %broadcast_in_dim.40, ...), dimensions={2} | concatenate | bytes 11796480 | tf_op jit(solution)/shard_map/concatenate | solution.py:780
  461.7 103.7 %shard_map.236 = (bf16[8,128,1536]{2,1,0:T(8,128)(2,1)S(1)}, bf16[8,128,1536]{2,1,0:T(8,128)(2,1)S(1)}, f32[96,1920]{1,0:T(8,128)S(1)}) custom-call(bf16[8,128,1536]{2,1,0:T(8,128)(2,1)S(1)} %bitcast.168, bf16[8,128,1536]{2,1,0:T(8,128)(2,1)S(1)} %copy-done, bf16[16,96,1920]{2,1,0:T(8,128)(2,1)} %concatenate.45.refs_2_), custom_call_target="tpu_custom_call" | custom-call | tf_op jit(solution)/shard_map/pallas_call | solution.py:342
  571.9 14.8 %shard_map.237 = f32[8,12,1920]{2,1,0:T(8,128)} custom-call(f32[8,12,1920]{2,1,0:T(8,128)} %reshape.337.refs_0_), custom_call_target="tpu_custom_call" | custom-call | tf_op jit(solution)/shard_map/pallas_call | solution.py:112
  590.7 5.0 fusion.20
  610.3 11.6 %collective-permute-done.10 = bf16[5,288,512]{2,1,0:T(8,128)(2,1)} collective-permute-done((bf16[5,288,512]{2,1,0:T(8,128)(2,1)}, bf16[5,288,512]{2,1,0:T(8,128)(2,1)}, u32[]{:S(2)}, u32[]{:S(2)}) %collective-permute-start.10) | collective-permute-done | bytes 1474592 | tf_op jit(solution)/shard_map/ppermute | solution.py:538
  (246 shorter events, 137.5 us)
Async XLA Ops:
  0.6 26.9 %copy-start.39 = (bf16[5,96,512]{2,1,0:T(8,128)(2,1)S(1)}, bf16[5,96,512]{2,1,0:T(8,128)(2,1)}, u32[]{:S(2)}) copy-start(bf16[5,96,512]{2,1,0:T(8,128)(2,1)} %param.25) | copy-start | bytes 1474564
  0.7 26.9 %copy-start.38 = (bf16[5,96,512]{2,1,0:T(8,128)(2,1)S(1)}, bf16[5,96,512]{2,1,0:T(8,128)(2,1)}, u32[]{:S(2)}) copy-start(bf16[5,96,512]{2,1,0:T(8,128)(2,1)} %param.26) | copy-start | bytes 1474564
  111.7 33.1 %collective-permute-start = (bf16[5,288,512]{2,1,0:T(8,128)(2,1)}, bf16[5,288,512]{2,1,0:T(8,128)(2,1)}, u32[]{:S(2)}, u32[]{:S(2)}) collective-permute-start(bf16[5,288,512]{2,1,0:T(8,128)(2,1)} %pad_maximum_fusion.refs_2_.refs_4_), channel_id=1, source_target_pairs={{0,64},{8,72},{16,80},{24,88},{32,96},{40,104},{48,112},{56,120},{... | collective-permute-start | bytes 4423688 | tf_op jit(solution)/shard_map/ppermute | solution.py:538
  111.8 55.3 %collective-permute-start.2 = (bf16[5,288,512]{2,1,0:T(8,128)(2,1)}, bf16[5,288,512]{2,1,0:T(8,128)(2,1)}, u32[]{:S(2)}, u32[]{:S(2)}) collective-permute-start(bf16[5,288,512]{2,1,0:T(8,128)(2,1)} %pad_maximum_fusion.refs_2_.refs_4_), channel_id=1, source_target_pairs={{0,16},{8,24},{16,32},{24,40},{32,48},{40,56},{48,0},{56,8},{64,80... | collective-permute-start | bytes 4423688 | tf_op jit(solution)/shard_map/ppermute | solution.py:538
  113.4 74.5 %collective-permute-start.1 = (bf16[5,288,512]{2,1,0:T(8,128)(2,1)}, bf16[5,288,512]{2,1,0:T(8,128)(2,1)}, u32[]{:S(2)}, u32[]{:S(2)}) collective-permute-start(bf16[5,288,512]{2,1,0:T(8,128)(2,1)} %pad_maximum_fusion.refs_2_.refs_4_), channel_id=1, source_target_pairs={{0,48},{8,56},{16,0},{24,8},{32,16},{40,24},{48,32},{56,40},{64,11... | collective-permute-start | bytes 4423688 | tf_op jit(solution)/shard_map/ppermute | solution.py:538
  134.7 19.8 %copy-start.46 = (f32[3,1024]{1,0:T(4,128)}, f32[3,1024]{1,0:T(4,128)S(1)}, u32[]{:S(2)}) copy-start(f32[3,1024]{1,0:T(4,128)S(1)} %get-tuple-element.88) | copy-start | bytes 36868
  144.8 33.8 %collective-permute-start.3 = (bf16[5,288,512]{2,1,0:T(8,128)(2,1)}, bf16[5,288,512]{2,1,0:T(8,128)(2,1)S(1)}, u32[]{:S(2)}, u32[]{:S(2)}) collective-permute-start(bf16[5,288,512]{2,1,0:T(8,128)(2,1)} %collective-permute-done.refs_3_.refs_5_), channel_id=1, source_target_pairs={{0,48},{8,56},{16,0},{24,8},{32,16},{40,24},{48,32},{56,40},{64,11... | collective-permute-start | bytes 4423688 | tf_op jit(solution)/shard_map/ppermute | solution.py:538
  154.5 27.7 %copy-start.19 = (bf16[128,1536]{1,0:T(8,128)(2,1)S(1)}, bf16[128,1536]{1,0:T(8,128)(2,1)}, u32[]{:S(2)}) copy-start(bf16[128,1536]{1,0:T(8,128)(2,1)} %refs_2_.1) | copy-start | bytes 1179652
  167.0 18.4 %copy-start.22 = (bf16[128,8,192]{0,2,1:T(8,128)(2,1)}, bf16[128,8,192]{0,2,1:T(8,128)(2,1)S(1)}, u32[]{:S(2)}) copy-start(bf16[128,8,192]{0,2,1:T(8,128)(2,1)S(1)} %copy.73) | copy-start | bytes 1179652
  167.0 36.8 %collective-permute-start.4 = (bf16[5,288,512]{2,1,0:T(8,128)(2,1)}, bf16[5,288,512]{2,1,0:T(8,128)(2,1)}, u32[]{:S(2)}, u32[]{:S(2)}) collective-permute-start(bf16[5,288,512]{2,1,0:T(8,128)(2,1)} %collective-permute-done.refs_3_.refs_5_), channel_id=1, source_target_pairs={{0,16},{8,24},{16,32},{24,40},{32,48},{40,56},{48,0},{56,8},{64,80... | collective-permute-start | bytes 4423688 | tf_op jit(solution)/shard_map/ppermute | solution.py:538
  167.1 64.4 %collective-permute-start.5 = (bf16[5,288,512]{2,1,0:T(8,128)(2,1)}, bf16[5,288,512]{2,1,0:T(8,128)(2,1)}, u32[]{:S(2)}, u32[]{:S(2)}) collective-permute-start(bf16[5,288,512]{2,1,0:T(8,128)(2,1)} %collective-permute-done.2.refs_5_.refs_7_), channel_id=1, source_target_pairs={{0,16},{8,24},{16,32},{24,40},{32,48},{40,56},{48,0},{56,8},{64,80... | collective-permute-start | bytes 4423688 | tf_op jit(solution)/shard_map/ppermute | solution.py:538
  178.6 52.9 %collective-permute-start.6 = (bf16[5,288,512]{2,1,0:T(8,128)(2,1)S(1)}, bf16[5,288,512]{2,1,0:T(8,128)(2,1)}, u32[]{:S(2)}, u32[]{:S(2)}) collective-permute-start(bf16[5,288,512]{2,1,0:T(8,128)(2,1)S(1)} %collective-permute-done.3.refs_6_.refs_8_), channel_id=1, source_target_pairs={{0,48},{8,56},{16,0},{24,8},{32,16},{40,24},{48,32},{56,40},{64,11... | collective-permute-start | bytes 4423688 | tf_op jit(solution)/shard_map/ppermute | solution.py:538
  185.4 169.7 %copy-start.7 = (f32[128,1536]{1,0:T(8,128)}, f32[128,1536]{1,0:T(8,128)S(1)}, u32[]{:S(2)}) copy-start(f32[128,1536]{1,0:T(8,128)S(1)} %get-tuple-element.91) | copy-start | bytes 2359300
  185.6 45.9 %copy-start.17 = (bf16[128,1536]{1,0:T(8,128)(2,1)}, bf16[128,1536]{1,0:T(8,128)(2,1)S(1)}, u32[]{:S(2)}) copy-start(bf16[128,1536]{1,0:T(8,128)(2,1)S(1)} %multiply_convert_fusion.refs_0_) | copy-start | bytes 1179652
  302.8 92.1 %collective-permute-start.7 = (bf16[8,5,288,512]{3,2,1,0:T(8,128)(2,1)}, bf16[8,5,288,512]{3,2,1,0:T(8,128)(2,1)}, u32[]{:S(2)}, u32[]{:S(2)}) collective-permute-start(bf16[8,5,288,512]{3,2,1,0:T(8,128)(2,1)} %get-tuple-element.53), channel_id=1, source_target_pairs={{0,8},{8,0},{16,24},{24,16},{32,40},{40,32},{48,56},{56,48},{64,72... | collective-permute-start | bytes 35389448 | tf_op jit(solution)/shard_map/ppermute | solution.py:538
  401.0 33.7 %collective-permute-start.12 = (bf16[5,288,512]{2,1,0:T(8,128)(2,1)}, bf16[5,288,512]{2,1,0:T(8,128)(2,1)}, u32[]{:S(2)}, u32[]{:S(2)}) collective-permute-start(bf16[5,288,512]{2,1,0:T(8,128)(2,1)} %get-tuple-element.65), channel_id=1, source_target_pairs={{0,48},{8,56},{16,0},{24,8},{32,16},{40,24},{48,32},{56,40},{64,11... | collective-permute-start | bytes 4423688 | tf_op jit(solution)/shard_map/ppermute | solution.py:538
  401.0 37.0 %collective-permute-start.8 = (bf16[5,288,512]{2,1,0:T(8,128)(2,1)}, bf16[5,288,512]{2,1,0:T(8,128)(2,1)}, u32[]{:S(2)}, u32[]{:S(2)}) collective-permute-start(bf16[5,288,512]{2,1,0:T(8,128)(2,1)} %get-tuple-element.64), channel_id=1, source_target_pairs={{0,16},{8,24},{16,32},{24,40},{32,48},{40,56},{48,0},{56,8},{64,80... | collective-permute-start | bytes 4423688 | tf_op jit(solution)/shard_map/ppermute | solution.py:538
  421.3 23.5 %copy-start.13 = (f32[128,1536]{1,0:T(8,128)S(1)}, f32[128,1536]{1,0:T(8,128)}, u32[]{:S(2)}) copy-start(f32[128,1536]{1,0:T(8,128)} %copy-done.12) | copy-start | bytes 2359300
  421.3 23.5 %copy-start.23 = (bf16[128,8,192]{0,2,1:T(8,128)(2,1)S(1)}, bf16[128,8,192]{0,2,1:T(8,128)(2,1)}, u32[]{:S(2)}) copy-start(bf16[128,8,192]{0,2,1:T(8,128)(2,1)} %copy-done.22) | copy-start | bytes 1179652
  421.3 169.4 %collective-permute-start.11 = (bf16[5,288,512]{2,1,0:T(8,128)(2,1)}, bf16[5,288,512]{2,1,0:T(8,128)(2,1)}, u32[]{:S(2)}, u32[]{:S(2)}) collective-permute-start(bf16[5,288,512]{2,1,0:T(8,128)(2,1)} %get-tuple-element.66), channel_id=1, source_target_pairs={{0,16},{8,24},{16,32},{24,40},{32,48},{40,56},{48,0},{56,8},{64,80... | collective-permute-start | bytes 4423688 | tf_op jit(solution)/shard_map/ppermute | solution.py:538
  444.6 146.2 %collective-permute-start.13 = (bf16[5,288,512]{2,1,0:T(8,128)(2,1)}, bf16[5,288,512]{2,1,0:T(8,128)(2,1)}, u32[]{:S(2)}, u32[]{:S(2)}) collective-permute-start(bf16[5,288,512]{2,1,0:T(8,128)(2,1)} %get-tuple-element.63), channel_id=1, source_target_pairs={{0,48},{8,56},{16,0},{24,8},{32,16},{40,24},{48,32},{56,40},{64,11... | collective-permute-start | bytes 4423688 | tf_op jit(solution)/shard_map/ppermute | solution.py:538
  588.6 33.2 %collective-permute-start.10 = (bf16[5,288,512]{2,1,0:T(8,128)(2,1)}, bf16[5,288,512]{2,1,0:T(8,128)(2,1)}, u32[]{:S(2)}, u32[]{:S(2)}) collective-permute-start(bf16[5,288,512]{2,1,0:T(8,128)(2,1)} %get-tuple-element.67), channel_id=1, source_target_pairs={{0,48},{8,56},{16,0},{24,8},{32,16},{40,24},{48,32},{56,40},{64,11... | collective-permute-start | bytes 4423688 | tf_op jit(solution)/shard_map/ppermute | solution.py:538
  590.2 35.0 %collective-permute-start.9 = (bf16[5,288,512]{2,1,0:T(8,128)(2,1)}, bf16[5,288,512]{2,1,0:T(8,128)(2,1)}, u32[]{:S(2)}, u32[]{:S(2)}) collective-permute-start(bf16[5,288,512]{2,1,0:T(8,128)(2,1)} %get-tuple-element.62), channel_id=1, source_target_pairs={{0,16},{8,24},{16,32},{24,40},{32,48},{40,56},{48,0},{56,8},{64,80... | collective-permute-start | bytes 4423688 | tf_op jit(solution)/shard_map/ppermute | solution.py:538
  595.7 33.3 %collective-permute-start.14 = (bf16[5,288,512]{2,1,0:T(8,128)(2,1)}, bf16[5,288,512]{2,1,0:T(8,128)(2,1)}, u32[]{:S(2)}, u32[]{:S(2)}) collective-permute-start(bf16[5,288,512]{2,1,0:T(8,128)(2,1)} %fusion.20), channel_id=1, source_target_pairs={{0,64},{8,72},{16,80},{24,88},{32,96},{40,104},{48,112},{56,120},{... | collective-permute-start | bytes 4423688 | tf_op jit(solution)/shard_map/ppermute | solution.py:538
  (52 other events, 287.2 us)

commit v2 on v1

--- a/solution.py
+++ b/solution.py
@@ -91,7 +91,11 @@
     ]
 
 
-def exchange(arrays, modes, cid):
+def lasting(us):
+    return pl.CostEstimate(flops=us * 1_000_000_000, bytes_accessed=0, transcendentals=0)
+
+
+def exchange(arrays, modes, cid, us=10):
     n = len(arrays)
 
     def kernel(*refs):
@@ -120,16 +124,20 @@
             pltpu.SemaphoreType.DMA((n,)),
         ],
         compiler_params=pltpu.CompilerParams(collective_id=cid, has_side_effects=True),
+        cost_estimate=lasting(us),
     )(*arrays)
 
 
-def gather_start(dense, arrays, modes, cid):
-    m, n = len(dense), len(arrays)
+def gather_start(slices, output, arrays, modes, cid):
+    n = len(arrays)
+    small = (slices, output)
+    widths = (slices.shape[-1], output.shape[-1])
 
     def kernel(*refs):
-        dins, ins = refs[:m], refs[m : m + n]
-        douts, outs = refs[m + n : 2 * m + n], refs[2 * m + n : 2 * (m + n)]
-        dsend, drecv, dlocal, send, recv, local = refs[2 * (m + n) :]
+        sins, ins = refs[:2], refs[2 : 2 + n]
+        douts, outs = refs[2 + n : 4 + n], refs[4 + n : 4 + 2 * n]
+        pieces, rows = refs[4 + 2 * n : 6 + 2 * n], refs[6 + 2 * n : 8 + 2 * n]
+        ssend, srecv, slocal, dsend, drecv, dlocal, send, recv, local = refs[8 + 2 * n :]
         x, y, core = dp_place()
         mine = dp_index(x, y, core)
         to_x, to_up, to_down, to_core = (
@@ -161,19 +169,30 @@
             started.append(c)
 
         sibling = [dp_index(x + rx, y + ry, core) for rx, ry in SLOTS]
-        locals_ = []
-        for i in range(m):
-            c = pltpu.make_async_copy(dins[i], douts[i].at[mine], dlocal.at[i])
-            c.start()
-            locals_.append(c)
-            go(move(i, 0, mine, to_x, dins[i]))
-            go(move(i, 1, mine, to_up, dins[i]))
-            go(move(i, 2, mine, to_down, dins[i]))
-            go(move(i, 7, mine, to_core, dins[i]))
+        first = []
+        for i, mode in enumerate(("exchange", "gather")):
+            part = expert_copies(
+                [sins[i]], [pieces[i]], [mode], ssend.at[pl.ds(i, 1)], srecv.at[pl.ds(i, 1)]
+            ) + own_copies([sins[i]], [pieces[i]], [mode], slocal.at[pl.ds(i, 1)])
+            for c in part:
+                c.start()
+            first.append(part)
         more = expert_copies(ins, outs, modes, send, recv) + own_copies(ins, outs, modes, local)
         for c in more:
             c.start()
-        for i in range(m):
+        locals_ = []
+        for i in range(2):
+            for c in first[i]:
+                c.wait()
+            rows[i][...] = jnp.concatenate([pieces[i][j] for j in range(PEERS)], axis=0)
+            c = pltpu.make_async_copy(rows[i], douts[i].at[mine], dlocal.at[i])
+            c.start()
+            locals_.append(c)
+            go(move(i, 0, mine, to_x, rows[i]))
+            go(move(i, 1, mine, to_up, rows[i]))
+            go(move(i, 2, mine, to_down, rows[i]))
+            go(move(i, 7, mine, to_core, rows[i]))
+        for i in range(2):
             arrived(i, 0, sibling[1])
             go(move(i, 3, sibling[1], to_up))
             go(move(i, 4, sibling[1], to_down))
@@ -183,18 +202,18 @@
             go(move(i, 10, sibling[3], to_core))
             arrived(i, 2, sibling[2])
             go(move(i, 9, sibling[2], to_core))
-        for i in range(m):
+        for i in range(2):
             arrived(i, 4, sibling[4])
             go(move(i, 6, sibling[4], to_down))
             go(move(i, 11, sibling[4], to_core))
             arrived(i, 3, sibling[5])
             go(move(i, 12, sibling[5], to_core))
-        for i in range(m):
+        for i in range(2):
             arrived(i, 5, sibling[6])
             go(move(i, 13, sibling[6], to_core))
             arrived(i, 6, sibling[7])
             go(move(i, 14, sibling[7], to_core))
-        for i in range(m):
+        for i in range(2):
             for k in range(8):
                 rx, ry = SLOTS[k]
                 arrived(i, 7 + k, dp_index(x + rx, y + ry, core + 1))
@@ -203,25 +222,31 @@
         for c in more + locals_:
             c.wait()
 
-    shapes = [jax.ShapeDtypeStruct((DP,) + a.shape, a.dtype) for a in dense] + [
+    shapes = [jax.ShapeDtypeStruct((DP, ROWS, w), BF) for w in widths] + [
         jax.ShapeDtypeStruct(((PEERS,) + a.shape) if k == "gather" else a.shape, a.dtype)
         for a, k in zip(arrays, modes)
     ]
     return pl.pallas_call(
         kernel,
         out_shape=shapes,
-        in_specs=any_specs(m + n),
-        out_specs=any_specs(m + n),
-        scratch_shapes=[
-            pltpu.SemaphoreType.DMA((m, 15)),
-            pltpu.SemaphoreType.DMA((m, 15)),
-            pltpu.SemaphoreType.DMA((m,)),
+        in_specs=any_specs(2 + n),
+        out_specs=any_specs(2 + n),
+        scratch_shapes=[pltpu.VMEM((PEERS, 12, w), BF) for w in widths]
+        + [pltpu.VMEM((ROWS, w), BF) for w in widths]
+        + [
+            pltpu.SemaphoreType.DMA((2, 7)),
+            pltpu.SemaphoreType.DMA((2, 7)),
+            pltpu.SemaphoreType.DMA((2,)),
+            pltpu.SemaphoreType.DMA((2, 15)),
+            pltpu.SemaphoreType.DMA((2, 15)),
+            pltpu.SemaphoreType.DMA((2,)),
             pltpu.SemaphoreType.DMA((n, 7)),
             pltpu.SemaphoreType.DMA((n, 7)),
             pltpu.SemaphoreType.DMA((n,)),
         ],
         compiler_params=pltpu.CompilerParams(collective_id=cid, has_side_effects=True),
-    )(*dense, *arrays)
+        cost_estimate=lasting(45),
+    )(*small, *arrays)
 
 
 def exchange_and_share(arrays, modes, pieces, cid):
@@ -269,99 +294,122 @@
             pltpu.SemaphoreType.DMA((m,)),
         ],
         compiler_params=pltpu.CompilerParams(collective_id=cid, has_side_effects=True),
+        cost_estimate=lasting(38),
     )(*arrays, *pieces)
 
 
 def scatter_sum(arrays, dense, cid):
-    n = len(arrays)
-    _, rows, cols = dense.shape
+    n, m = len(arrays), len(dense)
+    shapes = [(d.shape[1], d.shape[2]) for d in dense]
 
     def kernel(*refs):
-        ins, dref = refs[:n], refs[n]
-        outs, total = refs[n + 1 : 2 * n + 1], refs[2 * n + 1]
-        send, recv, local, mine, theirs, summed, got, lsem, csend, crecv, dsend, drecv = refs[
-            2 * n + 2 :
-        ]
+        ins, dins = refs[:n], refs[n : n + m]
+        outs, totals = refs[n + m : 2 * n + m], refs[2 * n + m : 2 * (n + m)]
+        refs = refs[2 * (n + m) :]
+        mine, theirs, along, last = refs[:m], refs[m : 2 * m], refs[2 * m : 3 * m], refs[3 * m : 4 * m]
+        send, recv, local, lsem, csend, crecv, ysend, yrecv, xsend, xrecv = refs[4 * m :]
         x, y, core = dp_place()
-        to_core = dp_index(x, y, core + 1)
-        targets = [dp_index(x + rx, y + ry, core) for rx, ry in SLOTS[1:]]
+        to_core, to_x = dp_index(x, y, core + 1), dp_index(x + 1, y, core)
+        to_y = [dp_index(x, y + r, core) for r in (1, 2, 3)]
         _, peers = expert_peers()
-        signal_all(peers, [to_core] + targets)
+        signal_all(peers, [to_core, to_x] + to_y)
         modes = ["exchange"] * n
-        loads, shares = [], []
-        for k, (rx, ry) in enumerate(SLOTS):
+        order = [(r, s) for r in (1, 0) for s in (2, 1, 3, 0)]
+        started, loads, shares = [], {}, {}
+
+        def remote(src, dst, s, r, target):
             c = pltpu.make_async_remote_copy(
-                src_ref=dref.at[dp_index(x + rx, y + ry, core + 1)],
-                dst_ref=theirs.at[k],
-                send_sem=csend.at[k],
-                recv_sem=crecv.at[k],
-                device_id={"dp": to_core},
+                src_ref=src,
+                dst_ref=dst,
+                send_sem=s,
+                recv_sem=r,
+                device_id={"dp": target},
                 device_id_type=MESH,
             )
             c.start()
-            shares.append(c)
-            c = pltpu.make_async_copy(
-                dref.at[dp_index(x + rx, y + ry, core)], mine.at[k], lsem.at[k]
-            )
-            c.start()
-            loads.append(c)
+            started.append(c)
+            return c
+
+        for i in range(m):
+            for r, s in order:
+                k = 4 * r + s
+                shares[i, k] = remote(
+                    dins[i].at[dp_index(x + r, y + s, core + 1)],
+                    theirs[i].at[k],
+                    csend.at[i, k],
+                    crecv.at[i, k],
+                    to_core,
+                )
+                loads[i, k] = pltpu.make_async_copy(
+                    dins[i].at[dp_index(x + r, y + s, core)], mine[i].at[k], lsem.at[i, k]
+                )
+                loads[i, k].start()
         copies = expert_copies(ins, outs, modes, send, recv) + own_copies(ins, outs, modes, local)
         for c in copies:
             c.start()
-        moves = []
-        for k in range(8):
-            loads[k].wait()
-            shares[k].wait_recv()
-            summed[k] = (mine[k].astype(F32) + theirs[k].astype(F32)).astype(BF)
-            if k > 0:
-                c = pltpu.make_async_remote_copy(
-                    src_ref=summed.at[k],
-                    dst_ref=got.at[k - 1],
-                    send_sem=dsend.at[k - 1],
-                    recv_sem=drecv.at[k - 1],
-                    device_id={"dp": targets[k - 1]},
-                    device_id_type=MESH,
-                )
-                c.start()
-                moves.append(c)
-        acc = summed[0].astype(F32)
-        for k, c in enumerate(moves):
-            c.wait_recv()
-            acc = acc + got[k].astype(F32)
-        total[...] = acc
-        for c in moves:
-            c.wait_send()
-        for c in shares:
+        moves = {}
+        for r, s in order:
+            k = 4 * r + s
+            for i in range(m):
+                loads[i, k].wait()
+                shares[i, k].wait_recv()
+                mine[i][k] = (mine[i][k].astype(F32) + theirs[i][k].astype(F32)).astype(BF)
+                if s > 0:
+                    moves[i, r, s] = remote(
+                        mine[i].at[k],
+                        along[i].at[3 * r + s - 1],
+                        ysend.at[i, 3 * r + s - 1],
+                        yrecv.at[i, 3 * r + s - 1],
+                        to_y[s - 1],
+                    )
+        crossings = []
+        for i in range(m):
+            acc = mine[i][4].astype(F32)
+            for s in (2, 1, 3):
+                moves[i, 1, s].wait_recv()
+                acc = acc + along[i][3 + s - 1].astype(F32)
+            mine[i][4] = acc.astype(BF)
+            crossings.append(remote(mine[i].at[4], last[i], xsend.at[i], xrecv.at[i], to_x))
+        for i in range(m):
+            acc = mine[i][0].astype(F32)
+            for s in (2, 1, 3):
+                moves[i, 0, s].wait_recv()
+                acc = acc + along[i][s - 1].astype(F32)
+            crossings[i].wait_recv()
+            totals[i][...] = acc + last[i][...].astype(F32)
+        for c in started:
             c.wait_send()
         for c in copies:
             c.wait()
 
-    shapes = [jax.ShapeDtypeStruct(a.shape, a.dtype) for a in arrays] + [
-        jax.ShapeDtypeStruct((rows, cols), F32)
-    ]
+    vmem = pl.BlockSpec(memory_space=pltpu.VMEM)
     return pl.pallas_call(
         kernel,
-        out_shape=shapes,
-        in_specs=any_specs(n + 1),
-        out_specs=any_specs(n) + [pl.BlockSpec(memory_space=pltpu.VMEM)],
-        scratch_shapes=[
+        out_shape=[jax.ShapeDtypeStruct(a.shape, a.dtype) for a in arrays]
+        + [jax.ShapeDtypeStruct(d, F32) for d in shapes],
+        in_specs=any_specs(n + m),
+        out_specs=any_specs(n) + [vmem] * m,
+        scratch_shapes=[pltpu.VMEM((8,) + d, BF) for d in shapes]
+        + [pltpu.VMEM((8,) + d, BF) for d in shapes]
+        + [pltpu.VMEM((6,) + d, BF) for d in shapes]
+        + [pltpu.VMEM(d, BF) for d in shapes]
+        + [
             pltpu.SemaphoreType.DMA((n, 7)),
             pltpu.SemaphoreType.DMA((n, 7)),
             pltpu.SemaphoreType.DMA((n,)),
-            pltpu.VMEM((8, rows, cols), BF),
-            pltpu.VMEM((8, rows, cols), BF),
-            pltpu.VMEM((8, rows, cols), BF),
-            pltpu.VMEM((7, rows, cols), BF),
-            pltpu.SemaphoreType.DMA((8,)),
-            pltpu.SemaphoreType.DMA((8,)),
-            pltpu.SemaphoreType.DMA((8,)),
-            pltpu.SemaphoreType.DMA((7,)),
-            pltpu.SemaphoreType.DMA((7,)),
+            pltpu.SemaphoreType.DMA((m, 8)),
+            pltpu.SemaphoreType.DMA((m, 8)),
+            pltpu.SemaphoreType.DMA((m, 8)),
+            pltpu.SemaphoreType.DMA((m, 6)),
+            pltpu.SemaphoreType.DMA((m, 6)),
+            pltpu.SemaphoreType.DMA((m,)),
+            pltpu.SemaphoreType.DMA((m,)),
         ],
         compiler_params=pltpu.CompilerParams(
             collective_id=cid, has_side_effects=True, vmem_limit_bytes=40 << 20
         ),
-    )(*arrays, dense)
+        cost_estimate=lasting(45),
+    )(*arrays, *dense)
 
 
 def dot(a, b, contract):
@@ -370,16 +418,18 @@
 
 def experts_kernel(*refs):
     (rows_ref, cot_ref, slot_ref, gate_ref), refs = refs[:4], refs[4:]
-    pieces, shared, refs = refs[:8], refs[8], refs[9:]
-    (out_ref, back_ref, inner_ref, keep_ref, give_ref), refs = refs[:5], refs[5:]
-    xg, cg, weights, grads, gates, inners, wsem, gsem = refs
+    pieces, shared, late, refs = refs[:8], refs[8], refs[9:11], refs[11:]
+    (out_ref, back_ref, inner_ref, keep_ref, given_ref), refs = refs[:5], refs[5:]
+    xg, cg, weights, grads, gates, inners, wsem, gsem, rsem = refs
     x, y, core = dp_place()
+    other = dp_index(x, y, core + 1)
+    signal_all([], [other])
 
     def loads(e, b):
         copies = []
         for k, (rx, ry) in enumerate(SLOTS):
             for c in range(2):
-                src = pieces[k].at[e] if c == 0 else shared.at[k, e]
+                src = pieces[k].at[e] if c == 0 else shared.at[k, e] if k < 6 else late[k - 6].at[e]
                 copies.append(
                     pltpu.make_async_copy(
                         src,
@@ -389,19 +439,32 @@
                 )
         return copies
 
-    def stores(e, b):
-        copies = []
-        for k, (rx, ry) in enumerate(SLOTS):
-            for c in range(2):
-                dst = keep_ref.at[k, e] if c == 0 else give_ref.at[k, e]
-                copies.append(
-                    pltpu.make_async_copy(
-                        grads.at[b, dp_index(x + rx, y + ry, core + c)],
-                        dst,
-                        gsem.at[b, 2 * k + c],
-                    )
-                )
-        return copies
+    def kept(e, b):
+        return [
+            pltpu.make_async_copy(
+                grads.at[b, dp_index(x + rx, y + ry, core)], keep_ref.at[k, e], gsem.at[b, k]
+            )
+            for k, (rx, ry) in enumerate(SLOTS)
+        ]
+
+    def given(e, b):
+        return [
+            pltpu.make_async_remote_copy(
+                src_ref=grads.at[b, dp_index(x + rx, y + ry, core + 1)],
+                dst_ref=given_ref.at[k, e],
+                send_sem=gsem.at[b, 8 + k],
+                recv_sem=rsem.at[e, k],
+                device_id={"dp": other},
+                device_id_type=MESH,
+            )
+            for k, (rx, ry) in enumerate(SLOTS)
+        ]
+
+    def stored(e, b):
+        for c in kept(e, b):
+            c.wait()
+        for c in given(e, b):
+            c.wait_send()
 
     for c in loads(0, 0):
         c.start()
@@ -434,8 +497,7 @@
 
         @pl.when(e >= 2)
         def _free():
-            for c in stores(e - 2, b):
-                c.wait()
+            stored(e - 2, b)
 
         span = pl.ds(pl.multiple_of(e * CAP, CAP), CAP)
         rows = xg[:, span, :].reshape(PEERS * CAP, DIM)
@@ -471,7 +533,7 @@
         grads[b, :, 96:192, :] = (
             dot(rows, grad_up, ((0,), (0,))).astype(BF).reshape(DP, ROWS, FFE)
         )
-        for c in stores(e, b):
+        for c in kept(e, b) + given(e, b):
             c.start()
         back = dot(grad_gate, w_gate, ((1,), (1,))) + dot(grad_up, w_up, ((1,), (1,)))
         xg[:, span, :] = back.astype(BF).reshape(PEERS, CAP, DIM)
@@ -495,11 +557,13 @@
 
     lax.fori_loop(0, PEERS, combine, 0)
     for e in (LOCAL - 2, LOCAL - 1):
-        for c in stores(e, e % 2):
-            c.wait()
-
-
-def run_experts(rows, cot, slots, gates, pieces, shared):
+        stored(e, e % 2)
+    for e in range(LOCAL):
+        for c in given(e, e % 2):
+            c.wait_recv()
+
+
+def run_experts(rows, cot, slots, gates, pieces, shared, late):
     vmem = pl.BlockSpec(memory_space=pltpu.VMEM)
     piece = (LOCAL, 3 * ROWS, FFE)
     return pl.pallas_call(
@@ -511,7 +575,7 @@
             jax.ShapeDtypeStruct((8,) + piece, BF),
             jax.ShapeDtypeStruct((8,) + piece, BF),
         ],
-        in_specs=[vmem] * 4 + any_specs(9),
+        in_specs=[vmem] * 4 + any_specs(11),
         out_specs=[vmem] * 3 + any_specs(2),
         scratch_shapes=[
             pltpu.VMEM((PEERS, LOCAL * CAP, DIM), BF),
@@ -522,12 +586,15 @@
             pltpu.VMEM((LOCAL, PEERS * CAP, 128), F32),
             pltpu.SemaphoreType.DMA((2, 16)),
             pltpu.SemaphoreType.DMA((2, 16)),
+            pltpu.SemaphoreType.DMA((LOCAL, 8)),
         ],
-        compiler_params=pltpu.CompilerParams(vmem_limit_bytes=60 << 20),
+        compiler_params=pltpu.CompilerParams(
+            collective_id=2, has_side_effects=True, vmem_limit_bytes=60 << 20
+        ),
         cost_estimate=pl.CostEstimate(
             flops=20_000_000_000, bytes_accessed=60_000_000, transcendentals=700_000
         ),
-    )(rows, cot, slots, gates, *pieces, shared)
+    )(rows, cot, slots, gates, *pieces, shared, *late)
 
 
 def shift(value, move):
@@ -552,6 +619,10 @@
 
 def other_core(value):
     return shift(value, lambda x, y, c: (x, y, c + 1))
+
+
+def to_peers(blocks):
+    return lax.all_to_all(blocks, "expert", split_axis=0, concat_axis=0, tiled=True)
 
 
 def add(a, b):
@@ -641,10 +712,6 @@
         ],
         axis=2,
     )
-    slices_rows, output_rows = exchange([slices, w_output], ["exchange", "gather"], 1)
-    slices_rows = slices_rows.reshape(ROWS, SLICE)
-    output_rows = output_rows.reshape(ROWS, DIM)
-
     member = jnp.any(
         expert_ids[None, :, :] == jnp.arange(EXPERTS, dtype=jnp.int32)[:, None, None], axis=-1
     )
@@ -652,13 +719,11 @@
     places = jnp.dot(member.astype(BF), before.astype(BF), preferred_element_type=F32)
     slot_table = by_peer(jnp.where(member, places, -1.0))
 
-    slices_all, output_all, tokens_all, cot_all, slots_all = gather_start(
-        [slices_rows, output_rows],
-        [tokens, cotangent, slot_table],
-        ["gather", "gather", "exchange"],
-        2,
-    )
-    piece, _ = lax.optimization_barrier((piece, slots_all))
+    slices_all, output_all, tokens_all, slots_all = gather_start(
+        slices, w_output, [tokens, slot_table], ["gather", "exchange"], 1
+    )
+    piece, cot, _ = lax.optimization_barrier((piece, cotangent, slots_all))
+    cot_all = to_peers(jnp.broadcast_to(cot[None], (PEERS, TOK, DIM)))
     x1 = across(piece)
     y3, y1 = up(piece), down(piece)
     x1y3, x1y1 = up(x1), down(x1)
@@ -707,28 +772,29 @@
     weight = jnp.where(member, jnp.exp(chosen - jnp.max(chosen, axis=0, keepdims=True)), 0.0)
     gate_values = weight / jnp.sum(weight, axis=0, keepdims=True)
 
+    late = [other_core(y2), other_core(x1y2)]
     rows_all, gates_all, shared = exchange_and_share(
-        [normed_two, by_peer(gate_values)], ["gather", "exchange"], pieces, 4
-    )
-    out_part, back_part, inner_part, keep, give = run_experts(
-        rows_all, cot_all, slots_all, gates_all, pieces, shared
-    )
-
-    given = other_core(give)
+        [normed_two, by_peer(gate_values)], ["gather", "exchange"], pieces[:6], 4
+    )
+    out_part, back_part, inner_part, keep, given = run_experts(
+        rows_all, cot_all, slots_all, gates_all, pieces, shared, late
+    )
+    back_all, inner_all = exchange([back_part, inner_part], ["exchange", "exchange"], 5, 38)
+
     sums = {s: add(keep[k], given[k]) for k, s in enumerate(SLOTS)}
-    sums[(0, 1)] = add(sums[(0, 1)], up(sums[(0, 2)]))
-    sums[(1, 3)] = add(sums[(1, 3)], down(sums[(1, 2)]))
-    halves = [
-        (
-            sums[(r, 0)].astype(F32)
-            + up(sums[(r, 1)]).astype(F32)
-            + down(sums[(r, 3)]).astype(F32)
-        )
-        for r in (0, 1)
-    ]
-    expert_grads = halves[0] + across(halves[1].astype(BF)).astype(F32)
-
-    back_all, inner_all = exchange([back_part, inner_part], ["exchange", "exchange"], 5)
+    up_two, down_two = up(sums[(0, 2)]), down(sums[(1, 2)])
+    far = (
+        sums[(1, 0)].astype(F32)
+        + up(sums[(1, 1)]).astype(F32)
+        + down(add(sums[(1, 3)], down_two)).astype(F32)
+    ).astype(BF)
+    near = (
+        sums[(0, 0)].astype(F32)
+        + up(add(sums[(0, 1)], up_two)).astype(F32)
+        + down(sums[(0, 3)]).astype(F32)
+    )
+    expert_grads = near + across(far).astype(F32)
+
     grad_normed_two = jnp.sum(back_all.astype(F32), axis=0)
     grad_gates = inner_all[:, :LOCAL, :].reshape(EXPERTS, TOK)
     grad_chosen = gate_values * (
@@ -750,6 +816,8 @@
     ).astype(BF)
     grad_attended = grad_attended.reshape(TOK, PEERS, QS).transpose(1, 0, 2)
     (grad_attended,) = exchange([grad_attended], ["exchange"], 6)
+    out_part, _ = lax.optimization_barrier((out_part, grad_attended))
+    out_all = to_peers(out_part)
     grad_attended = grad_attended.reshape(GROUP, REP, HEAD)
     grad_output = lax.dot_general(
         attended, grad_branch, (((0,), (0,)), ((), ())), preferred_element_type=F32
@@ -777,36 +845,39 @@
         grad_qkv, qkv_all, (((1,), (1,)), ((), ())), preferred_element_type=F32
     )
     grad_gain_one = jnp.sum(grad_normed * inputs_all * scale_all, axis=0)
-    dense = jnp.concatenate(
+    small = jnp.concatenate(
         [
-            grad_slices,
-            grad_gain_one[:, None],
-            grad_gain_two[:, None],
-            grad_router,
-            jnp.zeros((DIM, SLICE - QS - 2 * HEAD - 2 - EXPERTS), F32),
-            grad_output,
+            grad_slices.astype(BF),
+            grad_gain_one[:, None].astype(BF),
+            grad_gain_two[:, None].astype(BF),
+            grad_router.astype(BF),
+            jnp.zeros((DIM, SLICE - QS - 2 * HEAD - 2 - EXPERTS), BF),
         ],
         axis=1,
-    ).astype(BF)
-    normed_back, out_all, dense_rows = scatter_sum(
-        [grad_normed.astype(BF).reshape(PEERS, TOK, DIM), out_part],
-        dense.reshape(DP, ROWS, SLICE + DIM),
+    )
+    normed_back, small_rows, output_rows = scatter_sum(
+        [grad_normed.astype(BF).reshape(PEERS, TOK, DIM)],
+        [small.reshape(DP, ROWS, SLICE), grad_output.astype(BF).reshape(DP, ROWS, DIM)],
         7,
     )
     mixed = middle + jnp.sum(out_all.astype(F32), axis=0)
     grad_tokens = grad_middle + norm_back(
         inputs, scale_all_own(scale_all), gain_one, jnp.sum(normed_back.astype(F32), axis=0)
     )
-    (dense_own,) = exchange([dense_rows.reshape(PEERS, 12, SLICE + DIM)], ["exchange"], 8)
-    own_sum = jnp.sum(dense_own[:, :, QS + 2 * HEAD :], axis=0)
+    small_own, output_own = exchange(
+        [small_rows.reshape(PEERS, 12, SLICE), output_rows.reshape(PEERS, 12, DIM)],
+        ["exchange", "exchange"],
+        8,
+    )
+    own_sum = jnp.sum(small_own[:, :, QS + 2 * HEAD :], axis=0)
     last = QS + 2 * HEAD
     return (
         mixed.astype(BF),
         grad_tokens,
-        dense_own[:, :, :QS].transpose(1, 0, 2).reshape(12, DIM),
-        dense_own[:, :, QS : QS + HEAD].transpose(1, 0, 2).reshape(12, KV_HEADS * HEAD),
-        dense_own[:, :, QS + HEAD : last].transpose(1, 0, 2).reshape(12, KV_HEADS * HEAD),
-        own_sum[:, SLICE - last :],
+        small_own[:, :, :QS].transpose(1, 0, 2).reshape(12, DIM),
+        small_own[:, :, QS : QS + HEAD].transpose(1, 0, 2).reshape(12, KV_HEADS * HEAD),
+        small_own[:, :, QS + HEAD : last].transpose(1, 0, 2).reshape(12, KV_HEADS * HEAD),
+        jnp.sum(output_own, axis=0),
         own_sum[:, 0],
         own_sum[:, 1],
         own_sum[:, 2 : 2 + EXPERTS],

time: 647 us -> 599 us (0.926)
  Pallas kernels: 349 us -> 312 us
  local copies, waits for them, and re-layouts: 67.1 us -> 41.3 us
  starting transfers between devices: 16.8 us -> 41.4 us
  waiting for transfers between devices: 99.9 us -> 92 us
  matrix products: 53.6 us -> 46.4 us
    pallas_call x2, Pallas kernels: 187 us -> 151 us  [the longest x1 76.5 us: scatter_sum(): pl.pallas_call(kernel, out_shape=[jax.ShapeDtypeStruct(a.shape, a.dtype)...]
    ppermute x15 -> x16, starting transfers between devices: 16.8 us -> 31.6 us  [shift(): return lax.ppermute(value, 'dp', pairs)]
    concatenate x3 -> x1, local copies, waits for them, and re-layouts: 13.4 us -> 2.9 us  [local(): jnp.concatenate([grad_slices.astype(BF), grad_gain_one[:, None].astype(BF...]
    all_to_all x0 -> x2, starting transfers between devices: none -> 9.79 us  [to_peers(): lax.all_to_all(blocks, 'expert', split_axis=0, concat_axis=0, tiled=True)]
    ppermute x15 -> x16, waiting for transfers between devices: 99.9 us -> 92 us  [shift(): return lax.ppermute(value, 'dp', pairs)]
    pallas_call x5 -> x4, Pallas kernels: 90.8 us -> 86.3 us  [exchange(): pl.pallas_call(kernel, out_shape=shapes, in_specs=any_specs(n), out_specs...]
  transfers between devices with their start and end apart: 15 -> 18, of which waited for: 9 -> 6; matrix products, arithmetic and copies ran while one was open for 21% -> 12% of each run, Pallas kernels for 28% -> 26%
where the time goes in v2:
time: 599 us; the launch traced here: 589 us
  Pallas kernels  312 us (52%)
  waiting for transfers between devices  92 us (15%)
  other arithmetic  53.8 us (9%)
  matrix products  46.4 us (8%)
  starting transfers between devices  41.4 us (7%)
  local copies, waits for them, and re-layouts  41.3 us (7%)
    ppermute x16, waiting for transfers between devices, shift(): return lax.ppermute(value, 'dp', pairs)  92 us
    pallas_call x4, Pallas kernels, exchange(): pl.pallas_call(kernel, out_shape=shapes, in_specs=any_specs(n), out_specs...  86.3 us
    pallas_call x1, Pallas kernels, scatter_sum(): pl.pallas_call(kernel, out_shape=[jax.ShapeDtypeStruct(a.shape, a.dtype)...  76.5 us
    pallas_call x1, Pallas kernels, gather_start(): pl.pallas_call(kernel, out_shape=shapes, in_specs=any_specs(2 + n), out_s...  74 us
    pallas_call x1, Pallas kernels, exchange_and_share(): pl.pallas_call(kernel, out_shape=shapes, in_specs=any_specs(n + m), out_s...  40.3 us
    pallas_call x1, Pallas kernels, run_experts(): pl.pallas_call(experts_kernel, out_shape=[jax.ShapeDtypeStruct((PEERS, TO...  34.8 us
    ppermute x16, starting transfers between devices, shift(): return lax.ppermute(value, 'dp', pairs)  31.6 us
  transfers between devices with their start and end apart: 18, of which 6 were waited for; matrix products, arithmetic and copies ran while one was open for 12% of the time, Pallas kernels for 26%

profile of v2, /device:TPU:0, one launch (start us, length us, event | category | flops | bytes accessed | tf_op | source)
XLA Modules:
  0.0 588.7 jit_solution(11458654555675506356)
XLA Ops:
  10.5 74.0 %shard_map.229 = (bf16[16,96,384]{2,1,0:T(8,128)(2,1)}, bf16[16,96,1536]{2,1,0:T(8,128)(2,1)}, bf16[8,128,1536]{2,1,0:T(8,128)(2,1)}, f32[8,8,128]{2,1,0:T(8,128)}) custom-call(bf16[8,12,384]{2,1,0:T(8,128)(2,1)} %pad_maximum_fusion.7.refs_0_, bf16[12,1536]{1,0:T(8,128)(2,1)} %refs_1_.1, bf16[128,1536]{1,0:T(8,128)(2,1)} %refs_2_.1, f32[8,8,128]{2,1,0:T(8,128)} %pad.7.refs_3_), custom_call_target="tpu_custom_call" | custom-call | flops 44999999488 | tf_op jit(solution)/shard_map/pallas_call | solution.py:229
  91.3 4.6 all-to-all-start
  107.7 7.3 %fusion.77 = (f32[3,1024]{1,0:T(4,128)S(1)}, f32[3,1024,1024]{1,2,0:T(8,128)}) fusion(pred[1024,1024]{0,1:T(8,128)(4,1)S(1)} %fusion.13, bf16[1024,64,1]{0,1,2:T(8,128)(2,1)S(1)} %maximum_bitcast_fusion, bf16[1024,4,32]{0,2,1:T(8,128)(2,1)S(1)} %get-tuple-element.78, bf16[1024,4,32]{0,2,1:T(8,128)(2,1)S(1)} %get-tuple-element.77), kind=kOutput, calls=%fused_computation.159 | convolution fusion | flops 416023552 | bytes 14299136 | tf_op jit(solution)/shard_map/sub | solution.py:757
  115.0 5.0 collective-permute-done.refs_3_.refs_5_
  120.0 13.1 %collective-permute-start.3 = (bf16[5,288,512]{2,1,0:T(8,128)(2,1)}, bf16[5,288,512]{2,1,0:T(8,128)(2,1)}, u32[]{:S(2)}, u32[]{:S(2)}) collective-permute-start(bf16[5,288,512]{2,1,0:T(8,128)(2,1)} %collective-permute-done.refs_3_.refs_5_), channel_id=1, source_target_pairs={{0,48},{8,56},{16,0},{24,8},{32,16},{40,24},{48,32},{56,40},{64,11... | collective-permute-start | bytes 4423688 | tf_op jit(solution)/shard_map/ppermute | solution.py:605
  133.1 5.9 fusion.35
  140.2 20.0 %shard_map.230 = bf16[8,128,192]{2,1,0:T(8,128)(2,1)} custom-call(bf16[8,128,192]{2,1,0:T(8,128)(2,1)} %copy.72.refs_0_), custom_call_target="tpu_custom_call" | custom-call | flops 10000000000 | tf_op jit(solution)/shard_map/pallas_call | solution.py:116
  173.6 54.9 %collective-permute-done.5.refs_10_ = bf16[5,288,512]{2,1,0:T(8,128)(2,1)} collective-permute-done((bf16[5,288,512]{2,1,0:T(8,128)(2,1)}, bf16[5,288,512]{2,1,0:T(8,128)(2,1)}, u32[]{:S(2)}, u32[]{:S(2)}) %collective-permute-start.5) | collective-permute-done | bytes 1474592 | tf_op jit(solution)/shard_map/ppermute | solution.py:605
  229.0 40.3 %shard_map.231 = (bf16[8,128,1536]{2,1,0:T(8,128)(2,1)}, f32[8,8,128]{2,1,0:T(8,128)}, bf16[6,5,288,512]{3,2,1,0:T(8,128)(2,1)}) custom-call(bf16[128,1536]{1,0:T(8,128)(2,1)} %copy-done.5, f32[8,8,128]{2,1,0:T(8,128)} %pad.8.refs_1_, bf16[5,288,512]{2,1,0:T(8,128)(2,1)} %pad_maximum_fusion.refs_2_.refs_4_, ...), custom_call_target="tpu_custom_call" | custom-call | flops 38000001024 | tf_op jit(solution)/shard_map/pallas_call | solution.py:284
  269.4 34.8 %shard_map.232 = (bf16[8,128,1536]{2,1,0:T(8,128)(2,1)}, bf16[8,128,1536]{2,1,0:T(8,128)(2,1)}, f32[8,8,128]{2,1,0:T(8,128)}, bf16[8,5,288,512]{3,2,1,0:T(8,128)(2,1)}, bf16[8,5,288,512]{3,2,1,0:T(8,128)(2,1)}) custom-call(bf16[8,128,1536]{2,1,0:T(8,128)(2,1)} %get-tuple-element.39.refs_0_, bf16[8,128,1536]{2,1,0:T(8,128)(2,1)} %all-to-all-done.refs_1_, ...), custom_call_target="tpu_custom_call" | custom-call | flops 20000000000 | bytes 60000000 | tf_op jit(solution)/shard_map/pallas_call | solution.py:569
  304.2 40.7 %shard_map.233 = (bf16[8,128,1536]{2,1,0:T(8,128)(2,1)}, f32[8,8,128]{2,1,0:T(8,128)}) custom-call(bf16[8,128,1536]{2,1,0:T(8,128)(2,1)} %get-tuple-element.44.refs_0_, f32[8,8,128]{2,1,0:T(8,128)} %get-tuple-element.45.refs_1_), custom_call_target="tpu_custom_call" | custom-call | flops 38000001024 | tf_op jit(solution)/shard_map/pallas_call | solution.py:116
  356.3 11.2 %shard_map.234 = bf16[8,128,192]{2,1,0:T(8,128)(2,1)} custom-call(bf16[8,128,192]{2,1,0:T(8,128)(2,1)} %bitcast.185), custom_call_target="tpu_custom_call" | custom-call | flops 10000000000 | tf_op jit(solution)/shard_map/pallas_call | solution.py:116
  369.0 10.1 %fusion.1 = (f32[3,1024]{1,0:T(4,128)S(1)}, f32[1024,1024,3]{1,0,2:T(8,128)}) fusion(f32[3,1024,1024]{1,2,0:T(8,128)} %get-tuple-element.92, f32[3,1024]{1,0:T(4,128)S(1)} %copy-done.27, bf16[1024,3,64]{0,2,1:T(8,128)(2,1)S(1)} %reshape.351, f32[1024,320]{0,1:T(8,128)} %fusion.48), kind=kOutput, calls=%fused_computation.3 | convolution fusion | flops 412087296 | bytes 25714688 | tf_op jit(solution)/shard_map/qrh,kh->rqk/dot_general | solution.py:826
  379.2 10.4 %fusion.3 = bf16[3,1024,1024]{1,2,0:T(8,128)(2,1)S(1)} fusion(f32[1024,1024,3]{1,0,2:T(8,128)} %get-tuple-element.99, f32[3,1024]{1,0:T(4,128)S(1)} %get-tuple-element.98, f32[3,1024,1024]{1,2,0:T(8,128)} %get-tuple-element.92, f32[3,1024]{1,0:T(4,128)S(1)} %copy-done.27), kind=kLoop, calls=%fused_computation.5 | loop fusion | flops 12582912 | bytes 31481856 | tf_op jit(solution)/shard_map/convert_element_type | solution.py:829
  402.2 5.5 fusion.26
  417.5 5.2 all-to-all-start.1
  430.6 76.5 %shard_map.235 = (bf16[8,128,1536]{2,1,0:T(8,128)(2,1)S(1)}, f32[96,384]{1,0:T(8,128)S(1)}, f32[96,1536]{1,0:T(8,128)S(1)}) custom-call(bf16[8,128,1536]{2,1,0:T(8,128)(2,1)S(1)} %bitcast.159, bf16[16,96,384]{2,1,0:T(8,128)(2,1)S(1)} %concatenate.41.refs_1_, bf16[16,96,1536]{2,1,0:T(8,128)(2,1)S(1)} %bitcast.158), custom_call_target="tpu_custom_call" | custom-call | flops 44999999488 | tf_op jit(solution)/shard_map/pallas_call | solution.py:386
  507.6 6.5 %fusion.21 = (bf16[5,288,512]{2,1,0:T(8,128)(2,1)}, bf16[5,288,512]{2,1,0:T(8,128)(2,1)}) fusion(bf16[5,288,512]{2,1,0:T(8,128)(2,1)} %collective-permute-done.9, bf16[8,5,288,512]{3,2,1,0:T(8,128)(2,1)} %get-tuple-element.55, bf16[8,5,288,512]{3,2,1,0:T(8,128)(2,1)} %get-tuple-element.54, bf16[5,288,512]{2,1,0:T(8,128)(2,1)} %collective-permute-done.13), kind=kLoop, calls=%fused_computation.37 | loop fusion | flops 11796480 | bytes 11796480 | tf_op jit(solution)/shard_map/convert_element_type | solution.py:629
  515.9 14.4 %shard_map.236 = (f32[8,12,384]{2,1,0:T(8,128)}, f32[8,12,1536]{2,1,0:T(8,128)}) custom-call(f32[8,12,384]{2,1,0:T(8,128)} %reshape.355.refs_0_, f32[8,12,1536]{2,1,0:T(8,128)} %reshape.356.refs_1_), custom_call_target="tpu_custom_call" | custom-call | flops 10000000000 | tf_op jit(solution)/shard_map/pallas_call | solution.py:116
  534.0 11.4 %collective-permute-done.14 = bf16[5,288,512]{2,1,0:T(8,128)(2,1)} collective-permute-done((bf16[5,288,512]{2,1,0:T(8,128)(2,1)}, bf16[5,288,512]{2,1,0:T(8,128)(2,1)}, u32[]{:S(2)}, u32[]{:S(2)}) %collective-permute-start.14) | collective-permute-done | bytes 1474592 | tf_op jit(solution)/shard_map/ppermute | solution.py:605
  545.4 4.7 fusion.20
  561.0 6.9 %collective-permute-done.10 = bf16[5,288,512]{2,1,0:T(8,128)(2,1)} collective-permute-done((bf16[5,288,512]{2,1,0:T(8,128)(2,1)}, bf16[5,288,512]{2,1,0:T(8,128)(2,1)}, u32[]{:S(2)}, u32[]{:S(2)}) %collective-permute-start.10) | collective-permute-done | bytes 1474592 | tf_op jit(solution)/shard_map/ppermute | solution.py:605
  567.8 12.6 %collective-permute-done.15 = bf16[5,288,512]{2,1,0:T(8,128)(2,1)} collective-permute-done((bf16[5,288,512]{2,1,0:T(8,128)(2,1)}, bf16[5,288,512]{2,1,0:T(8,128)(2,1)}, u32[]{:S(2)}, u32[]{:S(2)}) %collective-permute-start.15) | collective-permute-done | bytes 1474592 | tf_op jit(solution)/shard_map/ppermute | solution.py:605
  580.4 4.1 fusion.23
  (215 shorter events, 106.8 us)
Async XLA Ops:
  10.5 78.8 %copy-start.13 = (bf16[128,1536]{1,0:T(8,128)(2,1)S(1)}, bf16[128,1536]{1,0:T(8,128)(2,1)}, u32[]{:S(2)}) copy-start(bf16[128,1536]{1,0:T(8,128)(2,1)} %param.15) | copy-start | bytes 1179652
  84.5 35.5 %collective-permute-start = (bf16[5,288,512]{2,1,0:T(8,128)(2,1)}, bf16[5,288,512]{2,1,0:T(8,128)(2,1)}, u32[]{:S(2)}, u32[]{:S(2)}) collective-permute-start(bf16[5,288,512]{2,1,0:T(8,128)(2,1)} %pad_maximum_fusion.refs_2_.refs_4_), channel_id=1, source_target_pairs={{0,64},{8,72},{16,80},{24,88},{32,96},{40,104},{48,112},{56,120},{... | collective-permute-start | bytes 4423688 | tf_op jit(solution)/shard_map/ppermute | solution.py:605
  86.1 77.1 %collective-permute-start.2 = (bf16[5,288,512]{2,1,0:T(8,128)(2,1)}, bf16[5,288,512]{2,1,0:T(8,128)(2,1)}, u32[]{:S(2)}, u32[]{:S(2)}) collective-permute-start(bf16[5,288,512]{2,1,0:T(8,128)(2,1)} %pad_maximum_fusion.refs_2_.refs_4_), channel_id=1, source_target_pairs={{0,16},{8,24},{16,32},{24,40},{32,48},{40,56},{48,0},{56,8},{64,80... | collective-permute-start | bytes 4423688 | tf_op jit(solution)/shard_map/ppermute | solution.py:605
  87.6 141.5 %collective-permute-start.1 = (bf16[5,288,512]{2,1,0:T(8,128)(2,1)}, bf16[5,288,512]{2,1,0:T(8,128)(2,1)}, u32[]{:S(2)}, u32[]{:S(2)}) collective-permute-start(bf16[5,288,512]{2,1,0:T(8,128)(2,1)} %pad_maximum_fusion.refs_2_.refs_4_), channel_id=1, source_target_pairs={{0,48},{8,56},{16,0},{24,8},{32,16},{40,24},{48,32},{56,40},{64,11... | collective-permute-start | bytes 4423688 | tf_op jit(solution)/shard_map/ppermute | solution.py:605
  91.3 178.1 %all-to-all-start = ((bf16[8,128,1536]{2,1,0:T(8,128)(2,1)}), bf16[8,128,1536]{2,1,0:T(8,128)(2,1)}, u32[]{:S(2)}, u32[]{:S(2)}) async-start(bf16[8,128,1536]{2,1,0:T(8,128)(2,1)} %broadcast_in_dim.41), calls=%async_computation | async-start | bytes 6291456 | tf_op jit(solution)/shard_map/all_to_all | solution.py:625
  115.0 24.0 %copy-start.26 = (f32[3,1024]{1,0:T(4,128)}, f32[3,1024]{1,0:T(4,128)S(1)}, u32[]{:S(2)}) copy-start(f32[3,1024]{1,0:T(4,128)S(1)} %get-tuple-element.91) | copy-start | bytes 36868
  120.0 45.3 %collective-permute-start.3 = (bf16[5,288,512]{2,1,0:T(8,128)(2,1)}, bf16[5,288,512]{2,1,0:T(8,128)(2,1)}, u32[]{:S(2)}, u32[]{:S(2)}) collective-permute-start(bf16[5,288,512]{2,1,0:T(8,128)(2,1)} %collective-permute-done.refs_3_.refs_5_), channel_id=1, source_target_pairs={{0,48},{8,56},{16,0},{24,8},{32,16},{40,24},{48,32},{56,40},{64,11... | collective-permute-start | bytes 4423688 | tf_op jit(solution)/shard_map/ppermute | solution.py:605
  140.1 27.8 %copy-start.3 = (bf16[128,1536]{1,0:T(8,128)(2,1)S(1)}, bf16[128,1536]{1,0:T(8,128)(2,1)}, u32[]{:S(2)}) copy-start(bf16[128,1536]{1,0:T(8,128)(2,1)} %refs_2_.1) | copy-start | bytes 1179652
  161.5 67.6 %collective-permute-start.4 = (bf16[5,288,512]{2,1,0:T(8,128)(2,1)}, bf16[5,288,512]{2,1,0:T(8,128)(2,1)}, u32[]{:S(2)}, u32[]{:S(2)}) collective-permute-start(bf16[5,288,512]{2,1,0:T(8,128)(2,1)} %collective-permute-done.refs_3_.refs_5_), channel_id=1, source_target_pairs={{0,16},{8,24},{16,32},{24,40},{32,48},{40,56},{48,0},{56,8},{64,80... | collective-permute-start | bytes 4423688 | tf_op jit(solution)/shard_map/ppermute | solution.py:605
  163.2 65.3 %collective-permute-start.5 = (bf16[5,288,512]{2,1,0:T(8,128)(2,1)}, bf16[5,288,512]{2,1,0:T(8,128)(2,1)}, u32[]{:S(2)}, u32[]{:S(2)}) collective-permute-start(bf16[5,288,512]{2,1,0:T(8,128)(2,1)} %collective-permute-done.2.refs_5_.refs_7_), channel_id=1, source_target_pairs={{0,16},{8,24},{16,32},{24,40},{32,48},{40,56},{48,0},{56,8},{64,80... | collective-permute-start | bytes 4423688 | tf_op jit(solution)/shard_map/ppermute | solution.py:605
  165.4 63.2 %collective-permute-start.6 = (bf16[5,288,512]{2,1,0:T(8,128)(2,1)}, bf16[5,288,512]{2,1,0:T(8,128)(2,1)}, u32[]{:S(2)}, u32[]{:S(2)}) collective-permute-start(bf16[5,288,512]{2,1,0:T(8,128)(2,1)} %collective-permute-done.3.refs_6_.refs_8_), channel_id=1, source_target_pairs={{0,48},{8,56},{16,0},{24,8},{32,16},{40,24},{48,32},{56,40},{64,11... | collective-permute-start | bytes 4423688 | tf_op jit(solution)/shard_map/ppermute | solution.py:605
  171.9 57.1 %copy-start.5 = (bf16[128,1536]{1,0:T(8,128)(2,1)}, bf16[128,1536]{1,0:T(8,128)(2,1)S(1)}, u32[]{:S(2)}) copy-start(bf16[128,1536]{1,0:T(8,128)(2,1)S(1)} %multiply_convert_fusion.refs_0_) | copy-start | bytes 1179652
  228.5 40.9 %collective-permute-start.7 = (bf16[5,288,512]{2,1,0:T(8,128)(2,1)}, bf16[5,288,512]{2,1,0:T(8,128)(2,1)}, u32[]{:S(2)}, u32[]{:S(2)}) collective-permute-start(bf16[5,288,512]{2,1,0:T(8,128)(2,1)} %collective-permute-done.5.refs_10_), channel_id=1, source_target_pairs={{0,8},{8,0},{16,24},{24,16},{32,40},{40,32},{48,56},{56,48},{64,72... | collective-permute-start | bytes 4423688 | tf_op jit(solution)/shard_map/ppermute | solution.py:605
  228.5 40.9 %collective-permute-start.8 = (bf16[5,288,512]{2,1,0:T(8,128)(2,1)}, bf16[5,288,512]{2,1,0:T(8,128)(2,1)}, u32[]{:S(2)}, u32[]{:S(2)}) collective-permute-start(bf16[5,288,512]{2,1,0:T(8,128)(2,1)} %collective-permute-done.6.refs_11_), channel_id=1, source_target_pairs={{0,8},{8,0},{16,24},{24,16},{32,40},{40,32},{48,56},{56,48},{64,72... | collective-permute-start | bytes 4423688 | tf_op jit(solution)/shard_map/ppermute | solution.py:605
  407.7 99.9 %collective-permute-start.13 = (bf16[5,288,512]{2,1,0:T(8,128)(2,1)}, bf16[5,288,512]{2,1,0:T(8,128)(2,1)}, u32[]{:S(2)}, u32[]{:S(2)}) collective-permute-start(bf16[5,288,512]{2,1,0:T(8,128)(2,1)} %get-tuple-element.67), channel_id=1, source_target_pairs={{0,48},{8,56},{16,0},{24,8},{32,16},{40,24},{48,32},{56,40},{64,11... | collective-permute-start | bytes 4423688 | tf_op jit(solution)/shard_map/ppermute | solution.py:605
  408.7 99.0 %collective-permute-start.9 = (bf16[5,288,512]{2,1,0:T(8,128)(2,1)}, bf16[5,288,512]{2,1,0:T(8,128)(2,1)}, u32[]{:S(2)}, u32[]{:S(2)}) collective-permute-start(bf16[5,288,512]{2,1,0:T(8,128)(2,1)} %get-tuple-element.66), channel_id=1, source_target_pairs={{0,16},{8,24},{16,32},{24,40},{32,48},{40,56},{48,0},{56,8},{64,80... | collective-permute-start | bytes 4423688 | tf_op jit(solution)/shard_map/ppermute | solution.py:605
  409.8 124.2 %collective-permute-start.12 = (bf16[5,288,512]{2,1,0:T(8,128)(2,1)}, bf16[5,288,512]{2,1,0:T(8,128)(2,1)}, u32[]{:S(2)}, u32[]{:S(2)}) collective-permute-start(bf16[5,288,512]{2,1,0:T(8,128)(2,1)} %get-tuple-element.68), channel_id=1, source_target_pairs={{0,16},{8,24},{16,32},{24,40},{32,48},{40,56},{48,0},{56,8},{64,80... | collective-permute-start | bytes 4423688 | tf_op jit(solution)/shard_map/ppermute | solution.py:605
  410.1 150.9 %collective-permute-start.11 = (bf16[5,288,512]{2,1,0:T(8,128)(2,1)}, bf16[5,288,512]{2,1,0:T(8,128)(2,1)}, u32[]{:S(2)}, u32[]{:S(2)}) collective-permute-start(bf16[5,288,512]{2,1,0:T(8,128)(2,1)} %get-tuple-element.69), channel_id=1, source_target_pairs={{0,48},{8,56},{16,0},{24,8},{32,16},{40,24},{48,32},{56,40},{64,11... | collective-permute-start | bytes 4423688 | tf_op jit(solution)/shard_map/ppermute | solution.py:605
  417.5 140.2 %all-to-all-start.1 = ((bf16[8,128,1536]{2,1,0:T(8,128)(2,1)}), bf16[8,128,1536]{2,1,0:T(8,128)(2,1)}, u32[]{:S(2)}, u32[]{:S(2)}) async-start(bf16[8,128,1536]{2,1,0:T(8,128)(2,1)} %get-tuple-element.48), calls=%async_computation.1 | async-start | bytes 6291456 | tf_op jit(solution)/shard_map/all_to_all | solution.py:625
  514.1 31.3 %collective-permute-start.14 = (bf16[5,288,512]{2,1,0:T(8,128)(2,1)}, bf16[5,288,512]{2,1,0:T(8,128)(2,1)}, u32[]{:S(2)}, u32[]{:S(2)}) collective-permute-start(bf16[5,288,512]{2,1,0:T(8,128)(2,1)} %get-tuple-element.65), channel_id=1, source_target_pairs={{0,48},{8,56},{16,0},{24,8},{32,16},{40,24},{48,32},{56,40},{64,11... | collective-permute-start | bytes 4423688 | tf_op jit(solution)/shard_map/ppermute | solution.py:605
  532.3 24.1 %copy-start.31 = (f32[128]{0:T(128)S(1)}, f32[128]{0:T(128)}, u32[]{:S(2)}) copy-start(f32[128]{0:T(128)} %get-tuple-element.85) | copy-start | bytes 1540
  532.3 24.1 %copy-start.32 = (f32[128]{0:T(128)S(1)}, f32[128]{0:T(128)}, u32[]{:S(2)}) copy-start(f32[128]{0:T(128)} %get-tuple-element.86) | copy-start | bytes 1540
  532.4 35.4 %collective-permute-start.10 = (bf16[5,288,512]{2,1,0:T(8,128)(2,1)}, bf16[5,288,512]{2,1,0:T(8,128)(2,1)}, u32[]{:S(2)}, u32[]{:S(2)}) collective-permute-start(bf16[5,288,512]{2,1,0:T(8,128)(2,1)} %get-tuple-element.64), channel_id=1, source_target_pairs={{0,16},{8,24},{16,32},{24,40},{32,48},{40,56},{48,0},{56,8},{64,80... | collective-permute-start | bytes 4423688 | tf_op jit(solution)/shard_map/ppermute | solution.py:605
  550.1 30.4 %collective-permute-start.15 = (bf16[5,288,512]{2,1,0:T(8,128)(2,1)}, bf16[5,288,512]{2,1,0:T(8,128)(2,1)}, u32[]{:S(2)}, u32[]{:S(2)}) collective-permute-start(bf16[5,288,512]{2,1,0:T(8,128)(2,1)} %fusion.20), channel_id=1, source_target_pairs={{0,64},{8,72},{16,80},{24,88},{32,96},{40,104},{48,112},{56,120},{... | collective-permute-start | bytes 4423688 | tf_op jit(solution)/shard_map/ppermute | solution.py:605
  (37 other events, 250.0 us)

commit v3 on v2

--- a/solution.py
+++ b/solution.py
@@ -1,3 +1,4 @@
+import functools
 import math
 
 import jax
@@ -23,6 +24,8 @@
 SLICE = 384
 QS = REP * HEAD
 ROWS = 96
+ROUTER = QS + 2 * HEAD
+GAINS = ROUTER + EXPERTS
 
 epsilon = 1e-06
 rope_base = 10000.0
@@ -128,174 +131,509 @@
     )(*arrays)
 
 
-def gather_start(slices, output, arrays, modes, cid):
-    n = len(arrays)
-    small = (slices, output)
-    widths = (slices.shape[-1], output.shape[-1])
-
-    def kernel(*refs):
-        sins, ins = refs[:2], refs[2 : 2 + n]
-        douts, outs = refs[2 + n : 4 + n], refs[4 + n : 4 + 2 * n]
-        pieces, rows = refs[4 + 2 * n : 6 + 2 * n], refs[6 + 2 * n : 8 + 2 * n]
-        ssend, srecv, slocal, dsend, drecv, dlocal, send, recv, local = refs[8 + 2 * n :]
+class Gather:
+    def __init__(self, src, out, send, recv, local):
+        self.src, self.out, self.send, self.recv, self.local = src, out, send, recv, local
+        me = lax.axis_index("expert")
+        z, x = me // 2, me % 2
+
+        def place(dz, dx):
+            return (z + dz) % 4 * 2 + (x + dx) % 2
+
+        self.me, self.across, self.up, self.down = me, place(0, 1), place(1, 0), place(3, 0)
+        self.slots = [
+            place(0, 1),
+            place(3, 0),
+            place(1, 0),
+            place(3, 1),
+            place(1, 1),
+            place(2, 0),
+            place(2, 1),
+        ]
+        self.started = []
+
+    def copy(self, k, src, slot, target):
+        c = pltpu.make_async_remote_copy(
+            src_ref=src,
+            dst_ref=self.out.at[slot],
+            send_sem=self.send.at[k],
+            recv_sem=self.recv.at[k],
+            device_id={"expert": target},
+            device_id_type=MESH,
+        )
+        c.start()
+        self.started.append(c)
+
+    def arrive(self, k):
+        pltpu.make_async_remote_copy(
+            src_ref=self.src,
+            dst_ref=self.out.at[self.slots[k]],
+            send_sem=self.send.at[k],
+            recv_sem=self.recv.at[k],
+            device_id={"expert": self.up},
+            device_id_type=MESH,
+        ).wait_recv()
+
+    def begin(self):
+        self.copy(0, self.src, self.me, self.across)
+        self.copy(1, self.src, self.me, self.up)
+        self.copy(2, self.src, self.me, self.down)
+        self.own = pltpu.make_async_copy(self.src, self.out.at[self.me], self.local)
+        self.own.start()
+
+    def first(self):
+        self.arrive(0)
+        self.copy(3, self.out.at[self.slots[0]], self.slots[0], self.up)
+        self.copy(4, self.out.at[self.slots[0]], self.slots[0], self.down)
+
+    def second(self):
+        self.arrive(1)
+        self.copy(5, self.out.at[self.slots[1]], self.slots[1], self.up)
+
+    def third(self):
+        self.arrive(4)
+        self.copy(6, self.out.at[self.slots[4]], self.slots[4], self.down)
+
+    def finish(self):
+        for k in (2, 3, 5, 6):
+            self.arrive(k)
+        for c in self.started:
+            c.wait_send()
+        self.own.wait()
+
+
+class Dense:
+    def __init__(self, rows, out, send, recv, local):
+        self.rows, self.out, self.send, self.recv, self.local = rows, out, send, recv, local
         x, y, core = dp_place()
-        mine = dp_index(x, y, core)
-        to_x, to_up, to_down, to_core = (
+        self.x, self.y, self.core = x, y, core
+        self.mine = dp_index(x, y, core)
+        self.to_x, self.to_up = dp_index(x + 1, y, core), dp_index(x, y + 1, core)
+        self.to_down, self.to_core = dp_index(x, y + 3, core), dp_index(x, y, core + 1)
+        self.slots = [dp_index(x + rx, y + ry, core) for rx, ry in SLOTS]
+        self.started = []
+
+    def descriptor(self, k, src, slot, target):
+        return pltpu.make_async_remote_copy(
+            src_ref=src,
+            dst_ref=self.out.at[slot],
+            send_sem=self.send.at[k],
+            recv_sem=self.recv.at[k],
+            device_id={"dp": target},
+            device_id_type=MESH,
+        )
+
+    def copy(self, k, slot, target, src=None):
+        c = self.descriptor(k, self.out.at[slot] if src is None else src, slot, target)
+        c.start()
+        self.started.append(c)
+
+    def arrive(self, k, slot):
+        self.descriptor(k, self.out.at[slot], slot, self.to_x).wait_recv()
+
+    def share(self, k):
+        self.copy(8 + k, self.slots[k], self.to_core)
+
+    def begin(self):
+        self.copy(1, self.mine, self.to_x, self.rows)
+        self.copy(3, self.mine, self.to_up, self.rows)
+        self.copy(2, self.mine, self.to_down, self.rows)
+        self.copy(8, self.mine, self.to_core, self.rows)
+        self.own = pltpu.make_async_copy(self.rows, self.out.at[self.mine], self.local)
+        self.own.start()
+
+    def first(self):
+        self.arrive(1, self.slots[1])
+        self.copy(5, self.slots[1], self.to_up)
+        self.copy(4, self.slots[1], self.to_down)
+        self.share(1)
+        self.arrive(3, self.slots[3])
+        self.copy(6, self.slots[3], self.to_up)
+        self.share(3)
+        self.arrive(2, self.slots[2])
+        self.share(2)
+
+    def second(self):
+        self.arrive(4, self.slots[4])
+        self.copy(7, self.slots[4], self.to_down)
+        self.share(4)
+        self.arrive(5, self.slots[5])
+        self.share(5)
+
+    def third(self):
+        for k in (6, 7):
+            self.arrive(k, self.slots[k])
+            self.share(k)
+
+    def finish(self):
+        for k, (rx, ry) in enumerate(SLOTS):
+            self.arrive(8 + k, dp_index(self.x + rx, self.y + ry, self.core + 1))
+        for c in self.started:
+            c.wait_send()
+        self.own.wait()
+
+
+class Pieces:
+    parts = ((0, 3), (3, 1), (4, 1))
+
+    def __init__(self, piece, out, send, recv, local):
+        self.piece, self.out, self.send, self.recv, self.local = piece, out, send, recv, local
+        x, y, core = dp_place()
+        self.x, self.y, self.core = x, y, core
+        self.mine = dp_index(x, y, core)
+        self.targets = {
+            "x": dp_index(x + 1, y, core),
+            "up": dp_index(x, y + 1, core),
+            "down": dp_index(x, y + 3, core),
+            "core": dp_index(x, y, core + 1),
+        }
+        self.slots = [dp_index(x + rx, y + ry, core) for rx, ry in SLOTS]
+        self.started = []
+
+    def descriptor(self, g, k, src, slot, target):
+        first, count = self.parts[g]
+        return pltpu.make_async_remote_copy(
+            src_ref=src.at[pl.ds(first, count)],
+            dst_ref=self.out.at[slot, pl.ds(first, count)],
+            send_sem=self.send.at[g, k],
+            recv_sem=self.recv.at[g, k],
+            device_id={"dp": target},
+            device_id_type=MESH,
+        )
+
+    def move(self, g, k, where, source=0):
+        src = self.piece if source == 0 else self.out.at[self.slots[source]]
+        c = self.descriptor(g, k, src, self.slots[source], self.targets[where])
+        c.start()
+        self.started.append(c)
+
+    def arrive(self, g, k, share=True):
+        slot = self.slots[k]
+        self.descriptor(g, k, self.out.at[slot], slot, self.targets["x"]).wait_recv()
+        if share:
+            self.move(g, 8 + k, "core", k)
+
+    def begin(self):
+        for g in range(3):
+            self.move(g, 8, "core")
+        self.own = pltpu.make_async_copy(self.piece, self.out.at[self.mine], self.local)
+        self.own.start()
+
+    def finish(self):
+        for g in range(3):
+            for k, (rx, ry) in enumerate(SLOTS):
+                slot = dp_index(self.x + rx, self.y + ry, self.core + 1)
+                self.descriptor(
+                    g, 8 + k, self.out.at[slot], slot, self.targets["x"]
+                ).wait_recv()
+        for c in self.started:
+            c.wait_send()
+        self.own.wait()
+
+
+def first_kernel(*refs):
+    (slices, output, tokens, cot, member_ref, slot_send, piece, cos_ref, sin_ref, start_ref) = refs[
+        :10
+    ]
+    (
+        pieces_out,
+        cot_all,
+        slots_all,
+        rows_all,
+        gates_all,
+        tokens_out,
+        normed_out,
+        small_out,
+        output_out,
+        query_ref,
+        key_ref,
+        value_ref,
+        log_ref,
+        attended_ref,
+        middle_ref,
+        normed_two_ref,
+        gates_ref,
+    ) = refs[10:27]
+    (
+        small_in,
+        output_in,
+        small_rows,
+        output_rows,
+        small,
+        dense,
+        tokens_in,
+        normed,
+        att_send,
+        gate_send,
+        s_small,
+        s_dense,
+        s_piece,
+        r_small,
+        r_dense,
+        r_piece,
+        s_gather,
+        r_gather,
+        s_direct,
+        r_direct,
+        l_sem,
+    ) = refs[27:]
+    _, peers = expert_peers()
+    x, y, core = dp_place()
+    signal_all(
+        peers,
+        [
             dp_index(x + 1, y, core),
             dp_index(x, y + 1, core),
             dp_index(x, y + 3, core),
             dp_index(x, y, core + 1),
+        ],
+    )
+
+    def direct(i, src, out, mode):
+        part = expert_copies(
+            [src], [out], [mode], s_direct.at[pl.ds(i, 1)], r_direct.at[pl.ds(i, 1)]
+        ) + own_copies([src], [out], [mode], l_sem.at[pl.ds(i, 1)])
+        for c in part:
+            c.start()
+        return part
+
+    def settle(part):
+        for c in part:
+            c.wait()
+
+    saved = []
+
+    def save(src, dst, i):
+        c = pltpu.make_async_copy(src, dst, l_sem.at[i])
+        c.start()
+        saved.append(c)
+
+    parts = [
+        direct(0, slices, small_in, "exchange"),
+        direct(1, output, output_in, "gather"),
+        direct(2, slot_send, slots_all, "exchange"),
+    ]
+    tokens_gather = Gather(tokens, tokens_in, s_gather.at[0], r_gather.at[0], l_sem.at[5])
+    tokens_gather.begin()
+    experts = Pieces(piece, pieces_out, s_piece, r_piece, l_sem.at[6])
+    experts.begin()
+    for g in (1, 2):
+        experts.move(g, 3, "up")
+        experts.move(g, 2, "down")
+
+    weights = []
+    for i, (landed, rows, out) in enumerate(
+        ((small_in, small_rows, small), (output_in, output_rows, dense))
+    ):
+        settle(parts[i])
+        rows[...] = jnp.concatenate([landed[j] for j in range(PEERS)], axis=0)
+        weights.append(Dense(rows, out, s_dense.at[i], r_dense.at[i], l_sem.at[7 + i]))
+        weights[i].begin()
+    experts.move(0, 1, "x")
+    for g in (1, 2):
+        experts.move(g, 1, "x")
+    tokens_gather.first()
+    for w in weights:
+        w.first()
+    tokens_gather.second()
+    for w in weights:
+        w.second()
+    tokens_gather.third()
+    experts.move(0, 3, "up")
+    experts.move(0, 2, "down")
+    cot_gather = Gather(cot, cot_all, s_gather.at[1], r_gather.at[1], l_sem.at[9])
+    cot_gather.begin()
+    for w in weights:
+        w.third()
+    weights[0].finish()
+    tokens_gather.finish()
+
+    for g in (1, 2):
+        experts.arrive(g, 3)
+        experts.arrive(g, 2)
+    experts.move(1, 6, "up", 3)
+    experts.move(2, 6, "down", 2)
+    for g in (1, 2):
+        experts.move(g, 5, "x", 3)
+        experts.move(g, 4, "x", 2)
+
+    w_small = small[...].reshape(DIM, SLICE)
+    pick = (
+        lax.broadcasted_iota(jnp.int32, (8, SLICE), 1)
+        == lax.broadcasted_iota(jnp.int32, (8, SLICE), 0) + GAINS
+    )
+    gains = dot(pick.astype(F32).astype(BF), w_small, ((1,), (1,)))
+    gain_one, gain_two = gains[0:1], gains[1:2]
+
+    def project(i, _):
+        values = tokens_in[pl.ds(2 * i, 2)].reshape(2 * TOK, DIM).astype(F32)
+        scale = lax.rsqrt(jnp.mean(values * values, axis=-1, keepdims=True) + epsilon)
+        low = (values * scale * gain_one).astype(BF)
+        normed[pl.ds(2 * i, 2)] = low.reshape(2, TOK, DIM)
+        qkv = dot(low, small[...].reshape(DIM, SLICE), ((1,), (0,)))
+        span = pl.ds(pl.multiple_of(i * 2 * TOK, 2 * TOK), 2 * TOK)
+        cosine, sine = cos_ref[span, :], sin_ref[span, :]
+        lane = lax.broadcasted_iota(jnp.int32, (2 * TOK, 128), 1)
+        turned = []
+        for h in range(2):
+            v = qkv[:, 128 * h : 128 * h + 128]
+            other = jnp.where(lane % HEAD < HEAD // 2, pltpu.roll(v, 96, 1), pltpu.roll(v, 32, 1))
+            turned.append((v * cosine + other * sine).astype(BF))
+        heads = (turned[0][:, :HEAD], turned[0][:, HEAD:], turned[1][:, :HEAD])
+        for b in range(2):
+            for h in range(REP):
+                query_ref[2 * i + b, h * TOK : (h + 1) * TOK, :] = heads[h][
+                    b * TOK : (b + 1) * TOK
+                ]
+        key_ref[span, :] = turned[1][:, HEAD:]
+        value_ref[span, :] = qkv[:, QS + HEAD : ROUTER].astype(BF)
+        return _
+
+    lax.fori_loop(0, 4, project, 0)
+    save(tokens_in, tokens_out, 10)
+    save(normed, normed_out, 11)
+    save(small, small_out, 12)
+
+    def attend(width, i, _):
+        scores = dot(query_ref[i], key_ref[0:width, :], ((1,), (1,))) * HEAD ** (-0.5)
+        keys = lax.broadcasted_iota(jnp.int32, (TOK, width), 1)
+        rows = lax.broadcasted_iota(jnp.int32, (TOK, width), 0) + i * TOK
+        begins = start_ref[pl.ds(pl.multiple_of(i * TOK, TOK), TOK), :][:, :1]
+        allowed = (keys <= rows) & (keys >= begins)
+        scores = jnp.where(allowed[None], scores.reshape(REP, TOK, width), masked_score)
+        top = jnp.max(scores, axis=-1, keepdims=True)
+        terms = jnp.exp(scores - top)
+        total = jnp.sum(terms, axis=-1, keepdims=True)
+        probs = (terms / total).astype(BF).reshape(REP * TOK, width)
+        out = dot(probs, value_ref[0:width, :], ((1,), (0,))).astype(BF)
+        att_send[i] = jnp.concatenate([out[h * TOK : (h + 1) * TOK] for h in range(REP)], axis=1)
+        log_ref[i] = jnp.broadcast_to(
+            (top + jnp.log(total)).reshape(REP * TOK, 1), (REP * TOK, 128)
         )
-        _, peers = expert_peers()
-        signal_all(peers, [to_x, to_up, to_down, to_core])
-
-        def move(i, k, slot, target, src=None):
-            return pltpu.make_async_remote_copy(
-                src_ref=douts[i].at[slot] if src is None else src,
-                dst_ref=douts[i].at[slot],
-                send_sem=dsend.at[i, k],
-                recv_sem=drecv.at[i, k],
-                device_id={"dp": target},
-                device_id_type=MESH,
-            )
-
-        def arrived(i, k, slot):
-            move(i, k, slot, to_x).wait_recv()
-
-        started = []
-
-        def go(c):
-            c.start()
-            started.append(c)
-
-        sibling = [dp_index(x + rx, y + ry, core) for rx, ry in SLOTS]
-        first = []
-        for i, mode in enumerate(("exchange", "gather")):
-            part = expert_copies(
-                [sins[i]], [pieces[i]], [mode], ssend.at[pl.ds(i, 1)], srecv.at[pl.ds(i, 1)]
-            ) + own_copies([sins[i]], [pieces[i]], [mode], slocal.at[pl.ds(i, 1)])
-            for c in part:
-                c.start()
-            first.append(part)
-        more = expert_copies(ins, outs, modes, send, recv) + own_copies(ins, outs, modes, local)
-        for c in more:
-            c.start()
-        locals_ = []
-        for i in range(2):
-            for c in first[i]:
-                c.wait()
-            rows[i][...] = jnp.concatenate([pieces[i][j] for j in range(PEERS)], axis=0)
-            c = pltpu.make_async_copy(rows[i], douts[i].at[mine], dlocal.at[i])
-            c.start()
-            locals_.append(c)
-            go(move(i, 0, mine, to_x, rows[i]))
-            go(move(i, 1, mine, to_up, rows[i]))
-            go(move(i, 2, mine, to_down, rows[i]))
-            go(move(i, 7, mine, to_core, rows[i]))
-        for i in range(2):
-            arrived(i, 0, sibling[1])
-            go(move(i, 3, sibling[1], to_up))
-            go(move(i, 4, sibling[1], to_down))
-            go(move(i, 8, sibling[1], to_core))
-            arrived(i, 1, sibling[3])
-            go(move(i, 5, sibling[3], to_up))
-            go(move(i, 10, sibling[3], to_core))
-            arrived(i, 2, sibling[2])
-            go(move(i, 9, sibling[2], to_core))
-        for i in range(2):
-            arrived(i, 4, sibling[4])
-            go(move(i, 6, sibling[4], to_down))
-            go(move(i, 11, sibling[4], to_core))
-            arrived(i, 3, sibling[5])
-            go(move(i, 12, sibling[5], to_core))
-        for i in range(2):
-            arrived(i, 5, sibling[6])
-            go(move(i, 13, sibling[6], to_core))
-            arrived(i, 6, sibling[7])
-            go(move(i, 14, sibling[7], to_core))
-        for i in range(2):
-            for k in range(8):
-                rx, ry = SLOTS[k]
-                arrived(i, 7 + k, dp_index(x + rx, y + ry, core + 1))
-        for c in started:
-            c.wait_send()
-        for c in more + locals_:
-            c.wait()
-
-    shapes = [jax.ShapeDtypeStruct((DP, ROWS, w), BF) for w in widths] + [
-        jax.ShapeDtypeStruct(((PEERS,) + a.shape) if k == "gather" else a.shape, a.dtype)
-        for a, k in zip(arrays, modes)
+        return _
+
+    experts.arrive(0, 1)
+    experts.move(0, 5, "up", 1)
+    experts.move(0, 4, "down", 1)
+    cot_gather.first()
+    cot_gather.second()
+    lax.fori_loop(0, 4, functools.partial(attend, GROUP // 2), 0)
+    for g in (1, 2):
+        experts.arrive(g, 1)
+    cot_gather.third()
+    lax.fori_loop(4, 8, functools.partial(attend, GROUP), 0)
+    parts.append(direct(3, att_send, attended_ref, "exchange"))
+    experts.arrive(0, 3)
+    experts.move(0, 6, "up", 3)
+    experts.arrive(0, 2)
+    for g in (1, 2):
+        experts.arrive(g, 4)
+        experts.arrive(g, 5)
+    settle(parts[3])
+    weights[1].finish()
+    save(dense, output_out, 13)
+
+    me = lax.axis_index("expert")
+    middle = tokens_in[me].astype(F32)
+    for j in range(PEERS):
+        middle = middle + dot(
+            attended_ref[j], dense[2 * j : 2 * j + 2].reshape(QS, DIM), ((1,), (0,))
+        )
+    middle_ref[...] = middle
+    scale_two = lax.rsqrt(jnp.mean(middle * middle, axis=-1, keepdims=True) + epsilon)
+    normed_two = (middle * scale_two * gain_two).astype(BF)
+    normed_two_ref[...] = normed_two
+    rows_gather = Gather(normed_two_ref, rows_all, s_gather.at[2], r_gather.at[2], l_sem.at[14])
+    rows_gather.begin()
+    logits = dot(small[:, :, 256:SLICE].reshape(DIM, SLICE - 256), normed_two, ((0,), (1,)))
+    logits = logits[ROUTER - 256 : GAINS - 256]
+    member = member_ref[...] >= 0.0
+    chosen = jnp.where(member, logits, masked_score)
+    weight = jnp.where(member, jnp.exp(chosen - jnp.max(chosen, axis=0, keepdims=True)), 0.0)
+    gates_ref[...] = weight / jnp.sum(weight, axis=0, keepdims=True)
+    gate_send[...] = jnp.zeros_like(gate_send)
+    for j in range(PEERS):
+        gate_send[j, 0:LOCAL, :] = gates_ref[LOCAL * j : LOCAL * (j + 1), :]
+    parts.append(direct(4, gate_send, gates_all, "exchange"))
+
+    rows_gather.first()
+    rows_gather.second()
+    experts.arrive(0, 4)
+    experts.move(0, 7, "down", 4)
+    experts.arrive(0, 5)
+    rows_gather.third()
+    for g in (1, 2):
+        experts.arrive(g, 6)
+        experts.move(g, 7, "x", 6)
+    cot_gather.finish()
+    rows_gather.finish()
+    settle(parts[2])
+    settle(parts[4])
+    experts.arrive(0, 6)
+    for g in (0, 1, 2):
+        experts.arrive(g, 7)
+    experts.finish()
+    for c in saved:
+        c.wait()
+
+
+def first_phase(slices, output, tokens, cot, member, slot_send, piece, cosine, sine, start):
+    hbm, vmem = pl.BlockSpec(memory_space=pl.ANY), pl.BlockSpec(memory_space=pltpu.VMEM)
+    shape = jax.ShapeDtypeStruct
+    blocks = (PEERS, TOK, DIM)
+    outs = [
+        (shape((DP,) + piece.shape, BF), hbm),
+        (shape(blocks, BF), hbm),
+        (shape((PEERS, 8, TOK), F32), hbm),
+        (shape(blocks, BF), hbm),
+        (shape((PEERS, 8, TOK), F32), hbm),
+        (shape(blocks, BF), hbm),
+        (shape(blocks, BF), hbm),
+        (shape((DP, ROWS, SLICE), BF), hbm),
+        (shape((DP, ROWS, DIM), BF), hbm),
+        (shape((PEERS, REP * TOK, HEAD), BF), vmem),
+        (shape((GROUP, HEAD), BF), vmem),
+        (shape((GROUP, HEAD), BF), vmem),
+        (shape((PEERS, REP * TOK, 128), F32), vmem),
+        (shape((PEERS, TOK, QS), BF), vmem),
+        (shape((TOK, DIM), F32), vmem),
+        (shape((TOK, DIM), BF), vmem),
+        (shape((EXPERTS, TOK), F32), vmem),
     ]
+    dma = pltpu.SemaphoreType.DMA
     return pl.pallas_call(
-        kernel,
-        out_shape=shapes,
-        in_specs=any_specs(2 + n),
-        out_specs=any_specs(2 + n),
-        scratch_shapes=[pltpu.VMEM((PEERS, 12, w), BF) for w in widths]
-        + [pltpu.VMEM((ROWS, w), BF) for w in widths]
-        + [
-            pltpu.SemaphoreType.DMA((2, 7)),
-            pltpu.SemaphoreType.DMA((2, 7)),
-            pltpu.SemaphoreType.DMA((2,)),
-            pltpu.SemaphoreType.DMA((2, 15)),
-            pltpu.SemaphoreType.DMA((2, 15)),
-            pltpu.SemaphoreType.DMA((2,)),
-            pltpu.SemaphoreType.DMA((n, 7)),
-            pltpu.SemaphoreType.DMA((n, 7)),
-            pltpu.SemaphoreType.DMA((n,)),
+        first_kernel,
+        out_shape=[o[0] for o in outs],
+        in_specs=[hbm] * 4 + [vmem] + [hbm] * 2 + [vmem] * 3,
+        out_specs=[o[1] for o in outs],
+        scratch_shapes=[
+            pltpu.VMEM((PEERS, 12, SLICE), BF),
+            pltpu.VMEM((PEERS, 12, DIM), BF),
+            pltpu.VMEM((ROWS, SLICE), BF),
+            pltpu.VMEM((ROWS, DIM), BF),
+            pltpu.VMEM((DP, ROWS, SLICE), BF),
+            pltpu.VMEM((DP, ROWS, DIM), BF),
+            pltpu.VMEM(blocks, BF),
+            pltpu.VMEM(blocks, BF),
+            pltpu.VMEM((PEERS, TOK, QS), BF),
+            pltpu.VMEM((PEERS, 8, TOK), F32),
+            dma((1,)),
+            dma((2, 16)),
+            dma((3, 16)),
+            dma((1,)),
+            dma((2, 16)),
+            dma((3, 16)),
+            dma((3, 7)),
+            dma((3, 7)),
+            dma((5, 7)),
+            dma((5, 7)),
+            dma((15,)),
         ],
-        compiler_params=pltpu.CompilerParams(collective_id=cid, has_side_effects=True),
-        cost_estimate=lasting(45),
-    )(*small, *arrays)
-
-
-def exchange_and_share(arrays, modes, pieces, cid):
-    n, m = len(arrays), len(pieces)
-
-    def kernel(*refs):
-        ins, parts = refs[:n], refs[n : n + m]
-        outs, shared = refs[n + m : 2 * n + m], refs[2 * n + m]
-        send, recv, local, csend, crecv = refs[2 * n + m + 1 :]
-        x, y, core = dp_place()
-        other = dp_index(x, y, core + 1)
-        _, peers = expert_peers()
-        signal_all(peers, [other])
-        copies = expert_copies(ins, outs, modes, send, recv) + own_copies(ins, outs, modes, local)
-        for k in range(m):
-            copies.append(
-                pltpu.make_async_remote_copy(
-                    src_ref=parts[k],
-                    dst_ref=shared.at[k],
-                    send_sem=csend.at[k],
-                    recv_sem=crecv.at[k],
-                    device_id={"dp": other},
-                    device_id_type=MESH,
-                )
-            )
-        for c in copies:
-            c.start()
-        for c in copies:
-            c.wait()
-
-    shapes = [
-        jax.ShapeDtypeStruct(((PEERS,) + a.shape) if k == "gather" else a.shape, a.dtype)
-        for a, k in zip(arrays, modes)
-    ] + [jax.ShapeDtypeStruct((m,) + pieces[0].shape, pieces[0].dtype)]
-    return pl.pallas_call(
-        kernel,
-        out_shape=shapes,
-        in_specs=any_specs(n + m),
-        out_specs=any_specs(n + 1),
-        scratch_shapes=[
-            pltpu.SemaphoreType.DMA((n, 7)),
-            pltpu.SemaphoreType.DMA((n, 7)),
-            pltpu.SemaphoreType.DMA((n,)),
-            pltpu.SemaphoreType.DMA((m,)),
-            pltpu.SemaphoreType.DMA((m,)),
-        ],
-        compiler_params=pltpu.CompilerParams(collective_id=cid, has_side_effects=True),
-        cost_estimate=lasting(38),
-    )(*arrays, *pieces)
+        compiler_params=pltpu.CompilerParams(
+            collective_id=1, has_side_effects=True, vmem_limit_bytes=50 << 20
+        ),
+        cost_estimate=lasting(120),
+    )(slices, output, tokens, cot, member, slot_send, piece, cosine, sine, start)
 
 
 def scatter_sum(arrays, dense, cid):
@@ -418,26 +756,15 @@
 
 def experts_kernel(*refs):
     (rows_ref, cot_ref, slot_ref, gate_ref), refs = refs[:4], refs[4:]
-    pieces, shared, late, refs = refs[:8], refs[8], refs[9:11], refs[11:]
+    pieces, refs = refs[0], refs[1:]
     (out_ref, back_ref, inner_ref, keep_ref, given_ref), refs = refs[:5], refs[5:]
     xg, cg, weights, grads, gates, inners, wsem, gsem, rsem = refs
     x, y, core = dp_place()
     other = dp_index(x, y, core + 1)
     signal_all([], [other])
 
-    def loads(e, b):
-        copies = []
-        for k, (rx, ry) in enumerate(SLOTS):
-            for c in range(2):
-                src = pieces[k].at[e] if c == 0 else shared.at[k, e] if k < 6 else late[k - 6].at[e]
-                copies.append(
-                    pltpu.make_async_copy(
-                        src,
-                        weights.at[b, dp_index(x + rx, y + ry, core + c)],
-                        wsem.at[b, 2 * k + c],
-                    )
-                )
-        return copies
+    def load(e, b):
+        return pltpu.make_async_copy(pieces.at[:, e], weights.at[b], wsem.at[b])
 
     def kept(e, b):
         return [
@@ -466,8 +793,7 @@
         for c in given(e, b):
             c.wait_send()
 
-    for c in loads(0, 0):
-        c.start()
+    load(0, 0).start()
 
     def onehot(b):
         places = lax.broadcasted_iota(jnp.int32, (CAP, TOK), 0).astype(F32)
@@ -487,13 +813,11 @@
 
     def expert(e, _):
         b = lax.rem(e, 2)
-        for c in loads(e, b):
-            c.wait()
+        load(e, b).wait()
 
         @pl.when(e + 1 < LOCAL)
         def _next():
-            for c in loads(e + 1, 1 - b):
-                c.start()
+            load(e + 1, 1 - b).start()
 
         @pl.when(e >= 2)
         def _free():
@@ -563,7 +887,7 @@
             c.wait_recv()
 
 
-def run_experts(rows, cot, slots, gates, pieces, shared, late):
+def run_experts(rows, cot, slots, gates, pieces):
     vmem = pl.BlockSpec(memory_space=pltpu.VMEM)
     piece = (LOCAL, 3 * ROWS, FFE)
     return pl.pallas_call(
@@ -575,7 +899,7 @@
             jax.ShapeDtypeStruct((8,) + piece, BF),
             jax.ShapeDtypeStruct((8,) + piece, BF),
         ],
-        in_specs=[vmem] * 4 + any_specs(11),
+        in_specs=[vmem] * 4 + any_specs(1),
         out_specs=[vmem] * 3 + any_specs(2),
         scratch_shapes=[
             pltpu.VMEM((PEERS, LOCAL * CAP, DIM), BF),
@@ -584,7 +908,7 @@
             pltpu.VMEM((2, DP, 3 * ROWS, FFE), BF),
             pltpu.VMEM((LOCAL, PEERS * CAP, 128), F32),
             pltpu.VMEM((LOCAL, PEERS * CAP, 128), F32),
-            pltpu.SemaphoreType.DMA((2, 16)),
+            pltpu.SemaphoreType.DMA((2,)),
             pltpu.SemaphoreType.DMA((2, 16)),
             pltpu.SemaphoreType.DMA((LOCAL, 8)),
         ],
@@ -594,7 +918,7 @@
         cost_estimate=pl.CostEstimate(
             flops=20_000_000_000, bytes_accessed=60_000_000, transcendentals=700_000
         ),
-    )(rows, cot, slots, gates, *pieces, shared, *late)
+    )(rows, cot, slots, gates, pieces)
 
 
 def shift(value, move):
@@ -700,14 +1024,14 @@
             jnp.broadcast_to(
                 jnp.concatenate(
                     [
+                        w_router,
                         norm_one[:, None],
                         norm_two[:, None],
-                        w_router,
-                        jnp.zeros((12, SLICE - QS - 2 * HEAD - 2 - EXPERTS), BF),
+                        jnp.zeros((12, SLICE - GAINS - 2), BF),
                     ],
                     axis=1,
                 )[None],
-                (PEERS, 12, SLICE - QS - 2 * HEAD),
+                (PEERS, 12, SLICE - ROUTER),
             ),
         ],
         axis=2,
@@ -717,67 +1041,65 @@
     )
     before = jnp.arange(TOK)[:, None] < jnp.arange(TOK)[None, :]
     places = jnp.dot(member.astype(BF), before.astype(BF), preferred_element_type=F32)
-    slot_table = by_peer(jnp.where(member, places, -1.0))
-
-    slices_all, output_all, tokens_all, slots_all = gather_start(
-        slices, w_output, [tokens, slot_table], ["gather", "exchange"], 1
-    )
-    piece, cot, _ = lax.optimization_barrier((piece, cotangent, slots_all))
-    cot_all = to_peers(jnp.broadcast_to(cot[None], (PEERS, TOK, DIM)))
-    x1 = across(piece)
-    y3, y1 = up(piece), down(piece)
-    x1y3, x1y1 = up(x1), down(x1)
-    y2, x1y2 = up(y3), down(x1y1)
-    pieces = [piece, x1, y1, y3, x1y1, x1y3, y2, x1y2]
-
+    slot_table = jnp.where(member, places, -1.0)
+
+    segment, offsets = layout(seq_lengths[0], GROUP)
+    cosine, sine_table = rope_tables(offsets, HEAD)
+    wide_cosine = jnp.tile(cosine[:, 0, :], (1, 4))
+    wide_sine = jnp.tile(jnp.concatenate([-sine_table[:, 0, :], sine_table[:, 0, :]], axis=1), (1, 2))
+    start = jnp.broadcast_to((jnp.arange(GROUP, dtype=jnp.int32) - offsets)[:, None], (GROUP, 128))
+    (
+        pieces,
+        cot_all,
+        slots_all,
+        rows_all,
+        gates_all,
+        tokens_all,
+        normed_all,
+        slices_all,
+        output_all,
+        query,
+        key,
+        value,
+        log_total,
+        attended,
+        middle,
+        normed_two,
+        gate_values,
+    ) = first_phase(
+        slices,
+        w_output,
+        tokens,
+        cotangent,
+        slot_table,
+        by_peer(slot_table),
+        piece,
+        wide_cosine,
+        wide_sine,
+        start,
+    )
     slices_all = slices_all.reshape(DIM, SLICE)
     output_all = output_all.reshape(DIM, DIM)
-    qkv_all = slices_all[:, : QS + 2 * HEAD]
-    gains = slices_all[:, QS + 2 * HEAD : QS + 2 * HEAD + 2].astype(F32).T
+    qkv_all = slices_all[:, :ROUTER]
+    gains = slices_all[:, GAINS : GAINS + 2].astype(F32).T
     gain_one, gain_two = gains[0], gains[1]
-    router_all = slices_all[:, QS + 2 * HEAD + 2 : QS + 2 * HEAD + 2 + EXPERTS]
-
-    segment, offsets = layout(seq_lengths[0], GROUP)
-    cosine, sine_table = rope_tables(offsets, HEAD)
+    router_all = slices_all[:, ROUTER:GAINS]
+    inputs = tokens.astype(F32)
+    inputs_all = tokens_all.reshape(GROUP, DIM).astype(F32)
+    normed_all = normed_all.reshape(GROUP, DIM)
+    scale_all = rms_scale(inputs_all)
+    scale_two = rms_scale(middle)
+    attended = attended.transpose(1, 0, 2).reshape(TOK, DIM)
+    query = query.reshape(PEERS, REP, TOK, HEAD).transpose(0, 2, 1, 3).reshape(GROUP, REP, HEAD)
+    log_total = log_total[:, :, 0].reshape(PEERS, REP, TOK).transpose(1, 0, 2).reshape(REP, GROUP, 1)
     places = jnp.arange(GROUP, dtype=jnp.int32)
     allowed = (segment[:, None] == segment[None, :]) & (places[None, :] <= places[:, None])
-
-    inputs_all = tokens_all.reshape(GROUP, DIM).astype(F32)
-    scale_all = rms_scale(inputs_all)
-    normed_all = (inputs_all * scale_all * gain_one).astype(BF)
-    qkv = jnp.dot(normed_all, qkv_all, preferred_element_type=F32)
-    heads = rotate(
-        qkv[:, : QS + HEAD].reshape(GROUP, REP + 1, HEAD), cosine, sine_table
-    ).astype(BF)
-    query, key = heads[:, :REP], heads[:, REP]
-    value = qkv[:, QS + HEAD :].astype(BF)
     scores = jnp.einsum("qrh,kh->rqk", query, key, preferred_element_type=F32) * score_scale
-    scores = jnp.where(allowed, scores, masked_score)
-    highest = jnp.max(scores, axis=-1, keepdims=True)
-    terms = jnp.exp(scores - highest)
-    probs = terms / jnp.sum(terms, axis=-1, keepdims=True)
+    probs = jnp.exp(jnp.where(allowed, scores, masked_score) - log_total)
     probs_low = probs.astype(BF)
-    attended = jnp.einsum("rqk,kh->qrh", probs_low, value, preferred_element_type=F32).astype(BF)
-    (attended,) = exchange([attended.reshape(PEERS, TOK, QS)], ["exchange"], 3)
-    attended = attended.transpose(1, 0, 2).reshape(TOK, DIM)
-
-    inputs = tokens.astype(F32)
-    middle = inputs + jnp.dot(attended, output_all, preferred_element_type=F32)
-    scale_two = rms_scale(middle)
-    normed_two = (middle * scale_two * gain_two).astype(BF)
-    logits = lax.dot_general(
-        router_all, normed_two, (((0,), (1,)), ((), ())), preferred_element_type=F32
-    )
-    chosen = jnp.where(member, logits, masked_score)
-    weight = jnp.where(member, jnp.exp(chosen - jnp.max(chosen, axis=0, keepdims=True)), 0.0)
-    gate_values = weight / jnp.sum(weight, axis=0, keepdims=True)
-
-    late = [other_core(y2), other_core(x1y2)]
-    rows_all, gates_all, shared = exchange_and_share(
-        [normed_two, by_peer(gate_values)], ["gather", "exchange"], pieces[:6], 4
-    )
+
     out_part, back_part, inner_part, keep, given = run_experts(
-        rows_all, cot_all, slots_all, gates_all, pieces, shared, late
+        rows_all, cot_all, slots_all, gates_all, pieces
     )
     back_all, inner_all = exchange([back_part, inner_part], ["exchange", "exchange"], 5, 38)
 
@@ -848,10 +1170,10 @@
     small = jnp.concatenate(
         [
             grad_slices.astype(BF),
+            grad_router.astype(BF),
             grad_gain_one[:, None].astype(BF),
             grad_gain_two[:, None].astype(BF),
-            grad_router.astype(BF),
-            jnp.zeros((DIM, SLICE - QS - 2 * HEAD - 2 - EXPERTS), BF),
+            jnp.zeros((DIM, SLICE - GAINS - 2), BF),
         ],
         axis=1,
     )
@@ -869,18 +1191,17 @@
         ["exchange", "exchange"],
         8,
     )
-    own_sum = jnp.sum(small_own[:, :, QS + 2 * HEAD :], axis=0)
-    last = QS + 2 * HEAD
+    own_sum = jnp.sum(small_own[:, :, ROUTER:], axis=0)
     return (
         mixed.astype(BF),
         grad_tokens,
         small_own[:, :, :QS].transpose(1, 0, 2).reshape(12, DIM),
         small_own[:, :, QS : QS + HEAD].transpose(1, 0, 2).reshape(12, KV_HEADS * HEAD),
-        small_own[:, :, QS + HEAD : last].transpose(1, 0, 2).reshape(12, KV_HEADS * HEAD),
+        small_own[:, :, QS + HEAD : ROUTER].transpose(1, 0, 2).reshape(12, KV_HEADS * HEAD),
         jnp.sum(output_own, axis=0),
-        own_sum[:, 0],
-        own_sum[:, 1],
-        own_sum[:, 2 : 2 + EXPERTS],
+        own_sum[:, EXPERTS],
+        own_sum[:, EXPERTS + 1],
+        own_sum[:, :EXPERTS],
         expert_grads[:, :ROWS],
         expert_grads[:, ROWS : 2 * ROWS],
         expert_grads[:, 2 * ROWS :]

time: 599 us -> 468 us (0.78); the launches traced: 589 us -> 464 us
  waiting for transfers between devices: 92 us -> 32.6 us
  starting transfers between devices: 41.4 us -> 16.8 us
  Pallas kernels: 312 us -> 289 us
  matrix products: 46.4 us -> 35.4 us
    ppermute x16 -> x7, waiting for transfers between devices: 92 us -> 32.6 us  [shift(): return lax.ppermute(value, 'dp', pairs)]
    pallas_call x1, Pallas kernels: 76.5 us -> 49.3 us  [scatter_sum(): pl.pallas_call(kernel, out_shape=[jax.ShapeDtypeStruct(a.shape, a.dtype)...]
    pallas_call x2 -> x1, Pallas kernels: 114 us -> 141 us  [first_phase(): pl.pallas_call(first_kernel, out_shape=[o[0] for o in outs], in_specs=[hb...]
    pallas_call x4 -> x3, Pallas kernels: 86.3 us -> 64.7 us  [exchange(): pl.pallas_call(kernel, out_shape=shapes, in_specs=any_specs(n), out_specs...]
    ppermute x16 -> x7, starting transfers between devices: 31.6 us -> 11.9 us  [shift(): return lax.ppermute(value, 'dp', pairs)]
    dot_general x4 -> x1, matrix products: 11.8 us -> 1.77 us  [local(): jnp.einsum('qrh,kh->rqk', query, key, preferred_element_type=F32)]
    sub x1 -> x0, matrix products: 7.27 us -> none  [local(): terms = jnp.exp(scores - highest)]
  transfers between devices with their start and end apart: 18 -> 8, of which waited for: 6 -> 3; matrix products, arithmetic and copies ran while one was open for 12% -> 21% of each run, Pallas kernels for 26% -> 25%
where the time goes in v3:
time: 468 us; the launch traced here: 464 us
  Pallas kernels  289 us (62%)
  other arithmetic  53.4 us (11%)
  local copies, waits for them, and re-layouts  35.4 us (8%)
  matrix products  35.4 us (8%)
  waiting for transfers between devices  32.6 us (7%)
  starting transfers between devices  16.8 us (4%)
    pallas_call x1, Pallas kernels, first_phase(): pl.pallas_call(first_kernel, out_shape=[o[0] for o in outs], in_specs=[hb...  141 us
    pallas_call x3, Pallas kernels, exchange(): pl.pallas_call(kernel, out_shape=shapes, in_specs=any_specs(n), out_specs...  64.7 us
    pallas_call x1, Pallas kernels, scatter_sum(): pl.pallas_call(kernel, out_shape=[jax.ShapeDtypeStruct(a.shape, a.dtype)...  49.3 us
    pallas_call x1, Pallas kernels, run_experts(): pl.pallas_call(experts_kernel, out_shape=[jax.ShapeDtypeStruct((PEERS, TO...  34.3 us
    ppermute x7, waiting for transfers between devices, shift(): return lax.ppermute(value, 'dp', pairs)  32.6 us
    convert_element_type x2, other arithmetic, add(): return (a.astype(F32) + b.astype(F32)).astype(BF)  13.5 us
    ppermute x7, starting transfers between devices, shift(): return lax.ppermute(value, 'dp', pairs)  11.9 us
  transfers between devices with their start and end apart: 8, of which 3 were waited for; matrix products, arithmetic and copies ran while one was open for 21% of the time, Pallas kernels for 25%

profile of v3, /device:TPU:0, one launch (start us, length us, event | category | flops | bytes accessed | tf_op | source)
XLA Modules:
  0.0 464.1 jit_solution(12211584426975276715)
XLA Ops:
  8.3 140.7 %shard_map.229 = (bf16[16,5,288,512]{3,2,1,0:T(8,128)(2,1)}, bf16[8,128,1536]{2,1,0:T(8,128)(2,1)}, f32[8,8,128]{2,1,0:T(8,128)S(1)}, bf16[8,128,1536]{2,1,0:T(8...) custom-call(bf16[8,12,384]{2,1,0:T(8,128)(2,1)S(1)} %pad_maximum_fus, ...), custom_call_target="tpu_custom_call" | custom-call | flops 120000004096 | tf_op jit(solution)/shard_map/pallas_call | solution.py:604
  150.2 34.3 %shard_map.230 = (bf16[8,128,1536]{2,1,0:T(8,128)(2,1)}, bf16[8,128,1536]{2,1,0:T(8,128)(2,1)}, f32[8,8,128]{2,1,0:T(8,128)}, bf16[8,5,288,512]{3,2,1,0:T(8,128)(2,1)}, bf16[8,5,288,512]{3,2,1,0:T(8,128)(2,1)}) custom-call(bf16[8,128,1536]{2,1,0:T(8,128)(2,1)} %get-tuple-element.43.refs_0_, bf16[8,128,1536]{2,1,0:T(8,128)(2,1)} %get-tuple-element.44.refs_1_, ...), custom_call_target="tpu_custom_call" | custom-call | flops 20000000000 | bytes 60000000 | tf_op jit(solution)/shard_map/pallas_call | solution.py:893
  184.6 7.0 %fusion.20 = (bf16[5,288,512]{2,1,0:T(8,128)(2,1)}, bf16[5,288,512]{2,1,0:T(8,128)(2,1)}, bf16[5,288,512]{2,1,0:T(8,128)(2,1)}, bf16[5,288,512]{2,1,0:T(8,128)(2,1)}) fusion(bf16[8,5,288,512]{3,2,1,0:T(8,128)(2,1)} %get-tuple-element.71, bf16[8,5,288,512]{3,2,1,0:T(8,128)(2,1)} %get-tuple-element.70), kind=kLoop, calls=%fused_computation.45 | loop fusion | flops 11796480 | bytes 17694720 | tf_op jit(solution)/shard_map/convert_element_type | solution.py:953
  195.5 2.9 collective-permute-start.2
  198.4 39.2 %shard_map.231 = (bf16[8,128,1536]{2,1,0:T(8,128)(2,1)}, f32[8,8,128]{2,1,0:T(8,128)}) custom-call(bf16[8,128,1536]{2,1,0:T(8,128)(2,1)} %get-tuple-element.49.refs_0_, f32[8,8,128]{2,1,0:T(8,128)} %get-tuple-element.50.refs_1_), custom_call_target="tpu_custom_call" | custom-call | flops 38000001024 | tf_op jit(solution)/shard_map/pallas_call | solution.py:119
  238.4 3.3 convert_reduce_fusion.2
  248.3 4.0 convolution_convert_fusion.2
  253.5 11.7 %shard_map.232 = bf16[8,128,192]{2,1,0:T(8,128)(2,1)} custom-call(bf16[8,128,192]{2,1,0:T(8,128)(2,1)} %bitcast.187), custom_call_target="tpu_custom_call" | custom-call | flops 10000000000 | tf_op jit(solution)/shard_map/pallas_call | solution.py:119
  265.2 4.9 %all-to-all-start = ((bf16[8,128,1536]{2,1,0:T(8,128)(2,1)}), bf16[8,128,1536]{2,1,0:T(8,128)(2,1)}, u32[]{:S(2)}, u32[]{:S(2)}) async-start(bf16[8,128,1536]{2,1,0:T(8,128)(2,1)} %get-tuple-element.56), calls=%async_computation | async-start | bytes 6291456 | tf_op jit(solution)/shard_map/all_to_all | solution.py:949
  279.3 6.6 %fusion = (f32[3,1024]{1,0:T(4,128)S(1)}, f32[1024,1024,3]{1,0,2:T(8,128)}) fusion(f32[1024,1024,3]{1,0,2:T(8,128)S(1)} %fusion.45, f32[3,1024]{1,0:T(4,128)S(1)} %bitcast.184, pred[1024,1024]{0,1:T(8,128)(4,1)S(1)} %fusion.11, bf16[1024,3,64]{0,2,1:T(8,128)(2,1)S(1)} %reshape.366, bf16[1024,64]{1,0:T(8,128)(2,1)S(1)} %get-tuple-element.61), kind=kOutput, calls=%fused_computation.2 | convolution fusion | flops 418378752 | bytes 26763264 | tf_op jit(solution)/shard_map/qrh,kh->rqk/dot_general | solution.py:1148
  285.8 6.9 %fusion.2 = bf16[3,1024,1024]{1,2,0:T(8,128)(2,1)S(1)} fusion(f32[1024,1024,3]{1,0,2:T(8,128)} %get-tuple-element.109, f32[1024,1024,3]{1,0,2:T(8,128)S(1)} %fusion.45, f32[3,1024]{1,0:T(4,128)S(1)} %get-tuple-element.108, f32[3,1024]{1,0:T(4,128)S(1)} %bitcast.185, pred[1024,1024]{0,1:T(8,128)(4,1)S(1)} %fusion.11), kind=kLoop, calls=%fused_computation.4 | loop fusion | flops 18874368 | bytes 32530432 | tf_op jit(solution)/shard_map/convert_element_type | solution.py:1151
  297.6 4.3 fusion.34
  302.2 3.5 convolution_convert_fusion
  308.5 3.1 convolution_convert_fusion.1
  315.8 5.2 %fusion.7 = (bf16[1536]{0:T(1024)(128)(2,1)S(1)}, bf16[1024,1536]{1,0:T(8,128)(2,1)}) fusion(f32[1024]{0:T(1024)S(1)} %get-tuple-element.102, bf16[8,128,1536]{2,1,0:T(8,128)(2,1)S(1)} %copy-done.11, bf16[1536,384]{1,0:T(8,128)(2,1)} %bitcast.192, bf16[1024,64]{0,1:T(8,128)(2,1)S(1)} %copy-done.26, bf16[1024,256]{0,1:T(8,128)(2,1)S(1)} %bitcast.189), kind=kOutput, calls=%fused_computation.12 | convolution fusion | flops 1015806464 | bytes 8133632 | tf_op jit(solution)/shard_map/dot_general | solution.py:1166
  323.3 2.8 concatenate.40.refs_1_
  330.3 49.3 %shard_map.233 = (bf16[8,128,1536]{2,1,0:T(8,128)(2,1)S(1)}, f32[96,384]{1,0:T(8,128)S(1)}, f32[96,1536]{1,0:T(8,128)S(1)}) custom-call(bf16[8,128,1536]{2,1,0:T(8,128)(2,1)S(1)} %bitcast.170, bf16[16,96,384]{2,1,0:T(8,128)(2,1)S(1)} %concatenate.40.refs_1_, bf16[16,96,1536]{2,1,0:T(8,128)(2,1)S(1)} %bitcast.168), custom_call_target="tpu_custom_call" | custom-call | flops 44999999488 | tf_op jit(solution)/shard_map/pallas_call | solution.py:724
  380.2 6.5 %fusion.15 = (bf16[5,288,512]{2,1,0:T(8,128)(2,1)}, bf16[5,288,512]{2,1,0:T(8,128)(2,1)}) fusion(bf16[5,288,512]{2,1,0:T(8,128)(2,1)} %collective-permute-done, bf16[8,5,288,512]{3,2,1,0:T(8,128)(2,1)} %get-tuple-element.71, bf16[8,5,288,512]{3,2,1,0:T(8,128)(2,1)} %get-tuple-element.70, bf16[5,288,512]{2,1,0:T(8,128)(2,1)} %collective-permute-done.4), kind=kLoop, calls=%fused_computation.27 | loop fusion | flops 11796480 | bytes 11796480 | tf_op jit(solution)/shard_map/convert_element_type | solution.py:953
  389.3 13.8 %shard_map.234 = (f32[8,12,384]{2,1,0:T(8,128)}, f32[8,12,1536]{2,1,0:T(8,128)}) custom-call(f32[8,12,384]{2,1,0:T(8,128)} %reshape.372.refs_0_, f32[8,12,1536]{2,1,0:T(8,128)} %reshape.373.refs_1_), custom_call_target="tpu_custom_call" | custom-call | flops 10000000000 | tf_op jit(solution)/shard_map/pallas_call | solution.py:119
  406.7 12.1 %collective-permute-done.5 = bf16[5,288,512]{2,1,0:T(8,128)(2,1)} collective-permute-done((bf16[5,288,512]{2,1,0:T(8,128)(2,1)}, bf16[5,288,512]{2,1,0:T(8,128)(2,1)}, u32[]{:S(2)}, u32[]{:S(2)}) %collective-permute-start.5) | collective-permute-done | bytes 1474592 | tf_op jit(solution)/shard_map/ppermute | solution.py:929
  418.8 4.7 %fusion.14 = bf16[5,288,512]{2,1,0:T(8,128)(2,1)} fusion(bf16[5,288,512]{2,1,0:T(8,128)(2,1)} %collective-permute-done.5, bf16[5,288,512]{2,1,0:T(8,128)(2,1)} %collective-permute-done.3, bf16[8,5,288,512]{3,2,1,0:T(8,128)(2,1)} %get-tuple-element.71, bf16[8,5,288,512]{3,2,1,0:T(8,128)(2,1)} %get-tuple-element.70), kind=kLoop, calls=%fused_computation.25 | loop fusion | flops 7372800 | bytes 7372800 | tf_op jit(solution)/shard_map/convert_element_type | solution.py:1112
  435.3 4.2 collective-permute-done.1
  439.4 16.4 %collective-permute-done.6 = bf16[5,288,512]{2,1,0:T(8,128)(2,1)} collective-permute-done((bf16[5,288,512]{2,1,0:T(8,128)(2,1)}, bf16[5,288,512]{2,1,0:T(8,128)(2,1)}, u32[]{:S(2)}, u32[]{:S(2)}) %collective-permute-start.6) | collective-permute-done | bytes 1474592 | tf_op jit(solution)/shard_map/ppermute | solution.py:929
  455.8 4.1 fusion.17
  (152 shorter events, 71.3 us)
Async XLA Ops:
  0.6 3.4 copy-start.20
  0.7 3.5 copy-start.21
  0.7 3.6 copy-start.18
  0.7 3.7 copy-start.24
  0.7 3.8 copy-start.25
  0.7 3.9 copy-start.22
  0.7 4.2 copy-start.16
  4.1 3.8 copy-start.23
  4.9 3.4 copy-start.1
  191.6 188.7 %collective-permute-start = (bf16[5,288,512]{2,1,0:T(8,128)(2,1)}, bf16[5,288,512]{2,1,0:T(8,128)(2,1)}, u32[]{:S(2)}, u32[]{:S(2)}) collective-permute-start(bf16[5,288,512]{2,1,0:T(8,128)(2,1)} %get-tuple-element.82), channel_id=1, source_target_pairs={{0,16},{8,24},{16,32},{24,40},{32,48},{40,56},{48,0},{56,8},{64,80... | collective-permute-start | bytes 4423688 | tf_op jit(solution)/shard_map/ppermute | solution.py:929
  193.5 186.8 %collective-permute-start.4 = (bf16[5,288,512]{2,1,0:T(8,128)(2,1)}, bf16[5,288,512]{2,1,0:T(8,128)(2,1)}, u32[]{:S(2)}, u32[]{:S(2)}) collective-permute-start(bf16[5,288,512]{2,1,0:T(8,128)(2,1)} %get-tuple-element.83), channel_id=1, source_target_pairs={{0,48},{8,56},{16,0},{24,8},{32,16},{40,24},{48,32},{56,40},{64,11... | collective-permute-start | bytes 4423688 | tf_op jit(solution)/shard_map/ppermute | solution.py:929
  195.1 211.6 %collective-permute-start.3 = (bf16[5,288,512]{2,1,0:T(8,128)(2,1)}, bf16[5,288,512]{2,1,0:T(8,128)(2,1)}, u32[]{:S(2)}, u32[]{:S(2)}) collective-permute-start(bf16[5,288,512]{2,1,0:T(8,128)(2,1)} %get-tuple-element.84), channel_id=1, source_target_pairs={{0,16},{8,24},{16,32},{24,40},{32,48},{40,56},{48,0},{56,8},{64,80... | collective-permute-start | bytes 4423688 | tf_op jit(solution)/shard_map/ppermute | solution.py:929
  195.5 239.8 %collective-permute-start.2 = (bf16[5,288,512]{2,1,0:T(8,128)(2,1)}, bf16[5,288,512]{2,1,0:T(8,128)(2,1)}, u32[]{:S(2)}, u32[]{:S(2)}) collective-permute-start(bf16[5,288,512]{2,1,0:T(8,128)(2,1)} %get-tuple-element.85), channel_id=1, source_target_pairs={{0,48},{8,56},{16,0},{24,8},{32,16},{40,24},{48,32},{56,40},{64,11... | collective-permute-start | bytes 4423688 | tf_op jit(solution)/shard_map/ppermute | solution.py:929
  237.5 4.2 copy-start.7
  265.2 166.8 %all-to-all-start = ((bf16[8,128,1536]{2,1,0:T(8,128)(2,1)}), bf16[8,128,1536]{2,1,0:T(8,128)(2,1)}, u32[]{:S(2)}, u32[]{:S(2)}) async-start(bf16[8,128,1536]{2,1,0:T(8,128)(2,1)} %get-tuple-element.56), calls=%async_computation | async-start | bytes 6291456 | tf_op jit(solution)/shard_map/all_to_all | solution.py:949
  270.1 6.7 %copy-start.19 = (s32[1024]{0:T(1024)S(1)}, s32[1024]{0:T(1024)}, u32[]{:S(2)}) copy-start(s32[1024]{0:T(1024)} %get-tuple-element.78) | copy-start | bytes 12292
  297.6 4.6 copy-start.9
  302.1 4.6 copy-start.13
  302.1 4.6 copy-start.15
  386.7 32.1 %collective-permute-start.5 = (bf16[5,288,512]{2,1,0:T(8,128)(2,1)}, bf16[5,288,512]{2,1,0:T(8,128)(2,1)}, u32[]{:S(2)}, u32[]{:S(2)}) collective-permute-start(bf16[5,288,512]{2,1,0:T(8,128)(2,1)} %get-tuple-element.81), channel_id=1, source_target_pairs={{0,48},{8,56},{16,0},{24,8},{32,16},{40,24},{48,32},{56,40},{64,11... | collective-permute-start | bytes 4423688 | tf_op jit(solution)/shard_map/ppermute | solution.py:929
  404.1 25.9 %copy-start.17 = (f32[12,64]{1,0:T(8,128)}, f32[12,64]{1,0:T(8,128)S(1)}, u32[]{:S(2)}) copy-start(f32[12,64]{1,0:T(8,128)S(1)} %get-tuple-element.93) | copy-start | bytes 9220
  405.1 25.7 %copy-start.10 = (f32[128,1536]{1,0:T(8,128)S(1)}, f32[128,1536]{1,0:T(8,128)}, u32[]{:S(2)}) copy-start(f32[128,1536]{1,0:T(8,128)} %copy-done.8) | copy-start | bytes 2359300
  405.1 34.4 %collective-permute-start.1 = (bf16[5,288,512]{2,1,0:T(8,128)(2,1)}, bf16[5,288,512]{2,1,0:T(8,128)(2,1)}, u32[]{:S(2)}, u32[]{:S(2)}) collective-permute-start(bf16[5,288,512]{2,1,0:T(8,128)(2,1)} %get-tuple-element.80), channel_id=1, source_target_pairs={{0,16},{8,24},{16,32},{24,40},{32,48},{40,56},{48,0},{56,8},{64,80... | collective-permute-start | bytes 4423688 | tf_op jit(solution)/shard_map/ppermute | solution.py:929
  423.5 32.3 %collective-permute-start.6 = (bf16[5,288,512]{2,1,0:T(8,128)(2,1)}, bf16[5,288,512]{2,1,0:T(8,128)(2,1)}, u32[]{:S(2)}, u32[]{:S(2)}) collective-permute-start(bf16[5,288,512]{2,1,0:T(8,128)(2,1)} %fusion.14), channel_id=1, source_target_pairs={{0,64},{8,72},{16,80},{24,88},{32,96},{40,104},{48,112},{56,120},{... | collective-permute-start | bytes 4423688 | tf_op jit(solution)/shard_map/ppermute | solution.py:929
  (11 other events, 21.5 us)

commit v4 on v3

--- a/solution.py
+++ b/solution.py
@@ -96,39 +96,6 @@
 
 def lasting(us):
     return pl.CostEstimate(flops=us * 1_000_000_000, bytes_accessed=0, transcendentals=0)
-
-
-def exchange(arrays, modes, cid, us=10):
-    n = len(arrays)
-
-    def kernel(*refs):
-        ins, outs = refs[:n], refs[n : 2 * n]
-        send, recv, local = refs[2 * n :]
-        _, peers = expert_peers()
-        signal_all(peers, [])
-        copies = expert_copies(ins, outs, modes, send, recv) + own_copies(ins, outs, modes, local)
-        for c in copies:
-            c.start()
-        for c in copies:
-            c.wait()
-
-    shapes = [
-        jax.ShapeDtypeStruct(((PEERS,) + a.shape) if m == "gather" else a.shape, a.dtype)
-        for a, m in zip(arrays, modes)
-    ]
-    return pl.pallas_call(
-        kernel,
-        out_shape=shapes,
-        in_specs=any_specs(n),
-        out_specs=any_specs(n),
-        scratch_shapes=[
-            pltpu.SemaphoreType.DMA((n, 7)),
-            pltpu.SemaphoreType.DMA((n, 7)),
-            pltpu.SemaphoreType.DMA((n,)),
-        ],
-        compiler_params=pltpu.CompilerParams(collective_id=cid, has_side_effects=True),
-        cost_estimate=lasting(us),
-    )(*arrays)
 
 
 class Gather:
@@ -636,122 +603,618 @@
     )(slices, output, tokens, cot, member, slot_send, piece, cosine, sine, start)
 
 
-def scatter_sum(arrays, dense, cid):
-    n, m = len(arrays), len(dense)
-    shapes = [(d.shape[1], d.shape[2]) for d in dense]
-
-    def kernel(*refs):
-        ins, dins = refs[:n], refs[n : n + m]
-        outs, totals = refs[n + m : 2 * n + m], refs[2 * n + m : 2 * (n + m)]
-        refs = refs[2 * (n + m) :]
-        mine, theirs, along, last = refs[:m], refs[m : 2 * m], refs[2 * m : 3 * m], refs[3 * m : 4 * m]
-        send, recv, local, lsem, csend, crecv, ysend, yrecv, xsend, xrecv = refs[4 * m :]
+def dot(a, b, contract):
+    return lax.dot_general(a, b, ((contract[0], contract[1]), ((), ())), preferred_element_type=F32)
+
+
+class Reduce:
+    def __init__(self, src, own, landed, send, recv):
+        self.src, self.own, self.landed = src, own, landed
+        self.send, self.recv = send, recv
+        me = lax.axis_index("expert")
+        z, x = me // 2, me % 2
+        self.place = lambda dz, dx: (z + dz) % 4 * 2 + (x + dx) % 2
+        self.targets = {"up": self.place(1, 0), "down": self.place(3, 0), "x": self.place(0, 1)}
+        self.started = []
+
+    def copy(self, k, src, where):
+        c = pltpu.make_async_remote_copy(
+            src_ref=src,
+            dst_ref=self.landed.at[k],
+            send_sem=self.send.at[k],
+            recv_sem=self.recv.at[k],
+            device_id={"expert": self.targets[where]},
+            device_id_type=MESH,
+        )
+        c.start()
+        self.started.append(c)
+
+    def got(self, k):
+        pltpu.make_async_remote_copy(
+            src_ref=self.landed.at[k],
+            dst_ref=self.landed.at[k],
+            send_sem=self.send.at[k],
+            recv_sem=self.recv.at[k],
+            device_id={"expert": self.targets["x"]},
+            device_id_type=MESH,
+        ).wait_recv()
+        return self.landed[k].astype(F32)
+
+    def begin(self):
+        self.copy(0, self.src.at[self.place(2, 1)], "up")
+        self.copy(1, self.src.at[self.place(2, 0)], "down")
+        self.copy(3, self.src.at[self.place(3, 1)], "down")
+
+    def relay(self):
+        self.landed[0] = (self.own(1, 1) + self.got(0)).astype(BF)
+        self.copy(2, self.landed.at[0], "up")
+        self.copy(4, self.src.at[self.place(1, 0)], "up")
+        self.landed[1] = (self.own(3, 0) + self.got(1)).astype(BF)
+        self.copy(5, self.landed.at[1], "down")
+
+    def cross(self):
+        self.landed[2] = (self.own(0, 1) + self.got(2) + self.got(3)).astype(BF)
+        self.copy(6, self.landed.at[2], "x")
+
+    def total(self):
+        return self.own(0, 0) + self.got(4) + self.got(5) + self.got(6)
+
+    def finish(self):
+        for c in self.started:
+            c.wait_send()
+
+
+class DenseSum:
+    def __init__(self, grads, theirs, landed, send, recv):
+        self.grads, self.theirs, self.landed, self.send, self.recv = grads, theirs, landed, send, recv
         x, y, core = dp_place()
-        to_core, to_x = dp_index(x, y, core + 1), dp_index(x + 1, y, core)
-        to_y = [dp_index(x, y + r, core) for r in (1, 2, 3)]
-        _, peers = expert_peers()
-        signal_all(peers, [to_core, to_x] + to_y)
-        modes = ["exchange"] * n
-        order = [(r, s) for r in (1, 0) for s in (2, 1, 3, 0)]
-        started, loads, shares = [], {}, {}
-
-        def remote(src, dst, s, r, target):
-            c = pltpu.make_async_remote_copy(
-                src_ref=src,
-                dst_ref=dst,
-                send_sem=s,
-                recv_sem=r,
-                device_id={"dp": target},
-                device_id_type=MESH,
+        self.targets = {
+            "x": dp_index(x + 1, y, core),
+            "up": dp_index(x, y + 1, core),
+            "down": dp_index(x, y + 3, core),
+            "core": dp_index(x, y, core + 1),
+        }
+        self.slots = [dp_index(x + rx, y + ry, core) for rx, ry in SLOTS]
+        self.others = [dp_index(x + rx, y + ry, core + 1) for rx, ry in SLOTS]
+        self.started = []
+
+    def descriptor(self, k, src, dst, where):
+        return pltpu.make_async_remote_copy(
+            src_ref=src,
+            dst_ref=dst,
+            send_sem=self.send.at[k],
+            recv_sem=self.recv.at[k],
+            device_id={"dp": self.targets[where]},
+            device_id_type=MESH,
+        )
+
+    def copy(self, k, src, dst, where):
+        c = self.descriptor(k, src, dst, where)
+        c.start()
+        self.started.append(c)
+
+    def begin(self):
+        for k in (6, 7, 4, 5, 2, 3, 1, 0):
+            self.copy(8 + k, self.grads.at[self.others[k]], self.theirs.at[k], "core")
+
+    def got(self, k):
+        self.descriptor(k, self.landed.at[k], self.landed.at[k], "x").wait_recv()
+        return self.landed[k].astype(F32)
+
+    def both(self, k):
+        self.descriptor(8 + k, self.theirs.at[k], self.theirs.at[k], "core").wait_recv()
+        return self.grads[self.slots[k]].astype(F32) + self.theirs[k].astype(F32)
+
+    def put(self, k, value, j, where):
+        self.grads[self.slots[k]] = value.astype(BF)
+        self.copy(j, self.grads.at[self.slots[k]], self.landed.at[j], where)
+
+    def first(self):
+        self.put(6, self.both(6), 0, "up")
+        self.put(7, self.both(7), 1, "down")
+        self.put(4, self.both(4), 2, "up")
+
+    def second(self):
+        self.put(5, self.both(5) + self.got(1), 3, "down")
+        self.put(2, self.both(2) + self.got(0), 4, "up")
+        self.put(3, self.both(3), 5, "down")
+
+    def third(self):
+        self.put(1, self.both(1) + self.got(2) + self.got(3), 6, "x")
+
+    def total(self):
+        return self.both(0) + self.got(4) + self.got(5) + self.got(6)
+
+    def finish(self):
+        for c in self.started:
+            c.wait_send()
+
+
+class ExpertSum:
+    def __init__(self, keep, given, near, far, stage, sends, far_sends, ends, s_near, r_near, s_far, r_far, l_sem):
+        self.keep, self.given, self.near, self.far, self.stage = keep, given, near, far, stage
+        self.sends, self.far_sends, self.ends = sends, far_sends, ends
+        self.s_near, self.r_near, self.s_far, self.r_far, self.l_sem = s_near, r_near, s_far, r_far, l_sem
+        x, y, core = dp_place()
+        self.targets = {
+            "x": dp_index(x + 1, y, core),
+            "up": dp_index(x, y + 1, core),
+            "down": dp_index(x, y + 3, core),
+        }
+        self.started = []
+
+    def descriptor(self, src, dst, send, recv, where):
+        return pltpu.make_async_remote_copy(
+            src_ref=src,
+            dst_ref=dst,
+            send_sem=send,
+            recv_sem=recv,
+            device_id={"dp": self.targets[where]},
+            device_id_type=MESH,
+        )
+
+    def add(self, refs, out, count):
+        def load(e):
+            return [
+                pltpu.make_async_copy(r.at[e], self.stage.at[e % 2, i], self.l_sem.at[e % 2, i])
+                for i, r in enumerate(refs)
+            ]
+
+        for c in load(0):
+            c.start()
+        for e in range(count):
+            if e + 1 < count:
+                for c in load(e + 1):
+                    c.start()
+            for c in load(e):
+                c.wait()
+            acc = self.stage[e % 2, 0].astype(F32)
+            for i in range(1, len(refs)):
+                acc = acc + self.stage[e % 2, i].astype(F32)
+            out[e] = acc.astype(out.dtype)
+
+    def parts(self, k, first, count):
+        span = pl.ds(first, count)
+        return [self.keep.at[k, span], self.given.at[k, span]]
+
+    def near_send(self, k, j, where, more=()):
+        for i in more:
+            self.near_got(i)
+        out = self.sends.at[j]
+        self.add(self.parts(k, 0, 3) + [self.near.at[i] for i in more], out, 3)
+        c = self.descriptor(out, self.near.at[j], self.s_near.at[j], self.r_near.at[j], where)
+        c.start()
+        self.started.append(c)
+
+    def near_got(self, j):
+        self.descriptor(
+            self.near.at[j], self.near.at[j], self.s_near.at[j], self.r_near.at[j], "x"
+        ).wait_recv()
+
+    def far_send(self, k, j, where, which=(0, 1), more=()):
+        for i in which:
+            for m in more:
+                if m < 4 or m == 4 + i:
+                    self.far_got(m, i)
+            out = self.far_sends.at[j, pl.ds(i, 1)]
+            self.add(
+                self.parts(k, 3 + i, 1)
+                + [self.far.at[m, pl.ds(i, 1)] for m in more if m < 4 or m == 4 + i],
+                out,
+                1,
+            )
+            c = self.descriptor(
+                out,
+                self.far.at[j, pl.ds(i, 1)],
+                self.s_far.at[j, i],
+                self.r_far.at[j, i],
+                where,
             )
             c.start()
-            started.append(c)
-            return c
-
-        for i in range(m):
-            for r, s in order:
-                k = 4 * r + s
-                shares[i, k] = remote(
-                    dins[i].at[dp_index(x + r, y + s, core + 1)],
-                    theirs[i].at[k],
-                    csend.at[i, k],
-                    crecv.at[i, k],
-                    to_core,
-                )
-                loads[i, k] = pltpu.make_async_copy(
-                    dins[i].at[dp_index(x + r, y + s, core)], mine[i].at[k], lsem.at[i, k]
-                )
-                loads[i, k].start()
-        copies = expert_copies(ins, outs, modes, send, recv) + own_copies(ins, outs, modes, local)
-        for c in copies:
+            self.started.append(c)
+
+    def far_got(self, j, i):
+        ref = self.far.at[j, pl.ds(i, 1)]
+        self.descriptor(ref, ref, self.s_far.at[j, i], self.r_far.at[j, i], "x").wait_recv()
+
+    def near_end(self):
+        for j in (4, 5, 6):
+            self.near_got(j)
+        self.add(
+            self.parts(0, 0, 3) + [self.near.at[j] for j in (4, 5, 6)],
+            self.ends,
+            3,
+        )
+
+    def far_end(self):
+        for j in (0, 6, 7):
+            for i in range(2):
+                self.far_got(j, i)
+        self.add(
+            self.parts(0, 3, 2) + [self.far.at[j] for j in (0, 6, 7)], self.ends, 2
+        )
+
+    def finish(self):
+        for c in self.started:
+            c.wait_send()
+
+
+def last_kernel(*refs):
+    (
+        back_part,
+        inner_part,
+        out_part,
+        keep,
+        given,
+        tokens_all,
+        normed_all,
+        small_hbm,
+        dense_hbm,
+        tokens,
+        cot,
+        gates_ref,
+        middle_ref,
+        normed_two_ref,
+        attended_ref,
+        query_ref,
+        key_ref,
+        value_ref,
+        log_ref,
+        cos_ref,
+        sin_ref,
+        start_ref,
+    ) = refs[:22]
+    mixed_ref, grad_tokens_ref, expert_ref, small_own, output_own, near, far = refs[22:29]
+    (
+        inner_in,
+        gates_grad,
+        logits_grad,
+        small,
+        dense,
+        grad_small,
+        normed,
+        token_rows,
+        grad_normed,
+        att_send,
+        att_in,
+        grad_query,
+        grad_key,
+        grad_value,
+        grad_qkv,
+        gain_sum,
+        grad_middle_ref,
+        z_own,
+        z_landed,
+        y_landed,
+        stage,
+        sends,
+        far_sends,
+        ends,
+        small_theirs,
+        small_landed,
+        dense_theirs,
+        dense_landed,
+        small_cut,
+        dense_cut,
+        dense_in,
+        s_direct,
+        r_direct,
+        s_reduce,
+        r_reduce,
+        s_dense,
+        r_dense,
+        s_near,
+        r_near,
+        s_far,
+        r_far,
+        l_sem,
+        l_add,
+    ) = refs[29:]
+    _, peers = expert_peers()
+    x, y, core = dp_place()
+    me = lax.axis_index("expert")
+    signal_all(
+        peers,
+        [
+            dp_index(x + 1, y, core),
+            dp_index(x, y + 1, core),
+            dp_index(x, y + 3, core),
+            dp_index(x, y, core + 1),
+        ],
+    )
+
+    def direct(i, src, out, mode):
+        part = expert_copies(
+            [src], [out], [mode], s_direct.at[pl.ds(i, 1)], r_direct.at[pl.ds(i, 1)]
+        ) + own_copies([src], [out], [mode], l_sem.at[pl.ds(i, 1)])
+        for c in part:
             c.start()
-        moves = {}
-        for r, s in order:
-            k = 4 * r + s
-            for i in range(m):
-                loads[i, k].wait()
-                shares[i, k].wait_recv()
-                mine[i][k] = (mine[i][k].astype(F32) + theirs[i][k].astype(F32)).astype(BF)
-                if s > 0:
-                    moves[i, r, s] = remote(
-                        mine[i].at[k],
-                        along[i].at[3 * r + s - 1],
-                        ysend.at[i, 3 * r + s - 1],
-                        yrecv.at[i, 3 * r + s - 1],
-                        to_y[s - 1],
-                    )
-        crossings = []
-        for i in range(m):
-            acc = mine[i][4].astype(F32)
-            for s in (2, 1, 3):
-                moves[i, 1, s].wait_recv()
-                acc = acc + along[i][3 + s - 1].astype(F32)
-            mine[i][4] = acc.astype(BF)
-            crossings.append(remote(mine[i].at[4], last[i], xsend.at[i], xrecv.at[i], to_x))
-        for i in range(m):
-            acc = mine[i][0].astype(F32)
-            for s in (2, 1, 3):
-                moves[i, 0, s].wait_recv()
-                acc = acc + along[i][s - 1].astype(F32)
-            crossings[i].wait_recv()
-            totals[i][...] = acc + last[i][...].astype(F32)
-        for c in started:
-            c.wait_send()
-        for c in copies:
+        return part
+
+    def settle(part):
+        for c in part:
             c.wait()
 
-    vmem = pl.BlockSpec(memory_space=pltpu.VMEM)
+    def load(src, dst, i):
+        c = pltpu.make_async_copy(src, dst, l_sem.at[i])
+        c.start()
+        return c
+
+    OWN = ((1, 1), (3, 0), (0, 1), (0, 0))
+
+    def own_blocks(reduce, src, base):
+        return [
+            load(src.at[reduce.place(*d)], z_own.at[i], base + i) for i, d in enumerate(OWN)
+        ]
+
+    def from_own(dz, dx):
+        return z_own[OWN.index((dz, dx))].astype(F32)
+
+    back = Reduce(back_part, from_own, z_landed, s_reduce.at[0], r_reduce.at[0])
+    back.begin()
+    loads = own_blocks(back, back_part, 8)
+    inner = direct(0, inner_part, inner_in, "exchange")
+    loads_small = load(small_hbm, small, 4)
+    loads_dense = load(dense_hbm, dense, 5)
+    loads_normed = load(normed_all, normed, 6)
+    experts = ExpertSum(
+        keep, given, near, far, stage, sends, far_sends, ends, s_near, r_near, s_far, r_far, l_add
+    )
+    experts.near_send(6, 0, "up")
+    experts.near_send(7, 1, "down")
+    settle(loads)
+    back.relay()
+    experts.far_send(7, 3, "x")
+    experts.far_send(4, 1, "x")
+    experts.near_send(4, 2, "up")
+    back.cross()
+    experts.far_send(6, 4, "up", (0,), (3,))
+    experts.far_send(6, 5, "down", (1,), (3,))
+    experts.near_send(5, 3, "down", (1,))
+    experts.near_send(2, 4, "up", (0,))
+    settle(inner)
+    settle([loads_small, loads_dense])
+
+    for j in range(PEERS):
+        gates_grad[LOCAL * j : LOCAL * (j + 1), :] = inner_in[j, 0:LOCAL, :]
+    gates = gates_ref[...]
+    grad_gates = gates_grad[...]
+    logits_grad[...] = jnp.zeros_like(logits_grad)
+    logits_grad[ROUTER - 256 : GAINS - 256, :] = gates * (
+        grad_gates - jnp.sum(gates * grad_gates, axis=0, keepdims=True)
+    )
+    pick = (
+        lax.broadcasted_iota(jnp.int32, (8, SLICE), 1)
+        == lax.broadcasted_iota(jnp.int32, (8, SLICE), 0) + GAINS
+    )
+    gains = dot(pick.astype(F32).astype(BF), small[...].reshape(DIM, SLICE), ((1,), (1,)))
+    gain_one, gain_two = gains[0:1], gains[1:2]
+    grad_logits = logits_grad[...].astype(BF)
+    router = small[:, :, 256:SLICE].reshape(DIM, SLICE - 256)
+    grad = back.total() + dot(grad_logits, router, ((0,), (1,)))
+    middle = middle_ref[...]
+    scale_two = lax.rsqrt(jnp.mean(middle * middle, axis=-1, keepdims=True) + epsilon)
+    gain_sum[0] = jnp.sum((grad * middle * scale_two).reshape(TOK // 8, 8, DIM), axis=0)
+    grad_middle = cot[...].astype(F32) + norm_back(middle, scale_two, gain_two, grad)
+    grad_middle_ref[...] = grad_middle
+    grad_branch = grad_middle.astype(BF)
+    for j in range(PEERS):
+        att_send[j] = dot(
+            grad_branch, dense[2 * j : 2 * j + 2].reshape(QS, DIM), ((1,), (1,))
+        ).astype(BF)
+    back.finish()
+    exchanged = direct(1, att_send, att_in, "exchange")
+    experts.far_send(5, 2, "x")
+    for j in range(PEERS):
+        dense[2 * j : 2 * j + 2] = (
+            dot(attended_ref[j], grad_branch, ((0,), (0,))).astype(BF).reshape(2, ROWS, DIM)
+        )
+    experts.near_send(3, 5, "down")
+    settle(exchanged)
+    out = Reduce(out_part, from_own, y_landed, s_reduce.at[1], r_reduce.at[1])
+    out.begin()
+    loads = own_blocks(out, out_part, 8)
+    sums = [
+        DenseSum(dense, dense_theirs, dense_landed, s_dense.at[0], r_dense.at[0]),
+        DenseSum(grad_small, small_theirs, small_landed, s_dense.at[1], r_dense.at[1]),
+    ]
+    sums[0].begin()
+    experts.far_send(1, 0, "x")
+
+    grad_key[...] = jnp.zeros_like(grad_key)
+    grad_value[...] = jnp.zeros_like(grad_value)
+
+    def attend(width, i, _):
+        queries = query_ref[i]
+        incoming = att_in[i]
+        incoming = jnp.concatenate(
+            [incoming[:, h * HEAD : (h + 1) * HEAD] for h in range(REP)], axis=0
+        )
+        scores = dot(queries, key_ref[0:width, :], ((1,), (1,))) * HEAD ** (-0.5)
+        keys = lax.broadcasted_iota(jnp.int32, (TOK, width), 1)
+        rows = lax.broadcasted_iota(jnp.int32, (TOK, width), 0) + i * TOK
+        begins = start_ref[pl.ds(pl.multiple_of(i * TOK, TOK), TOK), :][:, :1]
+        allowed = (keys <= rows) & (keys >= begins)
+        scores = jnp.where(allowed[None], scores.reshape(REP, TOK, width), masked_score)
+        probs = jnp.exp(scores.reshape(REP * TOK, width) - log_ref[i][:, :1])
+        grad_probs = dot(incoming, value_ref[0:width, :], ((1,), (1,)))
+        inner_sum = jnp.sum(probs * grad_probs, axis=-1, keepdims=True)
+        grad_scores = (probs * (grad_probs - inner_sum)).astype(BF)
+        grad_query[i] = dot(grad_scores, key_ref[0:width, :], ((1,), (0,))) * HEAD ** (-0.5)
+        grad_key[0:width, :] += dot(grad_scores, queries, ((0,), (0,))) * HEAD ** (-0.5)
+        grad_value[0:width, :] += dot(probs.astype(BF), incoming, ((0,), (0,)))
+        return _
+
+    lax.fori_loop(0, 4, functools.partial(attend, GROUP // 2), 0)
+    settle(loads)
+    out.relay()
+    experts.far_send(2, 6, "up", (0, 1), (1, 4))
+    experts.far_send(3, 7, "down", (0, 1), (2, 5))
+    experts.near_send(1, 6, "x", (2, 3))
+    lax.fori_loop(4, 8, functools.partial(attend, GROUP), 0)
+    out.cross()
+
+    settle([loads_normed])
+    gain_sum[1] = jnp.zeros((8, DIM), F32)
+
+    def project(i, _):
+        span = pl.ds(pl.multiple_of(i * 2 * TOK, 2 * TOK), 2 * TOK)
+        rows = load(tokens_all.at[pl.ds(2 * i, 2)], token_rows, 7)
+        cosine, sine = cos_ref[span, :], sin_ref[span, :]
+        lane = lax.broadcasted_iota(jnp.int32, (2 * TOK, 128), 1)
+        heads = [
+            jnp.concatenate(
+                [grad_query[2 * i + b, h * TOK : (h + 1) * TOK, :] for b in range(2)], axis=0
+            )
+            for h in range(REP)
+        ]
+        turned = []
+        for pair in ((heads[0], heads[1]), (heads[2], grad_key[span, :])):
+            v = jnp.concatenate(pair, axis=1)
+            other = jnp.where(lane % HEAD < HEAD // 2, pltpu.roll(v, 96, 1), pltpu.roll(v, 32, 1))
+            turned.append((v * cosine - other * sine).astype(BF))
+        tail = jnp.concatenate(
+            [grad_value[span, :], jnp.zeros((2 * TOK, SLICE - ROUTER), F32)], axis=1
+        ).astype(BF)
+        low = jnp.concatenate(turned + [tail], axis=1)
+        grad_qkv[span, :] = low
+        grad = dot(low, small[...].reshape(DIM, SLICE), ((1,), (1,)))
+        grad_normed[pl.ds(2 * i, 2)] = grad.astype(BF).reshape(2, TOK, DIM)
+        rows.wait()
+        values = token_rows[...].reshape(2 * TOK, DIM).astype(F32)
+        scale = lax.rsqrt(jnp.mean(values * values, axis=-1, keepdims=True) + epsilon)
+        gain_sum[1] += jnp.sum((grad * values * scale).reshape(2 * TOK // 8, 8, DIM), axis=0)
+        return _
+
+    lax.fori_loop(0, 4, project, 0)
+
+    def from_grad(dz, dx):
+        return grad_normed[first.place(dz, dx)].astype(F32)
+
+    first = Reduce(grad_normed, from_grad, z_landed, s_reduce.at[2], r_reduce.at[2])
+    first.begin()
+    sums[0].first()
+
+    lanes = lax.broadcasted_iota(jnp.int32, (8, 128), 1)
+    marks = [(lanes == GAINS - 256 + i).astype(F32).astype(BF) for i in range(2)]
+    first.relay()
+    for c in range(4):
+        span = slice(c * 384, (c + 1) * 384)
+        part = dot(normed[:, :, span].reshape(GROUP, 384), grad_qkv[...], ((0,), (0,)))
+        extra = dot(normed_two_ref[:, span], grad_logits, ((0,), (1,)))
+        for i in range(2):
+            value = gain_sum[1 - i, :, span]
+            high = value.astype(BF)
+            rest = (value - high.astype(F32)).astype(BF)
+            extra = extra + dot(high, marks[i], ((0,), (0,))) + dot(rest, marks[i], ((0,), (0,)))
+        grad_small[4 * c : 4 * c + 4, :, 0:256] = (
+            part[:, 0:256].astype(BF).reshape(4, ROWS, 256)
+        )
+        grad_small[4 * c : 4 * c + 4, :, 256:SLICE] = (
+            (part[:, 256:SLICE] + extra).astype(BF).reshape(4, ROWS, SLICE - 256)
+        )
+    sums[1].begin()
+    sums[0].second()
+    mixed_ref[...] = (middle_ref[...] + out.total()).astype(BF)
+    sums[1].first()
+    first.cross()
+    sums[1].second()
+    experts.far_end()
+    saved = load(ends.at[pl.ds(0, 2)], expert_ref.at[pl.ds(3, 2)], 4)
+    sums[0].third()
+    sums[1].third()
+    values = tokens[...].astype(F32)
+    scale = lax.rsqrt(jnp.mean(values * values, axis=-1, keepdims=True) + epsilon)
+    grad_tokens_ref[...] = grad_middle_ref[...] + norm_back(values, scale, gain_one, first.total())
+    total = sums[0].total()
+    for j in range(PEERS):
+        dense_cut[j] = total[12 * j : 12 * (j + 1)]
+    total = sums[1].total()
+    for j in range(PEERS):
+        small_cut[j] = total[12 * j : 12 * (j + 1)]
+    cuts = direct(2, dense_cut, dense_in, "exchange") + direct(3, small_cut, small_own, "exchange")
+    saved.wait()
+    experts.near_end()
+    saved = load(ends, expert_ref.at[pl.ds(0, 3)], 4)
+    settle(cuts)
+    acc = dense_in[0]
+    for j in range(1, PEERS):
+        acc = acc + dense_in[j]
+    output_own[...] = acc
+    for part in (out, first, sums[0], sums[1], experts):
+        part.finish()
+    saved.wait()
+
+
+def last_phase(*args):
+    hbm, vmem = pl.BlockSpec(memory_space=pl.ANY), pl.BlockSpec(memory_space=pltpu.VMEM)
+    shape, dma = jax.ShapeDtypeStruct, pltpu.SemaphoreType.DMA
+    blocks = (PEERS, TOK, DIM)
+    piece = (3 * ROWS, FFE)
+    outs = [
+        (shape((TOK, DIM), BF), vmem),
+        (shape((TOK, DIM), F32), vmem),
+        (shape((LOCAL,) + piece, F32), hbm),
+        (shape((PEERS, 12, SLICE), F32), hbm),
+        (shape((12, DIM), F32), vmem),
+        (shape((7, 3) + piece, BF), hbm),
+        (shape((8, 2) + piece, BF), hbm),
+    ]
     return pl.pallas_call(
-        kernel,
-        out_shape=[jax.ShapeDtypeStruct(a.shape, a.dtype) for a in arrays]
-        + [jax.ShapeDtypeStruct(d, F32) for d in shapes],
-        in_specs=any_specs(n + m),
-        out_specs=any_specs(n) + [vmem] * m,
-        scratch_shapes=[pltpu.VMEM((8,) + d, BF) for d in shapes]
-        + [pltpu.VMEM((8,) + d, BF) for d in shapes]
-        + [pltpu.VMEM((6,) + d, BF) for d in shapes]
-        + [pltpu.VMEM(d, BF) for d in shapes]
-        + [
-            pltpu.SemaphoreType.DMA((n, 7)),
-            pltpu.SemaphoreType.DMA((n, 7)),
-            pltpu.SemaphoreType.DMA((n,)),
-            pltpu.SemaphoreType.DMA((m, 8)),
-            pltpu.SemaphoreType.DMA((m, 8)),
-            pltpu.SemaphoreType.DMA((m, 8)),
-            pltpu.SemaphoreType.DMA((m, 6)),
-            pltpu.SemaphoreType.DMA((m, 6)),
-            pltpu.SemaphoreType.DMA((m,)),
-            pltpu.SemaphoreType.DMA((m,)),
+        last_kernel,
+        out_shape=[o[0] for o in outs],
+        in_specs=[hbm] * 9 + [vmem] * 13,
+        out_specs=[o[1] for o in outs],
+        scratch_shapes=[
+            pltpu.VMEM((PEERS, 8, TOK), F32),
+            pltpu.VMEM((EXPERTS, TOK), F32),
+            pltpu.VMEM((SLICE - 256, TOK), F32),
+            pltpu.VMEM((DP, ROWS, SLICE), BF),
+            pltpu.VMEM((DP, ROWS, DIM), BF),
+            pltpu.VMEM((DP, ROWS, SLICE), BF),
+            pltpu.VMEM(blocks, BF),
+            pltpu.VMEM((2, TOK, DIM), BF),
+            pltpu.VMEM(blocks, BF),
+            pltpu.VMEM((PEERS, TOK, QS), BF),
+            pltpu.VMEM((PEERS, TOK, QS), BF),
+            pltpu.VMEM((PEERS, REP * TOK, HEAD), F32),
+            pltpu.VMEM((GROUP, HEAD), F32),
+            pltpu.VMEM((GROUP, HEAD), F32),
+            pltpu.VMEM((GROUP, SLICE), BF),
+            pltpu.VMEM((2, 8, DIM), F32),
+            pltpu.VMEM((TOK, DIM), F32),
+            pltpu.VMEM((4, TOK, DIM), BF),
+            pltpu.VMEM((7, TOK, DIM), BF),
+            pltpu.VMEM((7, TOK, DIM), BF),
+            pltpu.VMEM((2, 5) + piece, BF),
+            pltpu.VMEM((7, 3) + piece, BF),
+            pltpu.VMEM((8, 2) + piece, BF),
+            pltpu.VMEM((3,) + piece, F32),
+            pltpu.VMEM((8, ROWS, SLICE), BF),
+            pltpu.VMEM((7, ROWS, SLICE), BF),
+            pltpu.VMEM((8, ROWS, DIM), BF),
+            pltpu.VMEM((7, ROWS, DIM), BF),
+            pltpu.VMEM((PEERS, 12, SLICE), F32),
+            pltpu.VMEM((PEERS, 12, DIM), F32),
+            pltpu.VMEM((PEERS, 12, DIM), F32),
+            dma((4, 7)),
+            dma((4, 7)),
+            dma((3, 7)),
+            dma((3, 7)),
+            dma((2, 16)),
+            dma((2, 16)),
+            dma((7,)),
+            dma((7,)),
+            dma((8, 2)),
+            dma((8, 2)),
+            dma((12,)),
+            dma((2, 5)),
         ],
         compiler_params=pltpu.CompilerParams(
-            collective_id=cid, has_side_effects=True, vmem_limit_bytes=40 << 20
+            collective_id=3, has_side_effects=True, vmem_limit_bytes=62 << 20
         ),
-        cost_estimate=lasting(45),
-    )(*arrays, *dense)
-
-
-def dot(a, b, contract):
-    return lax.dot_general(a, b, ((contract[0], contract[1]), ((), ())), preferred_element_type=F32)
+        cost_estimate=lasting(120),
+    )(*args)
 
 
 def experts_kernel(*refs):
@@ -921,55 +1384,11 @@
     )(rows, cot, slots, gates, pieces)
 
 
-def shift(value, move):
-    pairs = []
-    for d in range(DP):
-        x, y, core = move(d // 8, d // 2 % 4, d % 2)
-        pairs.append((d, (x % 2 * 4 + y % 4) * 2 + core % 2))
-    return lax.ppermute(value, "dp", pairs)
-
-
-def up(value):
-    return shift(value, lambda x, y, c: (x, y + 1, c))
-
-
-def down(value):
-    return shift(value, lambda x, y, c: (x, y + 3, c))
-
-
-def across(value):
-    return shift(value, lambda x, y, c: (x + 1, y, c))
-
-
-def other_core(value):
-    return shift(value, lambda x, y, c: (x, y, c + 1))
-
-
-def to_peers(blocks):
-    return lax.all_to_all(blocks, "expert", split_axis=0, concat_axis=0, tiled=True)
-
-
-def add(a, b):
-    return (a.astype(F32) + b.astype(F32)).astype(BF)
-
-
-def rms_scale(values):
-    return lax.rsqrt(jnp.mean(values * values, axis=-1, keepdims=True) + epsilon)
-
-
 def rope_tables(offsets, head_width):
     exponent = jnp.arange(head_width // 2, dtype=jnp.float32) * (2.0 / head_width)
     frequency = jnp.exp(-exponent * math.log(rope_base))
     phase_angles = offsets.astype(jnp.float32)[:, None] * frequency[None, :]
     return (jnp.cos(phase_angles)[:, None, :], jnp.sin(phase_angles)[:, None, :])
-
-
-def rotate(values, cosine, sine_table):
-    half = values.shape[-1] // 2
-    first, second = values[..., :half], values[..., half:]
-    return jnp.concatenate(
-        [first * cosine - second * sine_table, second * cosine + first * sine_table], axis=-1
-    )
 
 
 def layout(lengths, group_count):
@@ -1012,7 +1431,6 @@
     w_up,
     w_down,
 ):
-    score_scale = HEAD ** (-0.5)
     down_piece = w_down.reshape(LOCAL, 32, 3, FFE).transpose(0, 2, 1, 3).reshape(LOCAL, ROWS, FFE)
     piece = jnp.concatenate([w_gate, w_up, down_piece], axis=1)
 
@@ -1078,127 +1496,41 @@
         wide_sine,
         start,
     )
-    slices_all = slices_all.reshape(DIM, SLICE)
-    output_all = output_all.reshape(DIM, DIM)
-    qkv_all = slices_all[:, :ROUTER]
-    gains = slices_all[:, GAINS : GAINS + 2].astype(F32).T
-    gain_one, gain_two = gains[0], gains[1]
-    router_all = slices_all[:, ROUTER:GAINS]
-    inputs = tokens.astype(F32)
-    inputs_all = tokens_all.reshape(GROUP, DIM).astype(F32)
-    normed_all = normed_all.reshape(GROUP, DIM)
-    scale_all = rms_scale(inputs_all)
-    scale_two = rms_scale(middle)
-    attended = attended.transpose(1, 0, 2).reshape(TOK, DIM)
-    query = query.reshape(PEERS, REP, TOK, HEAD).transpose(0, 2, 1, 3).reshape(GROUP, REP, HEAD)
-    log_total = log_total[:, :, 0].reshape(PEERS, REP, TOK).transpose(1, 0, 2).reshape(REP, GROUP, 1)
-    places = jnp.arange(GROUP, dtype=jnp.int32)
-    allowed = (segment[:, None] == segment[None, :]) & (places[None, :] <= places[:, None])
-    scores = jnp.einsum("qrh,kh->rqk", query, key, preferred_element_type=F32) * score_scale
-    probs = jnp.exp(jnp.where(allowed, scores, masked_score) - log_total)
-    probs_low = probs.astype(BF)
-
     out_part, back_part, inner_part, keep, given = run_experts(
         rows_all, cot_all, slots_all, gates_all, pieces
     )
-    back_all, inner_all = exchange([back_part, inner_part], ["exchange", "exchange"], 5, 38)
-
-    sums = {s: add(keep[k], given[k]) for k, s in enumerate(SLOTS)}
-    up_two, down_two = up(sums[(0, 2)]), down(sums[(1, 2)])
-    far = (
-        sums[(1, 0)].astype(F32)
-        + up(sums[(1, 1)]).astype(F32)
-        + down(add(sums[(1, 3)], down_two)).astype(F32)
-    ).astype(BF)
-    near = (
-        sums[(0, 0)].astype(F32)
-        + up(add(sums[(0, 1)], up_two)).astype(F32)
-        + down(sums[(0, 3)]).astype(F32)
-    )
-    expert_grads = near + across(far).astype(F32)
-
-    grad_normed_two = jnp.sum(back_all.astype(F32), axis=0)
-    grad_gates = inner_all[:, :LOCAL, :].reshape(EXPERTS, TOK)
-    grad_chosen = gate_values * (
-        grad_gates - jnp.sum(gate_values * grad_gates, axis=0, keepdims=True)
-    )
-    grad_logits = grad_chosen.astype(BF)
-    grad_out = cotangent.astype(F32)
-    grad_router = lax.dot_general(
-        normed_two, grad_logits, (((0,), (1,)), ((), ())), preferred_element_type=F32
-    )
-    grad_normed_two = grad_normed_two + lax.dot_general(
-        grad_logits, router_all, (((0,), (1,)), ((), ())), preferred_element_type=F32
-    )
-    grad_gain_two = jnp.sum(grad_normed_two * middle * scale_two, axis=0)
-    grad_middle = grad_out + norm_back(middle, scale_two, gain_two, grad_normed_two)
-    grad_branch = grad_middle.astype(BF)
-    grad_attended = lax.dot_general(
-        grad_branch, output_all, (((1,), (1,)), ((), ())), preferred_element_type=F32
-    ).astype(BF)
-    grad_attended = grad_attended.reshape(TOK, PEERS, QS).transpose(1, 0, 2)
-    (grad_attended,) = exchange([grad_attended], ["exchange"], 6)
-    out_part, _ = lax.optimization_barrier((out_part, grad_attended))
-    out_all = to_peers(out_part)
-    grad_attended = grad_attended.reshape(GROUP, REP, HEAD)
-    grad_output = lax.dot_general(
-        attended, grad_branch, (((0,), (0,)), ((), ())), preferred_element_type=F32
-    )
-
-    grad_probs = jnp.einsum("qrh,kh->rqk", grad_attended, value, preferred_element_type=F32)
-    grad_scores = (
-        probs * (grad_probs - jnp.sum(probs * grad_probs, axis=-1, keepdims=True))
-    ).astype(BF)
-    grad_query = (
-        jnp.einsum("rqk,kh->qrh", grad_scores, key, preferred_element_type=F32) * score_scale
-    )
-    grad_key = (
-        jnp.einsum("rqk,qrh->kh", grad_scores, query, preferred_element_type=F32) * score_scale
-    )
-    grad_value = jnp.einsum("rqk,qrh->kh", probs_low, grad_attended, preferred_element_type=F32)
-    grad_heads = rotate(
-        jnp.concatenate([grad_query, grad_key[:, None, :]], axis=1), cosine, -sine_table
-    ).reshape(GROUP, QS + HEAD)
-    grad_qkv = jnp.concatenate([grad_heads, grad_value], axis=1).astype(BF)
-    grad_slices = lax.dot_general(
-        normed_all, grad_qkv, (((0,), (0,)), ((), ())), preferred_element_type=F32
-    )
-    grad_normed = lax.dot_general(
-        grad_qkv, qkv_all, (((1,), (1,)), ((), ())), preferred_element_type=F32
-    )
-    grad_gain_one = jnp.sum(grad_normed * inputs_all * scale_all, axis=0)
-    small = jnp.concatenate(
-        [
-            grad_slices.astype(BF),
-            grad_router.astype(BF),
-            grad_gain_one[:, None].astype(BF),
-            grad_gain_two[:, None].astype(BF),
-            jnp.zeros((DIM, SLICE - GAINS - 2), BF),
-        ],
-        axis=1,
-    )
-    normed_back, small_rows, output_rows = scatter_sum(
-        [grad_normed.astype(BF).reshape(PEERS, TOK, DIM)],
-        [small.reshape(DP, ROWS, SLICE), grad_output.astype(BF).reshape(DP, ROWS, DIM)],
-        7,
-    )
-    mixed = middle + jnp.sum(out_all.astype(F32), axis=0)
-    grad_tokens = grad_middle + norm_back(
-        inputs, scale_all_own(scale_all), gain_one, jnp.sum(normed_back.astype(F32), axis=0)
-    )
-    small_own, output_own = exchange(
-        [small_rows.reshape(PEERS, 12, SLICE), output_rows.reshape(PEERS, 12, DIM)],
-        ["exchange", "exchange"],
-        8,
+    mixed, grad_tokens, expert_grads, small_own, output_own, _, _ = last_phase(
+        back_part,
+        inner_part,
+        out_part,
+        keep,
+        given,
+        tokens_all,
+        normed_all,
+        slices_all,
+        output_all,
+        tokens,
+        cotangent,
+        gate_values,
+        middle,
+        normed_two,
+        attended,
+        query,
+        key,
+        value,
+        log_total,
+        wide_cosine,
+        wide_sine,
+        start,
     )
     own_sum = jnp.sum(small_own[:, :, ROUTER:], axis=0)
     return (
-        mixed.astype(BF),
+        mixed,
         grad_tokens,
         small_own[:, :, :QS].transpose(1, 0, 2).reshape(12, DIM),
         small_own[:, :, QS : QS + HEAD].transpose(1, 0, 2).reshape(12, KV_HEADS * HEAD),
         small_own[:, :, QS + HEAD : ROUTER].transpose(1, 0, 2).reshape(12, KV_HEADS * HEAD),
-        jnp.sum(output_own, axis=0),
+        output_own,
         own_sum[:, EXPERTS],
         own_sum[:, EXPERTS + 1],
         own_sum[:, :EXPERTS],
@@ -1211,10 +1543,6 @@
     )
 
 
-def scale_all_own(scale_all):
-    return lax.dynamic_slice_in_dim(scale_all, lax.axis_index("expert") * TOK, TOK)
-
-
 def solution(mesh):
     both = P(("dp", "expert"), None)
     line = P(("dp", "expert"))

time: 468 us -> 357 us (0.76)
  other arithmetic: 53.4 us -> 7.26 us
  Pallas kernels: 289 us -> 325 us
  matrix products: 35.4 us -> 0.14 us
  waiting for transfers between devices: 32.6 us -> 0 us
  starting transfers between devices: 16.8 us -> 0 us
  local copies, waits for them, and re-layouts: 35.4 us -> 21.7 us
    pallas_call x4 -> x1, Pallas kernels: 114 us -> 150 us  [last_phase(): pl.pallas_call(last_kernel, out_shape=[o[0] for o in outs], in_specs=[hbm...]
    dot_general x11 -> x0, matrix products: 35.3 us -> none  [the longest x1 6.58 us: local(): jnp.einsum('qrh,kh->rqk', grad_attended, value, preferred_element_type=F32)]
    ppermute x7 -> x0, waiting for transfers between devices: 32.6 us -> none  [shift(): return lax.ppermute(value, 'dp', pairs)]
    convert_element_type x6 -> x0, other arithmetic: 25.9 us -> none  [the longest x2 13.5 us: add(): return (a.astype(F32) + b.astype(F32)).astype(BF)]
    ppermute x7 -> x0, starting transfers between devices: 11.9 us -> none  [shift(): return lax.ppermute(value, 'dp', pairs)]
    reduce_sum x9 -> x1, other arithmetic: 11.7 us -> 0.08 us  [layout(): offsets = places - jnp.sum(member * starts[None, :], axis=1)]
    add x3 -> x0, other arithmetic: 5.62 us -> none  [the longest x1 4.14 us: local(): expert_grads = near + across(far).astype(F32)]
    all_to_all x1 -> x0, starting transfers between devices: 4.93 us -> none  [to_peers(): lax.all_to_all(blocks, 'expert', split_axis=0, concat_axis=0, tiled=True)]
  transfers between devices with their start and end apart: 8 -> 0, of which waited for: 3 -> 0; matrix products, arithmetic and copies ran while one was open for 21% -> 0% of each run, Pallas kernels for 25% -> 0%
where the time goes in v4:
time: 357 us; the launch traced here: 355 us
  Pallas kernels  325 us (91%)
  local copies, waits for them, and re-layouts  21.7 us (6%)
  other arithmetic  7.26 us (2%)
    pallas_call x1, Pallas kernels, last_phase(): pl.pallas_call(last_kernel, out_shape=[o[0] for o in outs], in_specs=[hbm...  150 us
    pallas_call x1, Pallas kernels, first_phase(): pl.pallas_call(first_kernel, out_shape=[o[0] for o in outs], in_specs=[hb...  141 us
    pallas_call x1, Pallas kernels, run_experts(): pl.pallas_call(experts_kernel, out_shape=[jax.ShapeDtypeStruct((PEERS, TO...  34.2 us

profile of v4, /device:TPU:0, one launch (start us, length us, event | category | flops | bytes accessed | tf_op | source)
XLA Modules:
  0.0 355.1 jit_solution(5999933228825129646)
XLA Ops:
  0.6 0.8 reduce-window.4
  2.3 0.7 copy.49
  3.1 0.8 copy.50
  3.8 0.8 maximum_maximum_fusion
  4.6 0.7 fusion
  5.5 0.8 reshape.126
  6.3 0.8 reshape.127
  7.2 0.9 reshape.125
  9.6 2.2 reshape.129
  11.8 2.5 pad_maximum_fusion.refs_6_
  14.3 140.7 %shard_map.229 = (bf16[16,5,288,512]{3,2,1,0:T(8,128)(2,1)}, bf16[8,128,1536]{2,1,0:T(8,128)(2,1)}, f32[8,8,128]{2,1,0:T(8,128)S(1)}, bf16[8,128,1536]{2,1,0:T(8...) custom-call(bf16[8,12,384]{2,1,0:T(8,128)(2,1)S(1)} %pad_maximum_fus, ...), custom_call_target="tpu_custom_call" | custom-call | flops 120000004096 | tf_op jit(solution)/shard_map/pallas_call | solution.py:571
  155.7 0.8 copy-done.8
  156.5 0.7 copy-done.9
  157.8 34.2 %shard_map.230 = (bf16[8,128,1536]{2,1,0:T(8,128)(2,1)}, bf16[8,128,1536]{2,1,0:T(8,128)(2,1)}, f32[8,8,128]{2,1,0:T(8,128)}, bf16[8,5,288,512]{3,2,1,0:T(8,128)(2,1)}, bf16[8,5,288,512]{3,2,1,0:T(8,128)(2,1)}) custom-call(bf16[8,128,1536]{2,1,0:T(8,128)(2,1)} %get-tuple-element.39.refs_0_, bf16[8,128,1536]{2,1,0:T(8,128)(2,1)} %get-tuple-element.40.refs_1_, ...), custom_call_target="tpu_custom_call" | custom-call | flops 20000000000 | bytes 60000000 | tf_op jit(solution)/shard_map/pallas_call | solution.py:1356
  192.1 150.2 %shard_map.231 = (bf16[128,1536]{1,0:T(8,128)(2,1)}, f32[128,1536]{1,0:T(8,128)}, f32[5,288,512]{2,1,0:T(8,128)}, f32[8,12,384]{2,1,0:T(8,128)}, f32[12,1536]{1,...) custom-call(bf16[8,128,1536]{2,1,0:T(8,128)(2,1)} %get-tuple-element.44.refs_0_, ...), custom_call_target="tpu_custom_call" | custom-call | flops 120000004096 | tf_op jit(solution)/shard_map/pallas_call | solution.py:1163
  342.3 0.9 slice_bitcast_fusion
  343.2 1.0 slice_reduce_fusion
  344.3 0.7 reshape.133
  345.0 0.7 reshape.135
  345.7 0.7 slice_reduce_fusion.1
  347.1 3.3 fusion.5
  351.2 1.7 reshape.137
  352.9 0.7 copy.69
  353.6 0.9 copy.70
  (59 shorter events, 5.8 us)
Async XLA Ops:
  9.0 5.3 %copy-start = (f32[1024,128]{1,0:T(8,128)}, f32[1024,128]{1,0:T(8,128)S(1)}, u32[]{:S(2)}) copy-start(f32[1024,128]{1,0:T(8,128)S(1)} %copy.53.refs_8_.refs_20_) | copy-start | bytes 1572868
  9.2 5.1 %copy-start.1 = (s32[1024,128]{1,0:T(8,128)}, s32[1024,128]{1,0:T(8,128)S(1)}, u32[]{:S(2)}) copy-start(s32[1024,128]{1,0:T(8,128)S(1)} %broadcast_in_dim.19.refs_9_.refs_21_) | copy-start | bytes 1572868
  9.3 5.0 %copy-start.3 = (bf16[128,1536]{1,0:T(8,128)(2,1)S(1)}, bf16[128,1536]{1,0:T(8,128)(2,1)}, u32[]{:S(2)}) copy-start(bf16[128,1536]{1,0:T(8,128)(2,1)} %refs_9_.1) | copy-start | bytes 1179652
  9.3 5.0 %copy-start.4 = (bf16[128,1536]{1,0:T(8,128)(2,1)S(1)}, bf16[128,1536]{1,0:T(8,128)(2,1)}, u32[]{:S(2)}) copy-start(bf16[128,1536]{1,0:T(8,128)(2,1)} %refs_10_.1) | copy-start | bytes 1179652
  9.3 5.0 %copy-start.5 = (bf16[12,1536]{1,0:T(8,128)(2,1)S(1)}, bf16[12,1536]{1,0:T(8,128)(2,1)}, u32[]{:S(2)}) copy-start(bf16[12,1536]{1,0:T(8,128)(2,1)} %refs_1_.1) | copy-start | bytes 110596
  9.5 145.5 %copy-start.2 = (f32[1024,128]{1,0:T(8,128)}, f32[1024,128]{1,0:T(8,128)S(1)}, u32[]{:S(2)}) copy-start(f32[1024,128]{1,0:T(8,128)S(1)} %copy.52.refs_7_.refs_19_) | copy-start | bytes 1572868
  155.1 0.6 copy-start.7
  155.7 0.8 copy-start.8
  156.5 0.7 copy-start.9
  157.2 0.6 copy-start.6
  157.2 34.8 %copy-start.10 = (bf16[1024,64]{1,0:T(8,128)(2,1)}, bf16[1024,64]{1,0:T(8,128)(2,1)S(1)}, u32[]{:S(2)}) copy-start(bf16[1024,64]{1,0:T(8,128)(2,1)S(1)} %get-tuple-element.58.refs_16_) | copy-start | bytes 393220
  157.2 34.8 %copy-start.11 = (bf16[1024,64]{1,0:T(8,128)(2,1)}, bf16[1024,64]{1,0:T(8,128)(2,1)S(1)}, u32[]{:S(2)}) copy-start(bf16[1024,64]{1,0:T(8,128)(2,1)S(1)} %get-tuple-element.59.refs_17_) | copy-start | bytes 393220
  157.2 34.9 %copy-start.12 = (f32[40,128]{1,0:T(8,128)}, f32[40,128]{1,0:T(8,128)S(1)}, u32[]{:S(2)}) copy-start(f32[40,128]{1,0:T(8,128)S(1)} %get-tuple-element.53.refs_11_) | copy-start | bytes 61444
  344.2 6.3 %copy-start.16 = (f32[12,64]{1,0:T(8,128)}, f32[12,64]{1,0:T(8,128)S(1)}, u32[]{:S(2)}) copy-start(f32[12,64]{1,0:T(8,128)S(1)} %get-tuple-element.71) | copy-start | bytes 9220
  350.5 2.4 copy-start.14
  350.5 3.1 copy-start.13
  350.5 4.0 %copy-start.15 = (f32[12,1536]{1,0:T(8,128)S(1)}, f32[12,1536]{1,0:T(8,128)}, u32[]{:S(2)}) copy-start(f32[12,1536]{1,0:T(8,128)} %get-tuple-element.98) | copy-start | bytes 221188

commit v5 on v4

--- a/solution.py
+++ b/solution.py
@@ -63,7 +63,7 @@
 
 
 def any_specs(count):
-    return [pl.BlockSpec(memory_space=pl.ANY)] * count
+    return [pl.BlockSpec(memory_space=pltpu.HBM)] * count
 
 
 def expert_copies(ins, outs, modes, send, recv):
@@ -107,7 +107,6 @@
         def place(dz, dx):
             return (z + dz) % 4 * 2 + (x + dx) % 2
 
-        self.me, self.across, self.up, self.down = me, place(0, 1), place(1, 0), place(3, 0)
         self.slots = [
             place(0, 1),
             place(3, 0),
@@ -117,10 +116,13 @@
             place(2, 0),
             place(2, 1),
         ]
+        self.me = me
+        x, up, down = place(0, 1), place(1, 0), place(3, 0)
+        self.moves = ((None, x), (None, up), (None, down), (0, up), (0, down), (1, up), (4, down))
         self.started = []
 
-    def copy(self, k, src, slot, target):
-        c = pltpu.make_async_remote_copy(
+    def descriptor(self, k, src, slot, target):
+        return pltpu.make_async_remote_copy(
             src_ref=src,
             dst_ref=self.out.at[slot],
             send_sem=self.send.at[k],
@@ -128,180 +130,132 @@
             device_id={"expert": target},
             device_id_type=MESH,
         )
+
+    def begin(self):
+        self.own = pltpu.make_async_copy(self.src, self.out.at[self.me], self.local)
+        self.own.start()
+
+    def issue(self, k):
+        source, target = self.moves[k]
+        slot = self.me if source is None else self.slots[source]
+        src = self.src if source is None else self.out.at[slot]
+        c = self.descriptor(k, src, slot, target)
         c.start()
         self.started.append(c)
 
     def arrive(self, k):
-        pltpu.make_async_remote_copy(
-            src_ref=self.src,
-            dst_ref=self.out.at[self.slots[k]],
-            send_sem=self.send.at[k],
-            recv_sem=self.recv.at[k],
-            device_id={"expert": self.up},
-            device_id_type=MESH,
-        ).wait_recv()
-
-    def begin(self):
-        self.copy(0, self.src, self.me, self.across)
-        self.copy(1, self.src, self.me, self.up)
-        self.copy(2, self.src, self.me, self.down)
-        self.own = pltpu.make_async_copy(self.src, self.out.at[self.me], self.local)
-        self.own.start()
-
-    def first(self):
-        self.arrive(0)
-        self.copy(3, self.out.at[self.slots[0]], self.slots[0], self.up)
-        self.copy(4, self.out.at[self.slots[0]], self.slots[0], self.down)
-
-    def second(self):
-        self.arrive(1)
-        self.copy(5, self.out.at[self.slots[1]], self.slots[1], self.up)
-
-    def third(self):
-        self.arrive(4)
-        self.copy(6, self.out.at[self.slots[4]], self.slots[4], self.down)
-
-    def finish(self):
-        for k in (2, 3, 5, 6):
-            self.arrive(k)
-        for c in self.started:
-            c.wait_send()
-        self.own.wait()
-
-
-class Dense:
-    def __init__(self, rows, out, send, recv, local):
-        self.rows, self.out, self.send, self.recv, self.local = rows, out, send, recv, local
+        self.descriptor(k, self.src, self.slots[k], self.moves[0][1]).wait_recv()
+
+
+class Line:
+    def __init__(self, src, view, moves, send, recv):
+        self.src, self.view, self.send, self.recv = src, view, send, recv
         x, y, core = dp_place()
-        self.x, self.y, self.core = x, y, core
-        self.mine = dp_index(x, y, core)
-        self.to_x, self.to_up = dp_index(x + 1, y, core), dp_index(x, y + 1, core)
-        self.to_down, self.to_core = dp_index(x, y + 3, core), dp_index(x, y, core + 1)
-        self.slots = [dp_index(x + rx, y + ry, core) for rx, ry in SLOTS]
-        self.started = []
-
-    def descriptor(self, k, src, slot, target):
-        return pltpu.make_async_remote_copy(
-            src_ref=src,
-            dst_ref=self.out.at[slot],
-            send_sem=self.send.at[k],
-            recv_sem=self.recv.at[k],
-            device_id={"dp": target},
-            device_id_type=MESH,
-        )
-
-    def copy(self, k, slot, target, src=None):
-        c = self.descriptor(k, self.out.at[slot] if src is None else src, slot, target)
-        c.start()
-        self.started.append(c)
-
-    def arrive(self, k, slot):
-        self.descriptor(k, self.out.at[slot], slot, self.to_x).wait_recv()
-
-    def share(self, k):
-        self.copy(8 + k, self.slots[k], self.to_core)
-
-    def begin(self):
-        self.copy(1, self.mine, self.to_x, self.rows)
-        self.copy(3, self.mine, self.to_up, self.rows)
-        self.copy(2, self.mine, self.to_down, self.rows)
-        self.copy(8, self.mine, self.to_core, self.rows)
-        self.own = pltpu.make_async_copy(self.rows, self.out.at[self.mine], self.local)
-        self.own.start()
-
-    def first(self):
-        self.arrive(1, self.slots[1])
-        self.copy(5, self.slots[1], self.to_up)
-        self.copy(4, self.slots[1], self.to_down)
-        self.share(1)
-        self.arrive(3, self.slots[3])
-        self.copy(6, self.slots[3], self.to_up)
-        self.share(3)
-        self.arrive(2, self.slots[2])
-        self.share(2)
-
-    def second(self):
-        self.arrive(4, self.slots[4])
-        self.copy(7, self.slots[4], self.to_down)
-        self.share(4)
-        self.arrive(5, self.slots[5])
-        self.share(5)
-
-    def third(self):
-        for k in (6, 7):
-            self.arrive(k, self.slots[k])
-            self.share(k)
-
-    def finish(self):
-        for k, (rx, ry) in enumerate(SLOTS):
-            self.arrive(8 + k, dp_index(self.x + rx, self.y + ry, self.core + 1))
-        for c in self.started:
-            c.wait_send()
-        self.own.wait()
-
-
-class Pieces:
-    parts = ((0, 3), (3, 1), (4, 1))
-
-    def __init__(self, piece, out, send, recv, local):
-        self.piece, self.out, self.send, self.recv, self.local = piece, out, send, recv, local
-        x, y, core = dp_place()
-        self.x, self.y, self.core = x, y, core
-        self.mine = dp_index(x, y, core)
         self.targets = {
             "x": dp_index(x + 1, y, core),
             "up": dp_index(x, y + 1, core),
             "down": dp_index(x, y + 3, core),
             "core": dp_index(x, y, core + 1),
         }
-        self.slots = [dp_index(x + rx, y + ry, core) for rx, ry in SLOTS]
+        self.moves = dict(moves)
+        for k in range(8):
+            self.moves[8 + k] = (k, "core")
+        self.slots = [dp_index(x + rx, y + ry, core + c) for c in range(2) for rx, ry in SLOTS]
         self.started = []
 
-    def descriptor(self, g, k, src, slot, target):
-        first, count = self.parts[g]
+    def descriptor(self, k, src, slot, where):
         return pltpu.make_async_remote_copy(
-            src_ref=src.at[pl.ds(first, count)],
-            dst_ref=self.out.at[slot, pl.ds(first, count)],
-            send_sem=self.send.at[g, k],
-            recv_sem=self.recv.at[g, k],
-            device_id={"dp": target},
+            src_ref=src,
+            dst_ref=self.view(slot),
+            send_sem=self.send.at[k],
+            recv_sem=self.recv.at[k],
+            device_id={"dp": self.targets[where]},
             device_id_type=MESH,
         )
 
-    def move(self, g, k, where, source=0):
-        src = self.piece if source == 0 else self.out.at[self.slots[source]]
-        c = self.descriptor(g, k, src, self.slots[source], self.targets[where])
+    def issue(self, k):
+        source, where = self.moves[k]
+        slot = self.slots[source]
+        src = self.src if source == 0 else self.view(slot)
+        c = self.descriptor(k, src, slot, where)
         c.start()
         self.started.append(c)
 
-    def arrive(self, g, k, share=True):
+    def arrive(self, k):
         slot = self.slots[k]
-        self.descriptor(g, k, self.out.at[slot], slot, self.targets["x"]).wait_recv()
-        if share:
-            self.move(g, 8 + k, "core", k)
-
-    def begin(self):
-        for g in range(3):
-            self.move(g, 8, "core")
-        self.own = pltpu.make_async_copy(self.piece, self.out.at[self.mine], self.local)
-        self.own.start()
-
-    def finish(self):
-        for g in range(3):
-            for k, (rx, ry) in enumerate(SLOTS):
-                slot = dp_index(self.x + rx, self.y + ry, self.core + 1)
-                self.descriptor(
-                    g, 8 + k, self.out.at[slot], slot, self.targets["x"]
-                ).wait_recv()
-        for c in self.started:
-            c.wait_send()
-        self.own.wait()
+        self.descriptor(k, self.view(slot), slot, "x").wait_recv()
+
+
+X_FIRST = {
+    1: (0, "x"),
+    2: (0, "down"),
+    3: (0, "up"),
+    4: (1, "down"),
+    5: (1, "up"),
+    6: (3, "up"),
+    7: (4, "down"),
+}
+Y_FIRST = {
+    1: (0, "x"),
+    2: (0, "down"),
+    3: (0, "up"),
+    4: (2, "x"),
+    5: (3, "x"),
+    6: (3, "up"),
+    7: (6, "x"),
+}
+Y_FIRST_DOWN = {**Y_FIRST, 6: (2, "down")}
+PARTS = (
+    ((0, 1), (0, 288), X_FIRST),
+    ((1, 1), (0, 288), X_FIRST),
+    ((2, 1), (0, 288), X_FIRST),
+    ((3, 1), (0, 288), Y_FIRST),
+    ((4, 1), (0, 192), Y_FIRST_DOWN),
+    ((4, 1), (192, 96), X_FIRST),
+)
+KEPT = tuple(
+    jax.ShapeDtypeStruct(shape, kind)
+    for shape, kind in (
+        ((PEERS, REP * TOK, HEAD), BF),
+        ((GROUP, HEAD), BF),
+        ((GROUP, HEAD), BF),
+        ((PEERS, REP * TOK, 128), F32),
+        ((PEERS, TOK, QS), BF),
+        ((TOK, DIM), F32),
+        ((TOK, DIM), BF),
+        ((EXPERTS, TOK), F32),
+        ((GROUP, 128), F32),
+        ((GROUP, 128), F32),
+        ((GROUP, 128), jnp.int32),
+    )
+)
+FIRST_STEPS = ("ss", "so", "sl", "a", "g", "ls", "lo", "P0", "P1", "A0", "A1", "A2", "C2", "gt", "tb")
+FIRST_STEPS = FIRST_STEPS + tuple("tr%d" % i for i in range(4))
+FIRST_LINES = ("t", "c", "r", "s", "o") + tuple("p%d." % i for i in range(len(PARTS)))
+FIRST_STEPS = FIRST_STEPS + tuple(n + str(k) for n in FIRST_LINES for k in range(16))
+FIRST_ORDER = (
+    1, -1, 2, 6, 76, 69, 70, 71, -2, 135, 166, 20, 108, 188, 38, 156, 124, 15, 3, -69, 77, -71, 79,
+    172, 21, -70, 78, 140, 7, 102, 92, -166, 174, 74, 73, -135, 143, 101, 22, 119, 16, -74, 82, 37,
+    150, 17, -73, 81, -102, 110, 149, 103, 72, -101, 109, 18, -20, 24, -119, 127, 170, -150, 158,
+    23, 19, -72, 80, 152, 105, 134, -149, 157, -103, 111, -170, 178, -21, 25, 85, -24, 26, 183, 75,
+    -152, 160, -105, 113, 87, 118, -134, 142, -183, 191, -75, 83, 181, -37, 41, -85, 93, 36, 89,
+    88, -22, -23, -25, -26, -76, -77, -78, -79, -80, -81, -82, -83, 8, -87, 90, 95, -118, 126,
+    -181, 184, 133, 189, 9, 185, 86, 10, -184, 187, -36, 40, -89, 97, 138, 39, 192, -88, 96, 91,
+    117, 11, -185, 193, -86, 94, -133, 141, 137, -187, 195, 136, 168, -90, 98, 12, 4, -138, 146,
+    -117, 125, -40, 42, -91, 99, -168, 176, 165, 151, 122, 120, 171, 104, -4, -92, -93, -94, -95,
+    -96, -97, -98, -99, 13, -151, 159, -165, 173, 53, 54, 52, -136, 144, -137, 145, 14, 5, -171,
+    179, -120, 128, 154, -122, 130, 139, -104, 112, 153, -53, 57, 106, -52, 56, -154, 162, 107,
+    -139, 147, 155, 167, -153, 161, 55, -106, 114, 123, -56, 58, -107, 115, 121, -167, 175, 169,
+    -155, 163, 182, -123, 131, 186, -169, 177, -121, 129, -182, 190, -186, 194, -108, -188, -156,
+    -124, -172, -140, -174, -143, -38, -3, -110, -109, -127, -158, -157, -111, -178, -160, -113,
+    -142, -191, -126, -189, -41, -192, -193, -141, -195, -39, -146, -125, -176, -42, -159, -173,
+    -144, -145, -179, -128, -130, -54, -112, -5, -162, -147, -161, -57, -114, -115, -175, -163,
+    -55, -131, -58, -177, -129, -190, -194,
+)
 
 
 def first_kernel(*refs):
-    (slices, output, tokens, cot, member_ref, slot_send, piece, cos_ref, sin_ref, start_ref) = refs[
-        :10
-    ]
+    w_dense, (output, tokens, cot, ids, lengths, w_gate, w_up, w_down) = refs[:4], refs[4:12]
     (
         pieces_out,
         cot_all,
@@ -312,6 +266,10 @@
         normed_out,
         small_out,
         output_out,
+    ) = refs[12:21]
+    kept_out = refs[21:32]
+    kept_refs = refs[32:43]
+    (
         query_ref,
         key_ref,
         value_ref,
@@ -320,8 +278,17 @@
         middle_ref,
         normed_two_ref,
         gates_ref,
-    ) = refs[10:27]
+        cos_ref,
+        sin_ref,
+        start_ref,
+    ) = kept_refs
+    w_query, w_key, w_value, tail = refs[43:47]
     (
+        piece,
+        ids_ref,
+        member_ref,
+        slot_send,
+        slices,
         small_in,
         output_in,
         small_rows,
@@ -343,9 +310,30 @@
         s_direct,
         r_direct,
         l_sem,
-    ) = refs[27:]
+    ) = refs[47:]
+    x, y, core = dp_place()
+    me = lax.axis_index("expert")
+    mine = dp_index(x, y, core)
+    loads = [
+        pltpu.make_async_copy(src, dst, l_sem.at[20 + i])
+        for i, (src, dst) in enumerate(
+            zip(w_dense + (ids,), (w_query, w_key, w_value, tail, ids_ref))
+        )
+    ]
+    own = [
+        pltpu.make_async_copy(w_gate, piece.at[:, pl.ds(0, ROWS)], l_sem.at[15]),
+        pltpu.make_async_copy(w_up, piece.at[:, pl.ds(ROWS, ROWS)], l_sem.at[16]),
+    ] + [
+        pltpu.make_async_copy(
+            w_down.at[:, :, pl.ds(k * FFE, FFE)],
+            piece.at[:, pl.ds(2 * ROWS + 32 * k, 32)],
+            l_sem.at[17 + k],
+        )
+        for k in range(3)
+    ]
+    for c in loads + own:
+        c.start()
     _, peers = expert_peers()
-    x, y, core = dp_place()
     signal_all(
         peers,
         [
@@ -355,18 +343,33 @@
             dp_index(x, y, core + 1),
         ],
     )
+    for c in loads + own:
+        c.wait()
+    for j in range(PEERS):
+        slices[j] = jnp.concatenate(
+            [
+                w_query[:, QS * j : QS * (j + 1)],
+                w_key[:, HEAD * j : HEAD * (j + 1)],
+                w_value[:, HEAD * j : HEAD * (j + 1)],
+                tail[...],
+            ],
+            axis=1,
+        )
 
     def direct(i, src, out, mode):
         part = expert_copies(
             [src], [out], [mode], s_direct.at[pl.ds(i, 1)], r_direct.at[pl.ds(i, 1)]
         ) + own_copies([src], [out], [mode], l_sem.at[pl.ds(i, 1)])
-        for c in part:
-            c.start()
-        return part
-
-    def settle(part):
-        for c in part:
-            c.wait()
+
+        def start():
+            for c in part:
+                c.start()
+
+        def wait():
+            for c in part:
+                c.wait()
+
+        return start, wait
 
     saved = []
 
@@ -375,67 +378,84 @@
         c.start()
         saved.append(c)
 
-    parts = [
-        direct(0, slices, small_in, "exchange"),
-        direct(1, output, output_in, "gather"),
-        direct(2, slot_send, slots_all, "exchange"),
-    ]
-    tokens_gather = Gather(tokens, tokens_in, s_gather.at[0], r_gather.at[0], l_sem.at[5])
-    tokens_gather.begin()
-    experts = Pieces(piece, pieces_out, s_piece, r_piece, l_sem.at[6])
-    experts.begin()
-    for g in (1, 2):
-        experts.move(g, 3, "up")
-        experts.move(g, 2, "down")
-
-    weights = []
-    for i, (landed, rows, out) in enumerate(
-        ((small_in, small_rows, small), (output_in, output_rows, dense))
+    issue, arrive = {}, {}
+    for i, (name, src, out, mode) in enumerate(
+        (
+            ("ss", slices, small_in, "exchange"),
+            ("so", output, output_in, "gather"),
+            ("sl", slot_send, slots_all, "exchange"),
+            ("a", att_send, attended_ref, "exchange"),
+            ("g", gate_send, gates_all, "exchange"),
+        )
     ):
-        settle(parts[i])
+        issue[name], arrive[name] = direct(i, src, out, mode)
+    lines = {}
+    for i, (name, src, out) in enumerate(
+        (("t", tokens, tokens_in), ("c", cot, cot_all), ("r", normed_two_ref, rows_all))
+    ):
+        lines[name] = Gather(src, out, s_gather.at[i], r_gather.at[i], l_sem.at[5 + i])
+    for i, (name, src, out) in enumerate((("s", small_rows, small), ("o", output_rows, dense))):
+        lines[name] = Line(src, lambda k, out=out: out.at[k], X_FIRST, s_dense.at[i], r_dense.at[i])
+    for i, ((expert, count), (row, rows), moves) in enumerate(PARTS):
+        def view(k, span=pl.ds(expert, count), part=pl.ds(row, rows)):
+            return pieces_out.at[k, span, part]
+
+        own_part = piece.at[pl.ds(expert, count), pl.ds(row, rows)]
+        lines["p%d." % i] = Line(own_part, view, moves, s_piece.at[i], r_piece.at[i])
+    for name, line in lines.items():
+        for k in range(16):
+            issue[name + str(k)] = functools.partial(line.issue, k)
+            arrive[name + str(k)] = functools.partial(line.arrive, k)
+
+    kept = {}
+
+    def lay_out(name, landed, rows, out, i):
         rows[...] = jnp.concatenate([landed[j] for j in range(PEERS)], axis=0)
-        weights.append(Dense(rows, out, s_dense.at[i], r_dense.at[i], l_sem.at[7 + i]))
-        weights[i].begin()
-    experts.move(0, 1, "x")
-    for g in (1, 2):
-        experts.move(g, 1, "x")
-    tokens_gather.first()
-    for w in weights:
-        w.first()
-    tokens_gather.second()
-    for w in weights:
-        w.second()
-    tokens_gather.third()
-    experts.move(0, 3, "up")
-    experts.move(0, 2, "down")
-    cot_gather = Gather(cot, cot_all, s_gather.at[1], r_gather.at[1], l_sem.at[9])
-    cot_gather.begin()
-    for w in weights:
-        w.third()
-    weights[0].finish()
-    tokens_gather.finish()
-
-    for g in (1, 2):
-        experts.arrive(g, 3)
-        experts.arrive(g, 2)
-    experts.move(1, 6, "up", 3)
-    experts.move(2, 6, "down", 2)
-    for g in (1, 2):
-        experts.move(g, 5, "x", 3)
-        experts.move(g, 4, "x", 2)
-
-    w_small = small[...].reshape(DIM, SLICE)
-    pick = (
-        lax.broadcasted_iota(jnp.int32, (8, SLICE), 1)
-        == lax.broadcasted_iota(jnp.int32, (8, SLICE), 0) + GAINS
-    )
-    gains = dot(pick.astype(F32).astype(BF), w_small, ((1,), (1,)))
-    gain_one, gain_two = gains[0:1], gains[1:2]
+        kept[name] = pltpu.make_async_copy(rows, out.at[mine], l_sem.at[8 + i])
+        kept[name].start()
+
+    def tables():
+        named = jnp.zeros((TOK, 128), F32)
+        experts = lax.broadcasted_iota(jnp.int32, (TOK, 128), 1)
+        for k in range(ids_ref.shape[1]):
+            named = named + (ids_ref[:, k : k + 1] == experts).astype(F32)
+        before = (lax.broadcasted_iota(jnp.int32, (TOK, 128), 0) > experts).astype(F32)
+        places = dot(before.astype(BF), named.astype(BF), ((1,), (0,)))
+        member_ref[...] = jnp.transpose(jnp.where(named > 0.0, places, -1.0))[:EXPERTS]
+        slot_send[...] = jnp.full_like(slot_send, -1.0)
+        for j in range(PEERS):
+            slot_send[j, 0:LOCAL, :] = member_ref[LOCAL * j : LOCAL * (j + 1), :]
+
+    def turns(first, last):
+        second = lengths[0, 0]
+        third = second + lengths[0, 1]
+        fourth = third + lengths[0, 2]
+
+        def block(i, _):
+            span = pl.ds(pl.multiple_of(i * TOK, TOK), TOK)
+            place = lax.broadcasted_iota(jnp.int32, (TOK, 128), 0) + i * TOK
+            begins = jnp.where(
+                place >= fourth,
+                fourth,
+                jnp.where(place >= third, third, jnp.where(place >= second, second, 0)),
+            )
+            start_ref[span, :] = begins
+            lane = lax.broadcasted_iota(jnp.int32, (TOK, 128), 1)
+            step = (lane % (HEAD // 2)).astype(F32) * (2.0 / HEAD)
+            angle = (place - begins).astype(F32) * jnp.exp(-step * math.log(rope_base))
+            cos_ref[span, :] = jnp.cos(angle)
+            sin_ref[span, :] = jnp.where(lane % HEAD < HEAD // 2, -1.0, 1.0) * jnp.sin(angle)
+            return _
+
+        lax.fori_loop(first, last, block, 0)
+
+    issue["ls"] = functools.partial(lay_out, "s", small_in, small_rows, small, 0)
+    issue["lo"] = functools.partial(lay_out, "o", output_in, output_rows, dense, 1)
 
     def project(i, _):
         values = tokens_in[pl.ds(2 * i, 2)].reshape(2 * TOK, DIM).astype(F32)
         scale = lax.rsqrt(jnp.mean(values * values, axis=-1, keepdims=True) + epsilon)
-        low = (values * scale * gain_one).astype(BF)
+        low = (values * scale * kept["gains"][0:1]).astype(BF)
         normed[pl.ds(2 * i, 2)] = low.reshape(2, TOK, DIM)
         qkv = dot(low, small[...].reshape(DIM, SLICE), ((1,), (0,)))
         span = pl.ds(pl.multiple_of(i * 2 * TOK, 2 * TOK), 2 * TOK)
@@ -456,10 +476,23 @@
         value_ref[span, :] = qkv[:, QS + HEAD : ROUTER].astype(BF)
         return _
 
-    lax.fori_loop(0, 4, project, 0)
-    save(tokens_in, tokens_out, 10)
-    save(normed, normed_out, 11)
-    save(small, small_out, 12)
+    def project_first():
+        lines["t"].own.wait()
+        kept["s"].wait()
+        pick = (
+            lax.broadcasted_iota(jnp.int32, (8, SLICE), 1)
+            == lax.broadcasted_iota(jnp.int32, (8, SLICE), 0) + GAINS
+        )
+        kept["gains"] = dot(
+            pick.astype(F32).astype(BF), small[...].reshape(DIM, SLICE), ((1,), (1,))
+        )
+        lax.fori_loop(0, 2, project, 0)
+
+    def project_rest():
+        lax.fori_loop(2, 4, project, 0)
+        save(tokens_in, tokens_out, 10)
+        save(normed, normed_out, 11)
+        save(small, small_out, 12)
 
     def attend(width, i, _):
         scores = dot(query_ref[i], key_ref[0:width, :], ((1,), (1,))) * HEAD ** (-0.5)
@@ -479,77 +512,62 @@
         )
         return _
 
-    experts.arrive(0, 1)
-    experts.move(0, 5, "up", 1)
-    experts.move(0, 4, "down", 1)
-    cot_gather.first()
-    cot_gather.second()
-    lax.fori_loop(0, 4, functools.partial(attend, GROUP // 2), 0)
-    for g in (1, 2):
-        experts.arrive(g, 1)
-    cot_gather.third()
-    lax.fori_loop(4, 8, functools.partial(attend, GROUP), 0)
-    parts.append(direct(3, att_send, attended_ref, "exchange"))
-    experts.arrive(0, 3)
-    experts.move(0, 6, "up", 3)
-    experts.arrive(0, 2)
-    for g in (1, 2):
-        experts.arrive(g, 4)
-        experts.arrive(g, 5)
-    settle(parts[3])
-    weights[1].finish()
-    save(dense, output_out, 13)
-
-    me = lax.axis_index("expert")
-    middle = tokens_in[me].astype(F32)
-    for j in range(PEERS):
-        middle = middle + dot(
-            attended_ref[j], dense[2 * j : 2 * j + 2].reshape(QS, DIM), ((1,), (0,))
-        )
-    middle_ref[...] = middle
-    scale_two = lax.rsqrt(jnp.mean(middle * middle, axis=-1, keepdims=True) + epsilon)
-    normed_two = (middle * scale_two * gain_two).astype(BF)
-    normed_two_ref[...] = normed_two
-    rows_gather = Gather(normed_two_ref, rows_all, s_gather.at[2], r_gather.at[2], l_sem.at[14])
-    rows_gather.begin()
-    logits = dot(small[:, :, 256:SLICE].reshape(DIM, SLICE - 256), normed_two, ((0,), (1,)))
-    logits = logits[ROUTER - 256 : GAINS - 256]
-    member = member_ref[...] >= 0.0
-    chosen = jnp.where(member, logits, masked_score)
-    weight = jnp.where(member, jnp.exp(chosen - jnp.max(chosen, axis=0, keepdims=True)), 0.0)
-    gates_ref[...] = weight / jnp.sum(weight, axis=0, keepdims=True)
-    gate_send[...] = jnp.zeros_like(gate_send)
-    for j in range(PEERS):
-        gate_send[j, 0:LOCAL, :] = gates_ref[LOCAL * j : LOCAL * (j + 1), :]
-    parts.append(direct(4, gate_send, gates_all, "exchange"))
-
-    rows_gather.first()
-    rows_gather.second()
-    experts.arrive(0, 4)
-    experts.move(0, 7, "down", 4)
-    experts.arrive(0, 5)
-    rows_gather.third()
-    for g in (1, 2):
-        experts.arrive(g, 6)
-        experts.move(g, 7, "x", 6)
-    cot_gather.finish()
-    rows_gather.finish()
-    settle(parts[2])
-    settle(parts[4])
-    experts.arrive(0, 6)
-    for g in (0, 1, 2):
-        experts.arrive(g, 7)
-    experts.finish()
+    issue["P0"], issue["P1"] = project_first, project_rest
+    for name, first, last, width in (("A0", 0, 4, 512), ("A1", 4, 6, 1024), ("A2", 6, 8, 1024)):
+        issue[name] = functools.partial(
+            lax.fori_loop, first, last, functools.partial(attend, width), 0
+        )
+
+    def out_project():
+        kept["o"].wait()
+        save(dense, output_out, 13)
+        middle = tokens_in[me].astype(F32)
+        for j in range(PEERS):
+            middle = middle + dot(
+                attended_ref[j], dense[2 * j : 2 * j + 2].reshape(QS, DIM), ((1,), (0,))
+            )
+        middle_ref[...] = middle
+        scale_two = lax.rsqrt(jnp.mean(middle * middle, axis=-1, keepdims=True) + epsilon)
+        normed_two_ref[...] = (middle * scale_two * kept["gains"][1:2]).astype(BF)
+        lines["r"].begin()
+
+    def choose():
+        router = small[:, :, 256:SLICE].reshape(DIM, SLICE - 256)
+        logits = dot(router, normed_two_ref[...], ((0,), (1,)))[ROUTER - 256 : GAINS - 256]
+        member = member_ref[...] >= 0.0
+        chosen = jnp.where(member, logits, masked_score)
+        weight = jnp.where(member, jnp.exp(chosen - jnp.max(chosen, axis=0, keepdims=True)), 0.0)
+        gates_ref[...] = weight / jnp.sum(weight, axis=0, keepdims=True)
+        gate_send[...] = jnp.zeros_like(gate_send)
+        for j in range(PEERS):
+            gate_send[j, 0:LOCAL, :] = gates_ref[LOCAL * j : LOCAL * (j + 1), :]
+
+    issue["C2"], issue["gt"] = out_project, choose
+    save(piece, pieces_out.at[mine], 14)
+    lines["t"].begin()
+    lines["c"].begin()
+    issue["tb"] = tables
+    for i in range(4):
+        issue["tr%d" % i] = functools.partial(turns, 2 * i, 2 * i + 2)
+    for step in FIRST_ORDER:
+        (issue if step > 0 else arrive)[FIRST_STEPS[abs(step) - 1]]()
+    lines["c"].own.wait()
+    lines["r"].own.wait()
+    for line in lines.values():
+        for c in line.started:
+            c.wait_send()
+    for i, (src, dst) in enumerate(zip(kept_refs, kept_out)):
+        save(src, dst, 25 + i)
     for c in saved:
         c.wait()
 
 
-def first_phase(slices, output, tokens, cot, member, slot_send, piece, cosine, sine, start):
-    hbm, vmem = pl.BlockSpec(memory_space=pl.ANY), pl.BlockSpec(memory_space=pltpu.VMEM)
+def first_phase(*args):
+    hbm, smem = pl.BlockSpec(memory_space=pltpu.HBM), pl.BlockSpec(memory_space=pltpu.SMEM)
     shape = jax.ShapeDtypeStruct
     blocks = (PEERS, TOK, DIM)
     outs = [
-        (shape((DP,) + piece.shape, BF), hbm),
+        (shape((DP, LOCAL, 3 * ROWS, FFE), BF), hbm),
         (shape(blocks, BF), hbm),
         (shape((PEERS, 8, TOK), F32), hbm),
         (shape(blocks, BF), hbm),
@@ -558,22 +576,21 @@
         (shape(blocks, BF), hbm),
         (shape((DP, ROWS, SLICE), BF), hbm),
         (shape((DP, ROWS, DIM), BF), hbm),
-        (shape((PEERS, REP * TOK, HEAD), BF), vmem),
-        (shape((GROUP, HEAD), BF), vmem),
-        (shape((GROUP, HEAD), BF), vmem),
-        (shape((PEERS, REP * TOK, 128), F32), vmem),
-        (shape((PEERS, TOK, QS), BF), vmem),
-        (shape((TOK, DIM), F32), vmem),
-        (shape((TOK, DIM), BF), vmem),
-        (shape((EXPERTS, TOK), F32), vmem),
-    ]
+    ] + [(k, hbm) for k in KEPT]
     dma = pltpu.SemaphoreType.DMA
     return pl.pallas_call(
         first_kernel,
         out_shape=[o[0] for o in outs],
-        in_specs=[hbm] * 4 + [vmem] + [hbm] * 2 + [vmem] * 3,
+        in_specs=[hbm] * 8 + [smem] + [hbm] * 3,
         out_specs=[o[1] for o in outs],
-        scratch_shapes=[
+        scratch_shapes=[pltpu.VMEM(k.shape, k.dtype) for k in KEPT]
+        + [pltpu.VMEM(a.shape, a.dtype) for a in args[:4]]
+        + [
+            pltpu.VMEM((LOCAL, 3 * ROWS, FFE), BF),
+            pltpu.VMEM((TOK, 8), jnp.int32),
+            pltpu.VMEM((EXPERTS, TOK), F32),
+            pltpu.VMEM((PEERS, 8, TOK), F32),
+            pltpu.VMEM((PEERS, 12, SLICE), BF),
             pltpu.VMEM((PEERS, 12, SLICE), BF),
             pltpu.VMEM((PEERS, 12, DIM), BF),
             pltpu.VMEM((ROWS, SLICE), BF),
@@ -586,21 +603,21 @@
             pltpu.VMEM((PEERS, 8, TOK), F32),
             dma((1,)),
             dma((2, 16)),
-            dma((3, 16)),
+            dma((len(PARTS), 16)),
             dma((1,)),
             dma((2, 16)),
-            dma((3, 16)),
+            dma((len(PARTS), 16)),
             dma((3, 7)),
             dma((3, 7)),
             dma((5, 7)),
             dma((5, 7)),
-            dma((15,)),
+            dma((40,)),
         ],
         compiler_params=pltpu.CompilerParams(
-            collective_id=1, has_side_effects=True, vmem_limit_bytes=50 << 20
+            collective_id=1, has_side_effects=True, vmem_limit_bytes=63 << 20
         ),
         cost_estimate=lasting(120),
-    )(slices, output, tokens, cot, member, slot_send, piece, cosine, sine, start)
+    )(*args)
 
 
 def dot(a, b, contract):
@@ -850,22 +867,31 @@
         normed_all,
         small_hbm,
         dense_hbm,
-        tokens,
-        cot,
-        gates_ref,
-        middle_ref,
-        normed_two_ref,
-        attended_ref,
+        tokens_hbm,
+        cot_hbm,
+    ) = refs[:11]
+    kept_in = refs[11:22]
+    mixed_out, grad_tokens_out, expert_ref, small_own, output_out, near, far = refs[22:29]
+    kept_refs = refs[29:40]
+    (
         query_ref,
         key_ref,
         value_ref,
         log_ref,
+        attended_ref,
+        middle_ref,
+        normed_two_ref,
+        gates_ref,
         cos_ref,
         sin_ref,
         start_ref,
-    ) = refs[:22]
-    mixed_ref, grad_tokens_ref, expert_ref, small_own, output_own, near, far = refs[22:29]
+    ) = kept_refs
     (
+        tokens,
+        cot,
+        mixed_ref,
+        grad_tokens_ref,
+        output_own,
         inner_in,
         gates_grad,
         logits_grad,
@@ -909,7 +935,7 @@
         r_far,
         l_sem,
         l_add,
-    ) = refs[29:]
+    ) = refs[40:]
     _, peers = expert_peers()
     x, y, core = dp_place()
     me = lax.axis_index("expert")
@@ -954,6 +980,8 @@
     back.begin()
     loads = own_blocks(back, back_part, 8)
     inner = direct(0, inner_part, inner_in, "exchange")
+    kept = [load(a, b, 16 + i) for i, (a, b) in enumerate(zip(kept_in, kept_refs))]
+    kept = kept + [load(tokens_hbm, tokens, 27), load(cot_hbm, cot, 28)]
     loads_small = load(small_hbm, small, 4)
     loads_dense = load(dense_hbm, dense, 5)
     loads_normed = load(normed_all, normed, 6)
@@ -965,15 +993,17 @@
     settle(loads)
     back.relay()
     experts.far_send(7, 3, "x")
-    experts.far_send(4, 1, "x")
+    experts.far_send(4, 1, "x", (0,))
     experts.near_send(4, 2, "up")
     back.cross()
+    experts.near_send(5, 3, "down", (1,))
     experts.far_send(6, 4, "up", (0,), (3,))
     experts.far_send(6, 5, "down", (1,), (3,))
-    experts.near_send(5, 3, "down", (1,))
     experts.near_send(2, 4, "up", (0,))
+    experts.near_send(3, 5, "down")
+    experts.far_send(4, 1, "x", (1,))
     settle(inner)
-    settle([loads_small, loads_dense])
+    settle([loads_small, loads_dense] + kept)
 
     for j in range(PEERS):
         gates_grad[LOCAL * j : LOCAL * (j + 1), :] = inner_in[j, 0:LOCAL, :]
@@ -1009,7 +1039,6 @@
         dense[2 * j : 2 * j + 2] = (
             dot(attended_ref[j], grad_branch, ((0,), (0,))).astype(BF).reshape(2, ROWS, DIM)
         )
-    experts.near_send(3, 5, "down")
     settle(exchanged)
     out = Reduce(out_part, from_own, y_landed, s_reduce.at[1], r_reduce.at[1])
     out.begin()
@@ -1048,9 +1077,8 @@
     lax.fori_loop(0, 4, functools.partial(attend, GROUP // 2), 0)
     settle(loads)
     out.relay()
-    experts.far_send(2, 6, "up", (0, 1), (1, 4))
-    experts.far_send(3, 7, "down", (0, 1), (2, 5))
     experts.near_send(1, 6, "x", (2, 3))
+    sums[0].first()
     lax.fori_loop(4, 8, functools.partial(attend, GROUP), 0)
     out.cross()
 
@@ -1093,11 +1121,9 @@
 
     first = Reduce(grad_normed, from_grad, z_landed, s_reduce.at[2], r_reduce.at[2])
     first.begin()
-    sums[0].first()
 
     lanes = lax.broadcasted_iota(jnp.int32, (8, 128), 1)
     marks = [(lanes == GAINS - 256 + i).astype(F32).astype(BF) for i in range(2)]
-    first.relay()
     for c in range(4):
         span = slice(c * 384, (c + 1) * 384)
         part = dot(normed[:, :, span].reshape(GROUP, 384), grad_qkv[...], ((0,), (0,)))
@@ -1114,18 +1140,21 @@
             (part[:, 256:SLICE] + extra).astype(BF).reshape(4, ROWS, SLICE - 256)
         )
     sums[1].begin()
+    first.relay()
     sums[0].second()
+    sums[1].first()
+    experts.far_send(2, 6, "up", (0, 1), (1, 4))
+    experts.far_send(3, 7, "down", (0, 1), (2, 5))
     mixed_ref[...] = (middle_ref[...] + out.total()).astype(BF)
-    sums[1].first()
+    saves = [load(mixed_ref, mixed_out, 29)]
     first.cross()
+    sums[0].third()
     sums[1].second()
-    experts.far_end()
-    saved = load(ends.at[pl.ds(0, 2)], expert_ref.at[pl.ds(3, 2)], 4)
-    sums[0].third()
     sums[1].third()
     values = tokens[...].astype(F32)
     scale = lax.rsqrt(jnp.mean(values * values, axis=-1, keepdims=True) + epsilon)
     grad_tokens_ref[...] = grad_middle_ref[...] + norm_back(values, scale, gain_one, first.total())
+    saves.append(load(grad_tokens_ref, grad_tokens_out, 30))
     total = sums[0].total()
     for j in range(PEERS):
         dense_cut[j] = total[12 * j : 12 * (j + 1)]
@@ -1133,6 +1162,8 @@
     for j in range(PEERS):
         small_cut[j] = total[12 * j : 12 * (j + 1)]
     cuts = direct(2, dense_cut, dense_in, "exchange") + direct(3, small_cut, small_own, "exchange")
+    experts.far_end()
+    saved = load(ends.at[pl.ds(0, 2)], expert_ref.at[pl.ds(3, 2)], 4)
     saved.wait()
     experts.near_end()
     saved = load(ends, expert_ref.at[pl.ds(0, 3)], 4)
@@ -1141,31 +1172,38 @@
     for j in range(1, PEERS):
         acc = acc + dense_in[j]
     output_own[...] = acc
+    saves.append(load(output_own, output_out, 31))
     for part in (out, first, sums[0], sums[1], experts):
         part.finish()
-    saved.wait()
+    settle(saves + [saved])
 
 
 def last_phase(*args):
-    hbm, vmem = pl.BlockSpec(memory_space=pl.ANY), pl.BlockSpec(memory_space=pltpu.VMEM)
+    hbm = pl.BlockSpec(memory_space=pltpu.HBM)
     shape, dma = jax.ShapeDtypeStruct, pltpu.SemaphoreType.DMA
     blocks = (PEERS, TOK, DIM)
     piece = (3 * ROWS, FFE)
     outs = [
-        (shape((TOK, DIM), BF), vmem),
-        (shape((TOK, DIM), F32), vmem),
+        (shape((TOK, DIM), BF), hbm),
+        (shape((TOK, DIM), F32), hbm),
         (shape((LOCAL,) + piece, F32), hbm),
         (shape((PEERS, 12, SLICE), F32), hbm),
-        (shape((12, DIM), F32), vmem),
+        (shape((12, DIM), F32), hbm),
         (shape((7, 3) + piece, BF), hbm),
         (shape((8, 2) + piece, BF), hbm),
     ]
     return pl.pallas_call(
         last_kernel,
         out_shape=[o[0] for o in outs],
-        in_specs=[hbm] * 9 + [vmem] * 13,
+        in_specs=[hbm] * 22,
         out_specs=[o[1] for o in outs],
-        scratch_shapes=[
+        scratch_shapes=[pltpu.VMEM(k.shape, k.dtype) for k in KEPT]
+        + [
+            pltpu.VMEM((TOK, DIM), BF),
+            pltpu.VMEM((TOK, DIM), BF),
+            pltpu.VMEM((TOK, DIM), BF),
+            pltpu.VMEM((TOK, DIM), F32),
+            pltpu.VMEM((12, DIM), F32),
             pltpu.VMEM((PEERS, 8, TOK), F32),
             pltpu.VMEM((EXPERTS, TOK), F32),
             pltpu.VMEM((SLICE - 256, TOK), F32),
@@ -1207,11 +1245,11 @@
             dma((7,)),
             dma((8, 2)),
             dma((8, 2)),
-            dma((12,)),
+            dma((32,)),
             dma((2, 5)),
         ],
         compiler_params=pltpu.CompilerParams(
-            collective_id=3, has_side_effects=True, vmem_limit_bytes=62 << 20
+            collective_id=3, has_side_effects=True, vmem_limit_bytes=63 << 20
         ),
         cost_estimate=lasting(120),
     )(*args)
@@ -1376,7 +1414,7 @@
             pltpu.SemaphoreType.DMA((LOCAL, 8)),
         ],
         compiler_params=pltpu.CompilerParams(
-            collective_id=2, has_side_effects=True, vmem_limit_bytes=60 << 20
+            collective_id=2, has_side_effects=True, vmem_limit_bytes=63 << 20
         ),
         cost_estimate=pl.CostEstimate(
             flops=20_000_000_000, bytes_accessed=60_000_000, transcendentals=700_000
@@ -1384,24 +1422,95 @@
     )(rows, cot, slots, gates, pieces)
 
 
-def rope_tables(offsets, head_width):
-    exponent = jnp.arange(head_width // 2, dtype=jnp.float32) * (2.0 / head_width)
-    frequency = jnp.exp(-exponent * math.log(rope_base))
-    phase_angles = offsets.astype(jnp.float32)[:, None] * frequency[None, :]
-    return (jnp.cos(phase_angles)[:, None, :], jnp.sin(phase_angles)[:, None, :])
-
-
-def layout(lengths, group_count):
-    seq_ends = jnp.cumsum(lengths)
-    starts = seq_ends - lengths
-    places = jnp.arange(group_count, dtype=jnp.int32)
-    member = ((places[:, None] >= starts[None, :]) & (places[:, None] < seq_ends[None, :])).astype(
-        jnp.int32
+def finish_kernel(mixed, tokens, experts, small, output, *refs):
+    outs, (mixed_ref, tokens_ref, experts_ref, small_ref, output_ref, cut_ref, sem) = (
+        refs[:10],
+        refs[10:],
     )
-    numbers = jnp.arange(lengths.shape[0], dtype=jnp.int32)
-    segment = jnp.sum(member * numbers[None, :], axis=1)
-    offsets = places - jnp.sum(member * starts[None, :], axis=1)
-    return (segment, offsets)
+    mixed_out, tokens_out, q_out, k_out, v_out, output_out, tail_out, gate, up, down = outs
+    loads = [
+        pltpu.make_async_copy(src, dst, sem.at[13 + i])
+        for i, (src, dst) in enumerate(
+            (
+                (small, small_ref),
+                (experts, experts_ref),
+                (tokens, tokens_ref),
+                (mixed, mixed_ref),
+                (output, output_ref),
+            )
+        )
+    ]
+    for c in loads:
+        c.start()
+    for c in loads[1:]:
+        c.wait()
+    copies = [
+        pltpu.make_async_copy(mixed_ref, mixed_out, sem.at[1]),
+        pltpu.make_async_copy(tokens_ref, tokens_out, sem.at[2]),
+        pltpu.make_async_copy(output_ref, output_out, sem.at[3]),
+        pltpu.make_async_copy(experts_ref.at[:, pl.ds(0, ROWS)], gate, sem.at[4]),
+        pltpu.make_async_copy(experts_ref.at[:, pl.ds(ROWS, ROWS)], up, sem.at[5]),
+    ] + [
+        pltpu.make_async_copy(
+            experts_ref.at[:, pl.ds(2 * ROWS + 32 * k, 32)],
+            down.at[:, :, pl.ds(k * FFE, FFE)],
+            sem.at[6 + k],
+        )
+        for k in range(3)
+    ]
+    for c in copies:
+        c.start()
+    loads[0].wait()
+    total = small_ref[0]
+    for j in range(1, PEERS):
+        total = total + small_ref[j]
+    cut_ref[...] = jnp.concatenate(
+        [small_ref[j, :, :QS] for j in range(PEERS)]
+        + [small_ref[j, :, QS : QS + HEAD] for j in range(PEERS)]
+        + [small_ref[j, :, QS + HEAD : ROUTER] for j in range(PEERS)]
+        + [total[:, 256:SLICE]],
+        axis=1,
+    )
+    widths = (DIM, KV_HEADS * HEAD, KV_HEADS * HEAD, SLICE - 256)
+    begins = (0, DIM, DIM + KV_HEADS * HEAD, DIM + 2 * KV_HEADS * HEAD)
+    for i, ref in enumerate((q_out, k_out, v_out, tail_out)):
+        c = pltpu.make_async_copy(cut_ref.at[:, pl.ds(begins[i], widths[i])], ref, sem.at[9 + i])
+        c.start()
+        copies.append(c)
+    for c in copies:
+        c.wait()
+
+
+def finish(*args):
+    shape = jax.ShapeDtypeStruct
+    width = KV_HEADS * HEAD
+    return pl.pallas_call(
+        finish_kernel,
+        out_shape=[
+            shape((TOK, DIM), BF),
+            shape((TOK, DIM), F32),
+            shape((12, DIM), F32),
+            shape((12, width), F32),
+            shape((12, width), F32),
+            shape((12, DIM), F32),
+            shape((12, SLICE - 256), F32),
+            shape((LOCAL, ROWS, FFE), F32),
+            shape((LOCAL, ROWS, FFE), F32),
+            shape((LOCAL, 32, DIM), F32),
+        ],
+        in_specs=any_specs(5),
+        out_specs=any_specs(10),
+        scratch_shapes=[
+            pltpu.VMEM((TOK, DIM), BF),
+            pltpu.VMEM((TOK, DIM), F32),
+            pltpu.VMEM((LOCAL, 3 * ROWS, FFE), F32),
+            pltpu.VMEM((PEERS, 12, SLICE), F32),
+            pltpu.VMEM((12, DIM), F32),
+            pltpu.VMEM((12, DIM + 2 * width + SLICE - 256), F32),
+            pltpu.SemaphoreType.DMA((18,)),
+        ],
+        compiler_params=pltpu.CompilerParams(vmem_limit_bytes=63 << 20),
+    )(*args)
 
 
 def norm_back(values, row_scale, gain_vector, grad_normed):
@@ -1409,10 +1518,6 @@
     return row_scale * weighted - values * row_scale**3 * jnp.mean(
         weighted * values, axis=-1, keepdims=True
     )
-
-
-def by_peer(table):
-    return jnp.pad(table.reshape(PEERS, LOCAL, TOK), ((0, 0), (0, 8 - LOCAL), (0, 0)))
 
 
 def local(
@@ -1431,41 +1536,10 @@
     w_up,
     w_down,
 ):
-    down_piece = w_down.reshape(LOCAL, 32, 3, FFE).transpose(0, 2, 1, 3).reshape(LOCAL, ROWS, FFE)
-    piece = jnp.concatenate([w_gate, w_up, down_piece], axis=1)
-
-    slices = jnp.concatenate(
-        [
-            w_query.reshape(12, PEERS, QS).transpose(1, 0, 2),
-            w_key.reshape(12, PEERS, HEAD).transpose(1, 0, 2),
-            w_value.reshape(12, PEERS, HEAD).transpose(1, 0, 2),
-            jnp.broadcast_to(
-                jnp.concatenate(
-                    [
-                        w_router,
-                        norm_one[:, None],
-                        norm_two[:, None],
-                        jnp.zeros((12, SLICE - GAINS - 2), BF),
-                    ],
-                    axis=1,
-                )[None],
-                (PEERS, 12, SLICE - ROUTER),
-            ),
-        ],
-        axis=2,
+    tail = jnp.concatenate(
+        [w_router, norm_one[:, None], norm_two[:, None], jnp.zeros((12, SLICE - GAINS - 2), BF)],
+        axis=1,
     )
-    member = jnp.any(
-        expert_ids[None, :, :] == jnp.arange(EXPERTS, dtype=jnp.int32)[:, None, None], axis=-1
-    )
-    before = jnp.arange(TOK)[:, None] < jnp.arange(TOK)[None, :]
-    places = jnp.dot(member.astype(BF), before.astype(BF), preferred_element_type=F32)
-    slot_table = jnp.where(member, places, -1.0)
-
-    segment, offsets = layout(seq_lengths[0], GROUP)
-    cosine, sine_table = rope_tables(offsets, HEAD)
-    wide_cosine = jnp.tile(cosine[:, 0, :], (1, 4))
-    wide_sine = jnp.tile(jnp.concatenate([-sine_table[:, 0, :], sine_table[:, 0, :]], axis=1), (1, 2))
-    start = jnp.broadcast_to((jnp.arange(GROUP, dtype=jnp.int32) - offsets)[:, None], (GROUP, 128))
     (
         pieces,
         cot_all,
@@ -1476,25 +1550,20 @@
         normed_all,
         slices_all,
         output_all,
-        query,
-        key,
-        value,
-        log_total,
-        attended,
-        middle,
-        normed_two,
-        gate_values,
+        *kept,
     ) = first_phase(
-        slices,
+        w_query,
+        w_key,
+        w_value,
+        tail,
         w_output,
         tokens,
         cotangent,
-        slot_table,
-        by_peer(slot_table),
-        piece,
-        wide_cosine,
-        wide_sine,
-        start,
+        expert_ids,
+        seq_lengths,
+        w_gate,
+        w_up,
+        w_down,
     )
     out_part, back_part, inner_part, keep, given = run_experts(
         rows_all, cot_all, slots_all, gates_all, pieces
@@ -1511,35 +1580,25 @@
         output_all,
         tokens,
         cotangent,
-        gate_values,
-        middle,
-        normed_two,
-        attended,
+        *kept,
+    )
+    mixed, grad_tokens, query, key, value, output, rest, gate, up, down = finish(
+        mixed, grad_tokens, expert_grads, small_own, output_own
+    )
+    rest = rest[:, ROUTER - 256 :]
+    return (
+        mixed,
+        grad_tokens,
         query,
         key,
         value,
-        log_total,
-        wide_cosine,
-        wide_sine,
-        start,
-    )
-    own_sum = jnp.sum(small_own[:, :, ROUTER:], axis=0)
-    return (
-        mixed,
-        grad_tokens,
-        small_own[:, :, :QS].transpose(1, 0, 2).reshape(12, DIM),
-        small_own[:, :, QS : QS + HEAD].transpose(1, 0, 2).reshape(12, KV_HEADS * HEAD),
-        small_own[:, :, QS + HEAD : ROUTER].transpose(1, 0, 2).reshape(12, KV_HEADS * HEAD),
-        output_own,
-        own_sum[:, EXPERTS],
-        own_sum[:, EXPERTS + 1],
-        own_sum[:, :EXPERTS],
-        expert_grads[:, :ROWS],
-        expert_grads[:, ROWS : 2 * ROWS],
-        expert_grads[:, 2 * ROWS :]
-        .reshape(LOCAL, 3, 32, FFE)
-        .transpose(0, 2, 1, 3)
-        .reshape(LOCAL, 32, DIM),
+        output,
+        rest[:, EXPERTS],
+        rest[:, EXPERTS + 1],
+        rest[:, :EXPERTS],
+        gate,
+        up,
+        down,
     )
 
 

time: 357 us -> 325 us (0.910)
  local copies, waits for them, and re-layouts: 21.7 us -> 5.83 us
  Pallas kernels: 325 us -> 316 us
  other arithmetic: 7.26 us -> 1.37 us
    reshape x11 -> x0, local copies, waits for them, and re-layouts: 9.17 us -> none  [the longest x2 2.35 us: local(): return (mixed, grad_tokens, small_own[:, :, :QS].transpose(1, 0, 2).resha...]
    pallas_call x1, Pallas kernels: 141 us -> 133 us  [first_phase(): pl.pallas_call(first_kernel, out_shape=[o[0] for o in outs], in_specs=[hb...]
    pallas_call x1, Pallas kernels: 150 us -> 144 us  [last_phase(): pl.pallas_call(last_kernel, out_shape=[o[0] for o in outs], in_specs=[hbm...]
    pallas_call x0 -> x1, Pallas kernels: none -> 4.44 us  [finish(): pl.pallas_call(finish_kernel, out_shape=[shape((TOK, DIM), BF), shape((TO...]
    unnamed x37 -> x1, local copies, waits for them, and re-layouts: 5.08 us -> 1.41 us
where the time goes in v5:
time: 325 us; the launch traced here: 324 us
  Pallas kernels  316 us (97%)
  local copies, waits for them, and re-layouts  5.83 us (2%)
    pallas_call x1, Pallas kernels, last_phase(): pl.pallas_call(last_kernel, out_shape=[o[0] for o in outs], in_specs=[hbm...  144 us
    pallas_call x1, Pallas kernels, first_phase(): pl.pallas_call(first_kernel, out_shape=[o[0] for o in outs], in_specs=[hb...  133 us
    pallas_call x1, Pallas kernels, run_experts(): pl.pallas_call(experts_kernel, out_shape=[jax.ShapeDtypeStruct((PEERS, TO...  34.7 us

profile of v5, /device:TPU:0, one launch (start us, length us, event | category | flops | bytes accessed | tf_op | source)
XLA Modules:
  0.0 324.2 jit_solution(355071174976499714)
XLA Ops:
  0.7 0.1 pad.3.clone
  0.7 0.7 copy.29
  1.5 0.8 copy.30
  2.2 1.4 maximum_maximum_fusion.refs_3_
  3.6 1.4 copy.31.refs_7_
  5.0 133.2 %shard_map.229 = (bf16[16,5,288,512]{3,2,1,0:T(8,128)(2,1)}, bf16[8,128,1536]{2,1,0:T(8,128)(2,1)}, f32[8,8,128]{2,1,0:T(8,128)}, bf16[8,128,1536]{2,1,0:T(8,128...) custom-call(bf16[12,1536]{1,0:T(8,128)(2,1)} %refs_0_.1, ...), custom_call_target="tpu_custom_call" | custom-call | flops 120000004096 | tf_op jit(solution)/shard_map/pallas_call | solution.py:581
  138.2 34.7 %shard_map.230 = (bf16[8,128,1536]{2,1,0:T(8,128)(2,1)}, bf16[8,128,1536]{2,1,0:T(8,128)(2,1)}, f32[8,8,128]{2,1,0:T(8,128)}, bf16[8,5,288,512]{3,2,1,0:T(8,128)(2,1)}, bf16[8,5,288,512]{3,2,1,0:T(8,128)(2,1)}) custom-call(bf16[8,128,1536]{2,1,0:T(8,128)(2,1)} %get-tuple-element.52.refs_0_, bf16[8,128,1536]{2,1,0:T(8,128)(2,1)} %get-tuple-element.53.refs_1_, ...), custom_call_target="tpu_custom_call" | custom-call | flops 20000000000 | bytes 60000000 | tf_op jit(solution)/shard_map/pallas_call | solution.py:1394
  172.9 144.0 %shard_map.231 = (bf16[128,1536]{1,0:T(8,128)(2,1)}, f32[128,1536]{1,0:T(8,128)}, f32[5,288,512]{2,1,0:T(8,128)}, f32[8,12,384]{2,1,0:T(8,128)}, f32[12,1536]{1,...) custom-call(bf16[8,128,1536]{2,1,0:T(8,128)(2,1)} %get-tuple-element.57.refs_0_, ...), custom_call_target="tpu_custom_call" | custom-call | flops 120000004096 | tf_op jit(solution)/shard_map/pallas_call | solution.py:1195
  316.9 4.4 %shard_map.232 = (bf16[128,1536]{1,0:T(8,128)(2,1)}, f32[128,1536]{1,0:T(8,128)}, f32[12,1536]{1,0:T(8,128)}, f32[12,512]{1,0:T(8,128)}, f32[12,512]{1,0:T(8,128...) custom-call(bf16[128,1536]{1,0:T(8,128)(2,1)} %get-tuple-element.77., ...), custom_call_target="tpu_custom_call" | custom-call | tf_op jit(solution)/shard_map/pallas_call | solution.py:1487
  321.4 1.5 slice_reduce_fusion
  322.9 1.4 slice.15
  (1 shorter events, 0.0 us)

commit v6 on v5

--- a/solution.py
+++ b/solution.py
@@ -631,68 +631,103 @@
         me = lax.axis_index("expert")
         z, x = me // 2, me % 2
         self.place = lambda dz, dx: (z + dz) % 4 * 2 + (x + dx) % 2
-        self.targets = {"up": self.place(1, 0), "down": self.place(3, 0), "x": self.place(0, 1)}
+        up, down, across = self.place(1, 0), self.place(3, 0), self.place(0, 1)
+        self.moves = {
+            0: ((2, 1), up),
+            1: ((2, 0), down),
+            2: (0, up),
+            3: ((3, 1), down),
+            4: ((1, 0), up),
+            5: (1, down),
+            6: (2, across),
+        }
         self.started = []
 
-    def copy(self, k, src, where):
+    def issue(self, k):
+        source, target = self.moves[k]
+        relayed = isinstance(source, int)
         c = pltpu.make_async_remote_copy(
-            src_ref=src,
+            src_ref=self.landed.at[source] if relayed else self.src.at[self.place(*source)],
             dst_ref=self.landed.at[k],
             send_sem=self.send.at[k],
             recv_sem=self.recv.at[k],
-            device_id={"expert": self.targets[where]},
+            device_id={"expert": target},
             device_id_type=MESH,
         )
         c.start()
         self.started.append(c)
 
-    def got(self, k):
+    def arrive(self, k):
         pltpu.make_async_remote_copy(
             src_ref=self.landed.at[k],
             dst_ref=self.landed.at[k],
             send_sem=self.send.at[k],
             recv_sem=self.recv.at[k],
-            device_id={"expert": self.targets["x"]},
+            device_id={"expert": self.moves[6][1]},
             device_id_type=MESH,
         ).wait_recv()
-        return self.landed[k].astype(F32)
-
-    def begin(self):
-        self.copy(0, self.src.at[self.place(2, 1)], "up")
-        self.copy(1, self.src.at[self.place(2, 0)], "down")
-        self.copy(3, self.src.at[self.place(3, 1)], "down")
-
-    def relay(self):
-        self.landed[0] = (self.own(1, 1) + self.got(0)).astype(BF)
-        self.copy(2, self.landed.at[0], "up")
-        self.copy(4, self.src.at[self.place(1, 0)], "up")
-        self.landed[1] = (self.own(3, 0) + self.got(1)).astype(BF)
-        self.copy(5, self.landed.at[1], "down")
-
-    def cross(self):
-        self.landed[2] = (self.own(0, 1) + self.got(2) + self.got(3)).astype(BF)
-        self.copy(6, self.landed.at[2], "x")
+
+    def sum(self, block, *landed):
+        total = self.own(*block)
+        for k in landed:
+            total = total + self.landed[k].astype(F32)
+        return total
+
+    def add(self, k):
+        block, landed = (((1, 1), (0,)), ((3, 0), (1,)), ((0, 1), (2, 3)))[k]
+        self.landed[k] = self.sum(block, *landed).astype(BF)
 
     def total(self):
-        return self.own(0, 0) + self.got(4) + self.got(5) + self.got(6)
+        return self.sum((0, 0), 4, 5, 6)
 
     def finish(self):
         for c in self.started:
             c.wait_send()
+        self.started = []
+
+
+RING = {
+    6: (0, "up", ()),
+    7: (1, "down", ()),
+    4: (2, "up", ()),
+    5: (3, "down", (1,)),
+    2: (4, "up", (0,)),
+    3: (5, "down", ()),
+    1: (6, "x", (2, 3)),
+    0: (None, None, (4, 5, 6)),
+}
+ACROSS = {
+    7: (3, "x", ()),
+    4: (1, "x", ()),
+    5: (2, "x", ()),
+    1: (0, "x", ()),
+    6: (4, "up", (3,)),
+    2: (6, "up", (1, 4)),
+    3: (7, "down", (2,)),
+    0: (None, None, (0, 6, 7)),
+}
+ACROSS_DOWN = {**ACROSS, 6: (4, "down", (3,)), 2: (6, "up", (1,)), 3: (7, "down", (2, 4))}
+WAYS = (RING, RING, RING, ACROSS, ACROSS_DOWN, RING)
+
+
+def dp_targets():
+    x, y, core = dp_place()
+    return {
+        "x": dp_index(x + 1, y, core),
+        "up": dp_index(x, y + 1, core),
+        "down": dp_index(x, y + 3, core),
+        "core": dp_index(x, y, core + 1),
+    }
 
 
 class DenseSum:
     def __init__(self, grads, theirs, landed, send, recv):
         self.grads, self.theirs, self.landed, self.send, self.recv = grads, theirs, landed, send, recv
+        self.targets = dp_targets()
         x, y, core = dp_place()
-        self.targets = {
-            "x": dp_index(x + 1, y, core),
-            "up": dp_index(x, y + 1, core),
-            "down": dp_index(x, y + 3, core),
-            "core": dp_index(x, y, core + 1),
-        }
         self.slots = [dp_index(x + rx, y + ry, core) for rx, ry in SLOTS]
         self.others = [dp_index(x + rx, y + ry, core + 1) for rx, ry in SLOTS]
+        self.carried = {j: (k, where) for k, (j, where, _) in RING.items()}
         self.started = []
 
     def descriptor(self, k, src, dst, where):
@@ -705,155 +740,163 @@
             device_id_type=MESH,
         )
 
-    def copy(self, k, src, dst, where):
+    def issue(self, k):
+        if k >= 8:
+            src, dst, where = self.grads.at[self.others[k - 8]], self.theirs.at[k - 8], "core"
+        else:
+            slot, where = self.carried[k]
+            src, dst = self.grads.at[self.slots[slot]], self.landed.at[k]
         c = self.descriptor(k, src, dst, where)
         c.start()
         self.started.append(c)
 
-    def begin(self):
-        for k in (6, 7, 4, 5, 2, 3, 1, 0):
-            self.copy(8 + k, self.grads.at[self.others[k]], self.theirs.at[k], "core")
-
-    def got(self, k):
-        self.descriptor(k, self.landed.at[k], self.landed.at[k], "x").wait_recv()
-        return self.landed[k].astype(F32)
-
-    def both(self, k):
-        self.descriptor(8 + k, self.theirs.at[k], self.theirs.at[k], "core").wait_recv()
-        return self.grads[self.slots[k]].astype(F32) + self.theirs[k].astype(F32)
-
-    def put(self, k, value, j, where):
-        self.grads[self.slots[k]] = value.astype(BF)
-        self.copy(j, self.grads.at[self.slots[k]], self.landed.at[j], where)
-
-    def first(self):
-        self.put(6, self.both(6), 0, "up")
-        self.put(7, self.both(7), 1, "down")
-        self.put(4, self.both(4), 2, "up")
-
-    def second(self):
-        self.put(5, self.both(5) + self.got(1), 3, "down")
-        self.put(2, self.both(2) + self.got(0), 4, "up")
-        self.put(3, self.both(3), 5, "down")
-
-    def third(self):
-        self.put(1, self.both(1) + self.got(2) + self.got(3), 6, "x")
-
-    def total(self):
-        return self.both(0) + self.got(4) + self.got(5) + self.got(6)
+    def arrive(self, k):
+        ref = self.theirs.at[k - 8] if k >= 8 else self.landed.at[k]
+        self.descriptor(k, ref, ref, "x").wait_recv()
+
+    def sum(self, k):
+        total = self.grads[self.slots[k]].astype(F32) + self.theirs[k].astype(F32)
+        for j in RING[k][2]:
+            total = total + self.landed[j].astype(F32)
+        return total
+
+    def add(self, k):
+        self.grads[self.slots[k]] = self.sum(k).astype(BF)
 
     def finish(self):
         for c in self.started:
             c.wait_send()
 
 
+class Stage:
+    def __init__(self, buffers, sems):
+        self.buffers, self.sems = buffers, sems
+        self.free = list(range(buffers.shape[0]))
+        self.held = {}
+
+    def fetch(self, name, src, rows):
+        i = self.free.pop(0)
+        ref = self.buffers.at[i, pl.ds(0, rows)]
+        c = pltpu.make_async_copy(src, ref, self.sems.at[i])
+        c.start()
+        self.held[name] = (i, ref, c)
+
+    def wait(self, name):
+        self.held[name][2].wait()
+
+    def take(self, name):
+        i, ref, _ = self.held.pop(name)
+        self.free.append(i)
+        return ref
+
+
 class ExpertSum:
-    def __init__(self, keep, given, near, far, stage, sends, far_sends, ends, s_near, r_near, s_far, r_far, l_sem):
-        self.keep, self.given, self.near, self.far, self.stage = keep, given, near, far, stage
-        self.sends, self.far_sends, self.ends = sends, far_sends, ends
-        self.s_near, self.r_near, self.s_far, self.r_far, self.l_sem = s_near, r_near, s_far, r_far, l_sem
-        x, y, core = dp_place()
-        self.targets = {
-            "x": dp_index(x + 1, y, core),
-            "up": dp_index(x, y + 1, core),
-            "down": dp_index(x, y + 3, core),
-        }
+    def __init__(self, own, given, landed, out, ends, way, stage, send, recv, store):
+        self.own, self.given, self.landed, self.out, self.ends = own, given, landed, out, ends
+        self.way, self.stage, self.send, self.recv, self.store = way, stage, send, recv, store
+        self.rows = own(0).shape[0]
+        self.targets = dp_targets()
+        self.carried = {j: (k, where) for k, (j, where, _) in way.items()}
         self.started = []
 
-    def descriptor(self, src, dst, send, recv, where):
+    def descriptor(self, j, src, where):
         return pltpu.make_async_remote_copy(
             src_ref=src,
-            dst_ref=dst,
-            send_sem=send,
-            recv_sem=recv,
+            dst_ref=self.landed(j),
+            send_sem=self.send.at[j],
+            recv_sem=self.recv.at[j],
             device_id={"dp": self.targets[where]},
             device_id_type=MESH,
         )
 
-    def add(self, refs, out, count):
-        def load(e):
-            return [
-                pltpu.make_async_copy(r.at[e], self.stage.at[e % 2, i], self.l_sem.at[e % 2, i])
-                for i, r in enumerate(refs)
-            ]
-
-        for c in load(0):
-            c.start()
-        for e in range(count):
-            if e + 1 < count:
-                for c in load(e + 1):
-                    c.start()
-            for c in load(e):
-                c.wait()
-            acc = self.stage[e % 2, 0].astype(F32)
-            for i in range(1, len(refs)):
-                acc = acc + self.stage[e % 2, i].astype(F32)
-            out[e] = acc.astype(out.dtype)
-
-    def parts(self, k, first, count):
-        span = pl.ds(first, count)
-        return [self.keep.at[k, span], self.given.at[k, span]]
-
-    def near_send(self, k, j, where, more=()):
-        for i in more:
-            self.near_got(i)
-        out = self.sends.at[j]
-        self.add(self.parts(k, 0, 3) + [self.near.at[i] for i in more], out, 3)
-        c = self.descriptor(out, self.near.at[j], self.s_near.at[j], self.r_near.at[j], where)
+    def issue(self, j):
+        k, where = self.carried[j]
+        c = self.descriptor(j, self.own(k), where)
         c.start()
         self.started.append(c)
 
-    def near_got(self, j):
-        self.descriptor(
-            self.near.at[j], self.near.at[j], self.s_near.at[j], self.r_near.at[j], "x"
-        ).wait_recv()
-
-    def far_send(self, k, j, where, which=(0, 1), more=()):
-        for i in which:
-            for m in more:
-                if m < 4 or m == 4 + i:
-                    self.far_got(m, i)
-            out = self.far_sends.at[j, pl.ds(i, 1)]
-            self.add(
-                self.parts(k, 3 + i, 1)
-                + [self.far.at[m, pl.ds(i, 1)] for m in more if m < 4 or m == 4 + i],
-                out,
-                1,
-            )
-            c = self.descriptor(
-                out,
-                self.far.at[j, pl.ds(i, 1)],
-                self.s_far.at[j, i],
-                self.r_far.at[j, i],
-                where,
-            )
-            c.start()
-            self.started.append(c)
-
-    def far_got(self, j, i):
-        ref = self.far.at[j, pl.ds(i, 1)]
-        self.descriptor(ref, ref, self.s_far.at[j, i], self.r_far.at[j, i], "x").wait_recv()
-
-    def near_end(self):
-        for j in (4, 5, 6):
-            self.near_got(j)
-        self.add(
-            self.parts(0, 0, 3) + [self.near.at[j] for j in (4, 5, 6)],
-            self.ends,
-            3,
-        )
-
-    def far_end(self):
-        for j in (0, 6, 7):
-            for i in range(2):
-                self.far_got(j, i)
-        self.add(
-            self.parts(0, 3, 2) + [self.far.at[j] for j in (0, 6, 7)], self.ends, 2
-        )
+    def arrive(self, j):
+        self.descriptor(j, self.landed(j), "x").wait_recv()
+
+    def fetch_given(self, k):
+        self.stage.fetch((id(self), "l", k), self.given(k), self.rows)
+
+    def fetch_landed(self, j):
+        self.stage.fetch((id(self), "h", j), self.landed(j), self.rows)
+
+    def wait_given(self, k):
+        self.stage.wait((id(self), "l", k))
+
+    def wait_landed(self, j):
+        self.stage.wait((id(self), "h", j))
+
+    def accumulate(self, k, names, out):
+        refs = [self.stage.take((id(self),) + n) for n in names]
+
+        def body(i, _):
+            span = pl.ds(pl.multiple_of(i * 32, 32), 32)
+            total = self.own(k)[span, :].astype(F32)
+            for r in refs:
+                total = total + r[span, :].astype(F32)
+            out[span, :] = total.astype(out.dtype)
+            return _
+
+        lax.fori_loop(0, self.rows // 32, body, 0)
+
+    def add_given(self, k):
+        self.accumulate(k, [("l", k)], self.own(k))
+
+    def add_landed(self, k):
+        out = self.own(k) if k > 0 else self.ends
+        self.accumulate(k, [("h", j) for j in self.way[k][2]], out)
+
+    def write(self):
+        self.save = pltpu.make_async_copy(self.ends, self.out, self.store)
+        self.save.start()
 
     def finish(self):
         for c in self.started:
             c.wait_send()
+
+
+LAST_STEPS = ("in", "e", "qo", "qs", "C4", "GO", "A0", "A1", "A2", "P0", "P1", "GS", "MX", "GT", "CO")
+LAST_STEPS = LAST_STEPS + ("CS", "FI", "lz", "lw", "ly")
+LAST_STEPS = LAST_STEPS + tuple(f + k for f in "zyg" for k in "0123456ABC")
+for family in "os":
+    LAST_STEPS = LAST_STEPS + tuple(family + str(k) for k in range(16))
+    LAST_STEPS = LAST_STEPS + tuple(family + "a%d" % k for k in range(8)) + (family + "t",)
+for part in range(len(PARTS)):
+    LAST_STEPS = LAST_STEPS + tuple("u%d." % part + f + str(k) for f in ("", "l", "S", "R", "h") for k in range(8))
+    LAST_STEPS = LAST_STEPS + ("u%d.w" % part,)
+LAST_ORDER = (
+    197, 277, 157, 21, 18, 22, 1, 19, -197, 205, 279, 183, -277, 285, 111, 266, -157, 165, 239,
+    143, -279, 287, 156, -111, 119, 315, -239, 247, 321, -156, 164, 198, 35, 142, 24, 227, -183,
+    -266, -22, -18, 29, -315, 323, 114, -321, 329, 110, 307, -198, 206, 236, -114, 122, 317, -21,
+    28, -143, 184, -110, 118, 154, -236, 244, 192, -317, 325, 280, -154, 162, 193, 144, -192, 200,
+    215, -280, 288, 273, -193, 201, 237, 225, -215, 209, 232, -273, 281, 155, -237, 245, 175, -307,
+    -232, 240, 115, 23, 26, -155, 163, 194, -142, -175, 171, 195, -115, 123, 316, -194, 202, 152,
+    -227, -195, 203, 314, -316, 324, 278, -152, 160, 319, -314, 322, 339, -278, 286, 174, -319,
+    327, 234, -339, 335, 318, -174, 168, 320, -234, 242, 113, -318, 326, 112, -320, 328, 275, -113,
+    121, 298, -112, 120, 153, -275, 283, 196, -298, 291, 151, -153, 161, 274, -196, 204, 233, -151,
+    159, 150, -274, 282, 276, 309, -233, 241, 191, -150, 158, 116, 306, -276, 284, 109, -191, 199,
+    235, -116, 124, 238, -109, 117, 259, 224, -235, 243, -238, 246, -259, 254, -184, 216, 145,
+    -144, 176, 228, -225, -216, 212, 257, -309, 25, 34, -306, 338, -338, 332, -23, -24, 30, 27,
+    186, 103, -224, -145, 177, -228, 260, -176, -177, 167, 31, -257, -260, 250, 32, 106, 308, 267,
+    -186, 218, -103, 135, 185, 146, 265, 102, 268, -25, -26, -27, -1, -19, 5, -267, -106, 20, 2,
+    -185, 217, 147, -308, 6, -265, 63, 61, 62, 230, -102, 134, 148, -31, -20, 38, 33, 64, -268,
+    -217, -218, 208, 59, -63, 71, 65, -146, -134, 130, 300, 53, 189, 104, 66, 60, -2, 7, -147, -66,
+    74, 52, 101, -230, 8, -104, 136, 226, -148, 188, 9, -189, -135, -136, 126, 178, 179, 180, 107,
+    187, 10, -101, 133, 311, -226, 11, 41, 44, -188, -133, 127, 340, 341, 105, -300, 295, 138, 269,
+    -178, -179, -180, 166, 299, 182, -64, -52, 72, -311, -65, 73, -187, -33, -34, 40, 54, -107,
+    139, 51, 37, 45, 42, 12, 86, 91, 89, 87, -105, 137, 84, -269, 301, 90, 85, 88, -340, -341, 331,
+    219, 220, 221, -32, 39, -91, 99, 77, -87, 95, -137, -138, -139, 125, 258, 141, -88, 96, 312,
+    81, -41, 48, 78, -60, -53, -54, 68, -90, 98, 76, 57, -89, -77, 97, 79, -62, 70, 271, 43, 56,
+    36, -61, -51, 69, -312, -299, -301, 292, 297, -219, -220, -221, 207, 343, 344, 223, -258, 251,
+    256, 262, -85, -78, -79, 93, -42, 49, -86, -76, 94, 80, 82, 55, 272, -271, 303, 46, -84, -80,
+    -81, -82, 100, 16, 4, 231, -43, -44, 50, 47, 310, -35, -36, -37, 13, -272, 304, -59, -55, -56,
+    -57, 75, 15, 3, -310, 342, -297, -303, -304, 289, 305, -342, -343, -344, 330, -231, 263, 346,
+    -256, -262, -263, 248, 264, -45, -46, -47, 14, -3, -4, 17, -182, -141, -223, -305, -346, -264,
+)
 
 
 def last_kernel(*refs):
@@ -871,8 +914,8 @@
         cot_hbm,
     ) = refs[:11]
     kept_in = refs[11:22]
-    mixed_out, grad_tokens_out, expert_ref, small_own, output_out, near, far = refs[22:29]
-    kept_refs = refs[29:40]
+    mixed_out, grad_tokens_out, expert_ref, small_own, output_out, landed = refs[22:28]
+    kept_refs = refs[28:39]
     (
         query_ref,
         key_ref,
@@ -913,8 +956,7 @@
         z_landed,
         y_landed,
         stage,
-        sends,
-        far_sends,
+        terms,
         ends,
         small_theirs,
         small_landed,
@@ -929,13 +971,11 @@
         r_reduce,
         s_dense,
         r_dense,
-        s_near,
-        r_near,
-        s_far,
-        r_far,
+        s_part,
+        r_part,
         l_sem,
-        l_add,
-    ) = refs[40:]
+        l_stage,
+    ) = refs[39:]
     _, peers = expert_peers()
     x, y, core = dp_place()
     me = lax.axis_index("expert")
@@ -953,105 +993,144 @@
         part = expert_copies(
             [src], [out], [mode], s_direct.at[pl.ds(i, 1)], r_direct.at[pl.ds(i, 1)]
         ) + own_copies([src], [out], [mode], l_sem.at[pl.ds(i, 1)])
-        for c in part:
-            c.start()
-        return part
-
-    def settle(part):
-        for c in part:
-            c.wait()
+
+        def start():
+            for c in part:
+                c.start()
+
+        def wait():
+            for c in part:
+                c.wait()
+
+        return start, wait
 
     def load(src, dst, i):
         c = pltpu.make_async_copy(src, dst, l_sem.at[i])
         c.start()
         return c
 
+    def settle(part):
+        for c in part:
+            c.wait()
+
     OWN = ((1, 1), (3, 0), (0, 1), (0, 0))
-
-    def own_blocks(reduce, src, base):
-        return [
-            load(src.at[reduce.place(*d)], z_own.at[i], base + i) for i, d in enumerate(OWN)
-        ]
 
     def from_own(dz, dx):
         return z_own[OWN.index((dz, dx))].astype(F32)
 
-    back = Reduce(back_part, from_own, z_landed, s_reduce.at[0], r_reduce.at[0])
-    back.begin()
-    loads = own_blocks(back, back_part, 8)
-    inner = direct(0, inner_part, inner_in, "exchange")
-    kept = [load(a, b, 16 + i) for i, (a, b) in enumerate(zip(kept_in, kept_refs))]
-    kept = kept + [load(tokens_hbm, tokens, 27), load(cot_hbm, cot, 28)]
-    loads_small = load(small_hbm, small, 4)
-    loads_dense = load(dense_hbm, dense, 5)
-    loads_normed = load(normed_all, normed, 6)
-    experts = ExpertSum(
-        keep, given, near, far, stage, sends, far_sends, ends, s_near, r_near, s_far, r_far, l_add
-    )
-    experts.near_send(6, 0, "up")
-    experts.near_send(7, 1, "down")
-    settle(loads)
-    back.relay()
-    experts.far_send(7, 3, "x")
-    experts.far_send(4, 1, "x", (0,))
-    experts.near_send(4, 2, "up")
-    back.cross()
-    experts.near_send(5, 3, "down", (1,))
-    experts.far_send(6, 4, "up", (0,), (3,))
-    experts.far_send(6, 5, "down", (1,), (3,))
-    experts.near_send(2, 4, "up", (0,))
-    experts.near_send(3, 5, "down")
-    experts.far_send(4, 1, "x", (1,))
-    settle(inner)
-    settle([loads_small, loads_dense] + kept)
-
-    for j in range(PEERS):
-        gates_grad[LOCAL * j : LOCAL * (j + 1), :] = inner_in[j, 0:LOCAL, :]
-    gates = gates_ref[...]
-    grad_gates = gates_grad[...]
-    logits_grad[...] = jnp.zeros_like(logits_grad)
-    logits_grad[ROUTER - 256 : GAINS - 256, :] = gates * (
-        grad_gates - jnp.sum(gates * grad_gates, axis=0, keepdims=True)
-    )
-    pick = (
-        lax.broadcasted_iota(jnp.int32, (8, SLICE), 1)
-        == lax.broadcasted_iota(jnp.int32, (8, SLICE), 0) + GAINS
-    )
-    gains = dot(pick.astype(F32).astype(BF), small[...].reshape(DIM, SLICE), ((1,), (1,)))
-    gain_one, gain_two = gains[0:1], gains[1:2]
-    grad_logits = logits_grad[...].astype(BF)
-    router = small[:, :, 256:SLICE].reshape(DIM, SLICE - 256)
-    grad = back.total() + dot(grad_logits, router, ((0,), (1,)))
-    middle = middle_ref[...]
-    scale_two = lax.rsqrt(jnp.mean(middle * middle, axis=-1, keepdims=True) + epsilon)
-    gain_sum[0] = jnp.sum((grad * middle * scale_two).reshape(TOK // 8, 8, DIM), axis=0)
-    grad_middle = cot[...].astype(F32) + norm_back(middle, scale_two, gain_two, grad)
-    grad_middle_ref[...] = grad_middle
-    grad_branch = grad_middle.astype(BF)
-    for j in range(PEERS):
-        att_send[j] = dot(
-            grad_branch, dense[2 * j : 2 * j + 2].reshape(QS, DIM), ((1,), (1,))
-        ).astype(BF)
-    back.finish()
-    exchanged = direct(1, att_send, att_in, "exchange")
-    experts.far_send(5, 2, "x")
-    for j in range(PEERS):
-        dense[2 * j : 2 * j + 2] = (
-            dot(attended_ref[j], grad_branch, ((0,), (0,))).astype(BF).reshape(2, ROWS, DIM)
-        )
-    settle(exchanged)
-    out = Reduce(out_part, from_own, y_landed, s_reduce.at[1], r_reduce.at[1])
-    out.begin()
-    loads = own_blocks(out, out_part, 8)
-    sums = [
-        DenseSum(dense, dense_theirs, dense_landed, s_dense.at[0], r_dense.at[0]),
-        DenseSum(grad_small, small_theirs, small_landed, s_dense.at[1], r_dense.at[1]),
-    ]
-    sums[0].begin()
-    experts.far_send(1, 0, "x")
-
-    grad_key[...] = jnp.zeros_like(grad_key)
-    grad_value[...] = jnp.zeros_like(grad_value)
+    def from_grad(dz, dx):
+        return grad_normed[sums["g"].place(dz, dx)].astype(F32)
+
+    sums = {
+        "z": Reduce(back_part, from_own, z_landed, s_reduce.at[0], r_reduce.at[0]),
+        "y": Reduce(out_part, from_own, y_landed, s_reduce.at[1], r_reduce.at[1]),
+        "g": Reduce(grad_normed, from_grad, z_landed, s_reduce.at[2], r_reduce.at[2]),
+        "o": DenseSum(dense, dense_theirs, dense_landed, s_dense.at[0], r_dense.at[0]),
+        "s": DenseSum(grad_small, small_theirs, small_landed, s_dense.at[1], r_dense.at[1]),
+    }
+    fetched = Stage(stage, l_stage)
+    for i, ((expert, _), (row, rows), _) in enumerate(PARTS):
+        span = pl.ds(row, rows)
+        sums["u%d." % i] = ExpertSum(
+            lambda k, e=expert, r=span: terms.at[e, k, r],
+            lambda k, e=expert, r=span: given.at[k, e, r],
+            lambda j, e=expert, r=span: landed.at[j, e, r],
+            expert_ref.at[expert, span],
+            ends.at[expert, span],
+            WAYS[i],
+            fetched,
+            s_part.at[i],
+            r_part.at[i],
+            l_sem.at[32 + i],
+        )
+    issue, arrive, done = {}, {}, {}
+    for i, (name, src, out) in enumerate(
+        (
+            ("in", inner_part, inner_in),
+            ("e", att_send, att_in),
+            ("qo", dense_cut, dense_in),
+            ("qs", small_cut, small_own),
+        )
+    ):
+        issue[name], arrive[name] = direct(i, src, out, "exchange")
+    for name, part in sums.items():
+        for k in range(16):
+            issue[name + str(k)] = functools.partial(part.issue, k)
+            arrive[name + str(k)] = functools.partial(part.arrive, k)
+        for k in range(8):
+            if name in "zyg":
+                issue[name + "ABCDEFGH"[k]] = functools.partial(part.add, k)
+            elif name in "os":
+                issue[name + "a%d" % k] = functools.partial(part.add, k)
+            else:
+                issue[name + "l%d" % k] = functools.partial(part.fetch_given, k)
+                arrive[name + "l%d" % k] = functools.partial(part.wait_given, k)
+                issue[name + "h%d" % k] = functools.partial(part.fetch_landed, k)
+                arrive[name + "h%d" % k] = functools.partial(part.wait_landed, k)
+                issue[name + "S%d" % k] = functools.partial(part.add_given, k)
+                issue[name + "R%d" % k] = functools.partial(part.add_landed, k)
+
+    def own_blocks(name, src, base):
+        def start():
+            done[name] = [
+                load(src.at[sums["z"].place(*d)], z_own.at[i], base + i) for i, d in enumerate(OWN)
+            ]
+
+        return start, lambda: settle(done[name])
+
+    issue["lz"], arrive["lz"] = own_blocks("lz", back_part, 8)
+    issue["ly"], arrive["ly"] = own_blocks("ly", out_part, 8)
+
+    def load_kept():
+        done["lw"] = [load(a, b, 16 + i) for i, (a, b) in enumerate(zip(kept_in, kept_refs))] + [
+            load(tokens_hbm, tokens, 27),
+            load(cot_hbm, cot, 28),
+            load(small_hbm, small, 4),
+            load(dense_hbm, dense, 5),
+            load(normed_all, normed, 6),
+        ]
+
+    issue["lw"], arrive["lw"] = load_kept, lambda: settle(done["lw"])
+
+    def back_to_middle():
+        for j in range(PEERS):
+            gates_grad[LOCAL * j : LOCAL * (j + 1), :] = inner_in[j, 0:LOCAL, :]
+        gates = gates_ref[...]
+        grad_gates = gates_grad[...]
+        logits_grad[...] = jnp.zeros_like(logits_grad)
+        logits_grad[ROUTER - 256 : GAINS - 256, :] = gates * (
+            grad_gates - jnp.sum(gates * grad_gates, axis=0, keepdims=True)
+        )
+        pick = (
+            lax.broadcasted_iota(jnp.int32, (8, SLICE), 1)
+            == lax.broadcasted_iota(jnp.int32, (8, SLICE), 0) + GAINS
+        )
+        gains = dot(pick.astype(F32).astype(BF), small[...].reshape(DIM, SLICE), ((1,), (1,)))
+        done["gain_one"], gain_two = gains[0:1], gains[1:2]
+        grad_logits = logits_grad[...].astype(BF)
+        done["grad_logits"] = grad_logits
+        router = small[:, :, 256:SLICE].reshape(DIM, SLICE - 256)
+        grad = sums["z"].total() + dot(grad_logits, router, ((0,), (1,)))
+        middle = middle_ref[...]
+        scale_two = lax.rsqrt(jnp.mean(middle * middle, axis=-1, keepdims=True) + epsilon)
+        gain_sum[0] = jnp.sum((grad * middle * scale_two).reshape(TOK // 8, 8, DIM), axis=0)
+        grad_middle = cot[...].astype(F32) + norm_back(middle, scale_two, gain_two, grad)
+        grad_middle_ref[...] = grad_middle
+        grad_branch = grad_middle.astype(BF)
+        done["grad_branch"] = grad_branch
+        for j in range(PEERS):
+            att_send[j] = dot(
+                grad_branch, dense[2 * j : 2 * j + 2].reshape(QS, DIM), ((1,), (1,))
+            ).astype(BF)
+        sums["z"].finish()
+
+    def output_grads():
+        for j in range(PEERS):
+            dense[2 * j : 2 * j + 2] = (
+                dot(attended_ref[j], done["grad_branch"], ((0,), (0,)))
+                .astype(BF)
+                .reshape(2, ROWS, DIM)
+            )
 
     def attend(width, i, _):
         queries = query_ref[i]
@@ -1074,16 +1153,11 @@
         grad_value[0:width, :] += dot(probs.astype(BF), incoming, ((0,), (0,)))
         return _
 
-    lax.fori_loop(0, 4, functools.partial(attend, GROUP // 2), 0)
-    settle(loads)
-    out.relay()
-    experts.near_send(1, 6, "x", (2, 3))
-    sums[0].first()
-    lax.fori_loop(4, 8, functools.partial(attend, GROUP), 0)
-    out.cross()
-
-    settle([loads_normed])
-    gain_sum[1] = jnp.zeros((8, DIM), F32)
+    def attend_blocks(first, last, width):
+        if first == 0:
+            grad_key[...] = jnp.zeros_like(grad_key)
+            grad_value[...] = jnp.zeros_like(grad_value)
+        lax.fori_loop(first, last, functools.partial(attend, width), 0)
 
     def project(i, _):
         span = pl.ds(pl.multiple_of(i * 2 * TOK, 2 * TOK), 2 * TOK)
@@ -1114,68 +1188,90 @@
         gain_sum[1] += jnp.sum((grad * values * scale).reshape(2 * TOK // 8, 8, DIM), axis=0)
         return _
 
-    lax.fori_loop(0, 4, project, 0)
-
-    def from_grad(dz, dx):
-        return grad_normed[first.place(dz, dx)].astype(F32)
-
-    first = Reduce(grad_normed, from_grad, z_landed, s_reduce.at[2], r_reduce.at[2])
-    first.begin()
-
-    lanes = lax.broadcasted_iota(jnp.int32, (8, 128), 1)
-    marks = [(lanes == GAINS - 256 + i).astype(F32).astype(BF) for i in range(2)]
-    for c in range(4):
-        span = slice(c * 384, (c + 1) * 384)
-        part = dot(normed[:, :, span].reshape(GROUP, 384), grad_qkv[...], ((0,), (0,)))
-        extra = dot(normed_two_ref[:, span], grad_logits, ((0,), (1,)))
-        for i in range(2):
-            value = gain_sum[1 - i, :, span]
-            high = value.astype(BF)
-            rest = (value - high.astype(F32)).astype(BF)
-            extra = extra + dot(high, marks[i], ((0,), (0,))) + dot(rest, marks[i], ((0,), (0,)))
-        grad_small[4 * c : 4 * c + 4, :, 0:256] = (
-            part[:, 0:256].astype(BF).reshape(4, ROWS, 256)
-        )
-        grad_small[4 * c : 4 * c + 4, :, 256:SLICE] = (
-            (part[:, 256:SLICE] + extra).astype(BF).reshape(4, ROWS, SLICE - 256)
-        )
-    sums[1].begin()
-    first.relay()
-    sums[0].second()
-    sums[1].first()
-    experts.far_send(2, 6, "up", (0, 1), (1, 4))
-    experts.far_send(3, 7, "down", (0, 1), (2, 5))
-    mixed_ref[...] = (middle_ref[...] + out.total()).astype(BF)
-    saves = [load(mixed_ref, mixed_out, 29)]
-    first.cross()
-    sums[0].third()
-    sums[1].second()
-    sums[1].third()
-    values = tokens[...].astype(F32)
-    scale = lax.rsqrt(jnp.mean(values * values, axis=-1, keepdims=True) + epsilon)
-    grad_tokens_ref[...] = grad_middle_ref[...] + norm_back(values, scale, gain_one, first.total())
-    saves.append(load(grad_tokens_ref, grad_tokens_out, 30))
-    total = sums[0].total()
-    for j in range(PEERS):
-        dense_cut[j] = total[12 * j : 12 * (j + 1)]
-    total = sums[1].total()
-    for j in range(PEERS):
-        small_cut[j] = total[12 * j : 12 * (j + 1)]
-    cuts = direct(2, dense_cut, dense_in, "exchange") + direct(3, small_cut, small_own, "exchange")
-    experts.far_end()
-    saved = load(ends.at[pl.ds(0, 2)], expert_ref.at[pl.ds(3, 2)], 4)
-    saved.wait()
-    experts.near_end()
-    saved = load(ends, expert_ref.at[pl.ds(0, 3)], 4)
-    settle(cuts)
-    acc = dense_in[0]
-    for j in range(1, PEERS):
-        acc = acc + dense_in[j]
-    output_own[...] = acc
-    saves.append(load(output_own, output_out, 31))
-    for part in (out, first, sums[0], sums[1], experts):
+    def project_blocks(first, last):
+        if first == 0:
+            gain_sum[1] = jnp.zeros((8, DIM), F32)
+        lax.fori_loop(first, last, project, 0)
+
+    def small_grads():
+        lanes = lax.broadcasted_iota(jnp.int32, (8, 128), 1)
+        marks = [(lanes == GAINS - 256 + i).astype(F32).astype(BF) for i in range(2)]
+        for c in range(4):
+            span = slice(c * 384, (c + 1) * 384)
+            part = dot(normed[:, :, span].reshape(GROUP, 384), grad_qkv[...], ((0,), (0,)))
+            extra = dot(normed_two_ref[:, span], done["grad_logits"], ((0,), (1,)))
+            for i in range(2):
+                value = gain_sum[1 - i, :, span]
+                high = value.astype(BF)
+                rest = (value - high.astype(F32)).astype(BF)
+                extra = extra + dot(high, marks[i], ((0,), (0,)))
+                extra = extra + dot(rest, marks[i], ((0,), (0,)))
+            grad_small[4 * c : 4 * c + 4, :, 0:256] = (
+                part[:, 0:256].astype(BF).reshape(4, ROWS, 256)
+            )
+            grad_small[4 * c : 4 * c + 4, :, 256:SLICE] = (
+                (part[:, 256:SLICE] + extra).astype(BF).reshape(4, ROWS, SLICE - 256)
+            )
+
+    saves = []
+
+    def mix():
+        mixed_ref[...] = (middle_ref[...] + sums["y"].total()).astype(BF)
+        saves.append(load(mixed_ref, mixed_out, 29))
+
+    def token_grads():
+        values = tokens[...].astype(F32)
+        scale = lax.rsqrt(jnp.mean(values * values, axis=-1, keepdims=True) + epsilon)
+        grad_tokens_ref[...] = grad_middle_ref[...] + norm_back(
+            values, scale, done["gain_one"], sums["g"].total()
+        )
+        saves.append(load(grad_tokens_ref, grad_tokens_out, 30))
+
+    def total_of(name):
+        done[name] = sums[name].sum(0)
+
+    def cut(name, ref):
+        for j in range(PEERS):
+            ref[j] = done[name][12 * j : 12 * (j + 1)]
+
+    def own_output():
+        acc = dense_in[0]
+        for j in range(1, PEERS):
+            acc = acc + dense_in[j]
+        output_own[...] = acc
+        saves.append(load(output_own, output_out, 31))
+
+    issue["C4"], issue["GO"], issue["GS"] = back_to_middle, output_grads, small_grads
+    issue["A0"] = functools.partial(attend_blocks, 0, 4, GROUP // 2)
+    issue["A1"] = functools.partial(attend_blocks, 4, 6, GROUP)
+    issue["A2"] = functools.partial(attend_blocks, 6, 8, GROUP)
+    issue["P0"] = functools.partial(project_blocks, 0, 2)
+    issue["P1"] = functools.partial(project_blocks, 2, 4)
+    issue["MX"], issue["GT"], issue["FI"] = mix, token_grads, own_output
+    issue["ot"], issue["st"] = functools.partial(total_of, "o"), functools.partial(total_of, "s")
+    issue["CO"] = functools.partial(cut, "o", dense_cut)
+    issue["CS"] = functools.partial(cut, "s", small_cut)
+
+    mine = [load(keep.at[:, e], terms.at[e], 38 + e) for e in range(LOCAL)]
+    held = set()
+    for step in LAST_ORDER:
+        name = LAST_STEPS[abs(step) - 1]
+        if name[0] == "u" and name[3] == "S":
+            expert = PARTS[int(name[1])][0][0]
+            if expert not in held:
+                held.add(expert)
+                mine[expert].wait()
+        if name[0] == "u" and name[3:] == "w":
+            part = sums[name[:3]]
+            if step > 0:
+                part.write()
+            else:
+                part.save.wait()
+            continue
+        (issue if step > 0 else arrive)[name]()
+    for part in sums.values():
         part.finish()
-    settle(saves + [saved])
+    settle(saves)
 
 
 def last_phase(*args):
@@ -1189,8 +1285,7 @@
         (shape((LOCAL,) + piece, F32), hbm),
         (shape((PEERS, 12, SLICE), F32), hbm),
         (shape((12, DIM), F32), hbm),
-        (shape((7, 3) + piece, BF), hbm),
-        (shape((8, 2) + piece, BF), hbm),
+        (shape((8, LOCAL) + piece, BF), hbm),
     ]
     return pl.pallas_call(
         last_kernel,
@@ -1224,10 +1319,9 @@
             pltpu.VMEM((4, TOK, DIM), BF),
             pltpu.VMEM((7, TOK, DIM), BF),
             pltpu.VMEM((7, TOK, DIM), BF),
-            pltpu.VMEM((2, 5) + piece, BF),
-            pltpu.VMEM((7, 3) + piece, BF),
-            pltpu.VMEM((8, 2) + piece, BF),
-            pltpu.VMEM((3,) + piece, F32),
+            pltpu.VMEM((8,) + piece, BF),
+            pltpu.VMEM((LOCAL, 8) + piece, BF),
+            pltpu.VMEM((LOCAL,) + piece, F32),
             pltpu.VMEM((8, ROWS, SLICE), BF),
             pltpu.VMEM((7, ROWS, SLICE), BF),
             pltpu.VMEM((8, ROWS, DIM), BF),
@@ -1241,12 +1335,10 @@
             dma((3, 7)),
             dma((2, 16)),
             dma((2, 16)),
-            dma((7,)),
-            dma((7,)),
-            dma((8, 2)),
-            dma((8, 2)),
-            dma((32,)),
-            dma((2, 5)),
+            dma((len(PARTS), 8)),
+            dma((len(PARTS), 8)),
+            dma((43,)),
+            dma((8,)),
         ],
         compiler_params=pltpu.CompilerParams(
             collective_id=3, has_side_effects=True, vmem_limit_bytes=63 << 20
@@ -1568,7 +1660,7 @@
     out_part, back_part, inner_part, keep, given = run_experts(
         rows_all, cot_all, slots_all, gates_all, pieces
     )
-    mixed, grad_tokens, expert_grads, small_own, output_own, _, _ = last_phase(
+    mixed, grad_tokens, expert_grads, small_own, output_own, _ = last_phase(
         back_part,
         inner_part,
         out_part,

time: 325 us -> 318 us (0.978)
  Pallas kernels: 316 us -> 309 us
    pallas_call x1, Pallas kernels: 144 us -> 137 us  [last_phase(): pl.pallas_call(last_kernel, out_shape=[o[0] for o in outs], in_specs=[hbm...]
where the time goes in v6:
time: 318 us; the launch traced here: 317 us
  Pallas kernels  309 us (97%)
  local copies, waits for them, and re-layouts  5.83 us (2%)
    pallas_call x1, Pallas kernels, last_phase(): pl.pallas_call(last_kernel, out_shape=[o[0] for o in outs], in_specs=[hbm...  137 us
    pallas_call x1, Pallas kernels, first_phase(): pl.pallas_call(first_kernel, out_shape=[o[0] for o in outs], in_specs=[hb...  133 us
    pallas_call x1, Pallas kernels, run_experts(): pl.pallas_call(experts_kernel, out_shape=[jax.ShapeDtypeStruct((PEERS, TO...  34.7 us

profile of v6, /device:TPU:0, one launch (start us, length us, event | category | flops | bytes accessed | tf_op | source)
XLA Modules:
  0.0 317.2 jit_solution(9821736760673580978)
XLA Ops:
  0.7 0.1 pad.3.clone
  0.7 0.7 copy.29
  1.5 0.8 copy.30
  2.2 1.4 maximum_maximum_fusion.refs_3_
  3.6 1.4 copy.31.refs_7_
  5.0 133.2 %shard_map.229 = (bf16[16,5,288,512]{3,2,1,0:T(8,128)(2,1)}, bf16[8,128,1536]{2,1,0:T(8,128)(2,1)}, f32[8,8,128]{2,1,0:T(8,128)}, bf16[8,128,1536]{2,1,0:T(8,128...) custom-call(bf16[12,1536]{1,0:T(8,128)(2,1)} %refs_0_.1, ...), custom_call_target="tpu_custom_call" | custom-call | flops 120000004096 | tf_op jit(solution)/shard_map/pallas_call | solution.py:581
  138.2 34.7 %shard_map.230 = (bf16[8,128,1536]{2,1,0:T(8,128)(2,1)}, bf16[8,128,1536]{2,1,0:T(8,128)(2,1)}, f32[8,8,128]{2,1,0:T(8,128)}, bf16[8,5,288,512]{3,2,1,0:T(8,128)(2,1)}, bf16[8,5,288,512]{3,2,1,0:T(8,128)(2,1)}) custom-call(bf16[8,128,1536]{2,1,0:T(8,128)(2,1)} %get-tuple-element.52.refs_0_, bf16[8,128,1536]{2,1,0:T(8,128)(2,1)} %get-tuple-element.53.refs_1_, ...), custom_call_target="tpu_custom_call" | custom-call | flops 20000000000 | bytes 60000000 | tf_op jit(solution)/shard_map/pallas_call | solution.py:1486
  172.9 137.0 %shard_map.231 = (bf16[128,1536]{1,0:T(8,128)(2,1)}, f32[128,1536]{1,0:T(8,128)}, f32[5,288,512]{2,1,0:T(8,128)}, f32[8,12,384]{2,1,0:T(8,128)}, f32[12,1536]{1,0:T(8,128)}, /*index=5*/bf16[8,5,288,512]{3,2,1,0:T(8,128)(2,1)}) custom-call(bf16[8,128,1536]{2,1,0:T(8,128)(2,1)} %get-tuple-element.57.refs_0_, f32[8,8,128]{2,1,0:T(8,128)} %get-tuple-element.58.refs_1_, ...), custom_call_target="tpu_custom_call" | custom-call | flops 120000004096 | tf_op jit(solution)/shard_map/pallas_call | solution.py:1290
  309.9 4.4 %shard_map.232 = (bf16[128,1536]{1,0:T(8,128)(2,1)}, f32[128,1536]{1,0:T(8,128)}, f32[12,1536]{1,0:T(8,128)}, f32[12,512]{1,0:T(8,128)}, f32[12,512]{1,0:T(8,128...) custom-call(bf16[128,1536]{1,0:T(8,128)(2,1)} %get-tuple-element.77., ...), custom_call_target="tpu_custom_call" | custom-call | tf_op jit(solution)/shard_map/pallas_call | solution.py:1579
  314.4 1.5 slice_reduce_fusion
  315.8 1.4 slice.15
  (1 shorter events, 0.0 us)

commit v7 on v6

--- a/solution.py
+++ b/solution.py
@@ -59,7 +59,7 @@
         pl.semaphore_signal(barrier, inc=1, device_id={"expert": p}, device_id_type=MESH)
     for p in dp_ids:
         pl.semaphore_signal(barrier, inc=1, device_id={"dp": p}, device_id_type=MESH)
-    pl.semaphore_wait(barrier, len(expert_ids) + len(dp_ids))
+    return lambda: pl.semaphore_wait(barrier, len(expert_ids) + len(dp_ids))
 
 
 def any_specs(count):
@@ -334,7 +334,7 @@
     for c in loads + own:
         c.start()
     _, peers = expert_peers()
-    signal_all(
+    greeted = signal_all(
         peers,
         [
             dp_index(x + 1, y, core),
@@ -355,6 +355,7 @@
             ],
             axis=1,
         )
+    greeted()
 
     def direct(i, src, out, mode):
         part = expert_copies(
@@ -979,7 +980,7 @@
     _, peers = expert_peers()
     x, y, core = dp_place()
     me = lax.axis_index("expert")
-    signal_all(
+    greeted = signal_all(
         peers,
         [
             dp_index(x + 1, y, core),
@@ -1253,6 +1254,7 @@
     issue["CS"] = functools.partial(cut, "s", small_cut)
 
     mine = [load(keep.at[:, e], terms.at[e], 38 + e) for e in range(LOCAL)]
+    greeted()
     held = set()
     for step in LAST_ORDER:
         name = LAST_STEPS[abs(step) - 1]
@@ -1354,7 +1356,7 @@
     xg, cg, weights, grads, gates, inners, wsem, gsem, rsem = refs
     x, y, core = dp_place()
     other = dp_index(x, y, core + 1)
-    signal_all([], [other])
+    greeted = signal_all([], [other])
 
     def load(e, b):
         return pltpu.make_async_copy(pieces.at[:, e], weights.at[b], wsem.at[b])
@@ -1403,6 +1405,7 @@
         return _
 
     lax.fori_loop(0, PEERS, collect, 0)
+    greeted()
 
     def expert(e, _):
         b = lax.rem(e, 2)

time: 318 us -> 315 us (level)
    pallas_call x1, Pallas kernels: 137 us -> 134 us  [last_phase(): pl.pallas_call(last_kernel, out_shape=[o[0] for o in outs], in_specs=[hbm...]
where the time goes in v7:
time: 315 us; the launch traced here: 314 us
  Pallas kernels  306 us (97%)
  local copies, waits for them, and re-layouts  5.83 us (2%)
    pallas_call x1, Pallas kernels, last_phase(): pl.pallas_call(last_kernel, out_shape=[o[0] for o in outs], in_specs=[hbm...  134 us
    pallas_call x1, Pallas kernels, first_phase(): pl.pallas_call(first_kernel, out_shape=[o[0] for o in outs], in_specs=[hb...  133 us
    pallas_call x1, Pallas kernels, run_experts(): pl.pallas_call(experts_kernel, out_shape=[jax.ShapeDtypeStruct((PEERS, TO...  34.5 us

profile of v7, /device:TPU:0, one launch (start us, length us, event | category | flops | bytes accessed | tf_op | source)
XLA Modules:
  0.0 313.5 jit_solution(15403678325305599577)
XLA Ops:
  0.7 0.1 pad.3.clone
  0.7 0.7 copy.29
  1.5 0.8 copy.30
  2.2 1.4 maximum_maximum_fusion.refs_3_
  3.6 1.4 copy.31.refs_7_
  5.0 133.1 %shard_map.229 = (bf16[16,5,288,512]{3,2,1,0:T(8,128)(2,1)}, bf16[8,128,1536]{2,1,0:T(8,128)(2,1)}, f32[8,8,128]{2,1,0:T(8,128)}, bf16[8,128,1536]{2,1,0:T(8,128...) custom-call(bf16[12,1536]{1,0:T(8,128)(2,1)} %refs_0_.1, ...), custom_call_target="tpu_custom_call" | custom-call | flops 120000004096 | tf_op jit(solution)/shard_map/pallas_call | solution.py:582
  138.1 34.5 %shard_map.230 = (bf16[8,128,1536]{2,1,0:T(8,128)(2,1)}, bf16[8,128,1536]{2,1,0:T(8,128)(2,1)}, f32[8,8,128]{2,1,0:T(8,128)}, bf16[8,5,288,512]{3,2,1,0:T(8,128)(2,1)}, bf16[8,5,288,512]{3,2,1,0:T(8,128)(2,1)}) custom-call(bf16[8,128,1536]{2,1,0:T(8,128)(2,1)} %get-tuple-element.52.refs_0_, bf16[8,128,1536]{2,1,0:T(8,128)(2,1)} %get-tuple-element.53.refs_1_, ...), custom_call_target="tpu_custom_call" | custom-call | flops 20000000000 | bytes 60000000 | tf_op jit(solution)/shard_map/pallas_call | solution.py:1489
  172.6 133.7 %shard_map.231 = (bf16[128,1536]{1,0:T(8,128)(2,1)}, f32[128,1536]{1,0:T(8,128)}, f32[5,288,512]{2,1,0:T(8,128)}, f32[8,12,384]{2,1,0:T(8,128)}, f32[12,1536]{1,0:T(8,128)}, /*index=5*/bf16[8,5,288,512]{3,2,1,0:T(8,128)(2,1)}) custom-call(bf16[8,128,1536]{2,1,0:T(8,128)(2,1)} %get-tuple-element.57.refs_0_, f32[8,8,128]{2,1,0:T(8,128)} %get-tuple-element.58.refs_1_, ...), custom_call_target="tpu_custom_call" | custom-call | flops 120000004096 | tf_op jit(solution)/shard_map/pallas_call | solution.py:1292
  306.2 4.4 %shard_map.232 = (bf16[128,1536]{1,0:T(8,128)(2,1)}, f32[128,1536]{1,0:T(8,128)}, f32[12,1536]{1,0:T(8,128)}, f32[12,512]{1,0:T(8,128)}, f32[12,512]{1,0:T(8,128...) custom-call(bf16[128,1536]{1,0:T(8,128)(2,1)} %get-tuple-element.77., ...), custom_call_target="tpu_custom_call" | custom-call | tf_op jit(solution)/shard_map/pallas_call | solution.py:1582
  310.7 1.5 slice_reduce_fusion
  312.2 1.4 slice.15
  (1 shorter events, 0.0 us)
